TPU v7x, 512 devices: a whole 4x8x8 slice. The times are simulated.
512 devices in a mesh: dp: 8 (over y), feat: 64 (over x, z, core).
Axes of the slice: x: 4, y: 8, z: 8, core: 2. Of those that a mesh axis runs over, the one named last changes fastest.
Arguments:
- features: bfloat16 [8, 16384, 128], P('dp', None, 'feat'), may hold values from -6 to 6
- tile_weights: bfloat16 [8, 1536, 128, 128], P('dp', 'feat'), may hold values from -0.15625 to 0.15625
- tile_rows: int32 [8, 1536], P('dp', 'feat'), may hold values from 0 to 1
- tile_owners: int32 [8, 1536, 1], P('dp', 'feat'), may hold values from 0 to 63; in each aligned block of 24 rows (0 to 23, 24 to 47, ..., all dimensions but the last counted through in order) at most 2 rows name the same one
- tile_blocks: int32 [8, 1536], P('dp', 'feat'), may hold values from 0 to 1
- tile_counts: int32 [8, 64], P('dp', 'feat'), may hold values from 6 to 24, as said below
- cotangent: bfloat16 [8, 16384, 1024], P('dp', 'feat'), may hold values from -0.046875 to 0.046875
- w_self: bfloat16 [128, 1024], replicated, may hold values from -0.5 to 0.5
- w_neigh: bfloat16 [128, 1024], replicated, may hold values from -0.5 to 0.5
- bias: float32 [1024], replicated, may hold values from -4 to 4
Outputs:
- grad_self: float32 [128, 1024], P(None, 'feat')
- grad_neigh: float32 [128, 1024], P(None, 'feat')
- grad_bias: float32 [1024], P('feat')
Inputs may be any that keep to these rules, and one draw needn't show every extreme that they name: `tile_owners`: among the 24 tile slots of one device at most 2 name one owner, a bound that some block of them reaches. `tile_counts`: in every batch some device has all 24 slots live.
All inputs are finite; a program needn't handle non-finite values.
Results may differ from a plain program's by a relative error of at most 0.008.
Values may be sent and summed in bfloat16 or wider, within the bound.
No kernel may reach another device: no remote copies, remote signals or barrier semaphores. Data moves between devices by JAX's collectives and lax.ppermute only.
A program may use at most 64 MiB of HBM per device.

v0:
```python
import jax
import jax.numpy as jnp
from jax import lax
from jax.sharding import PartitionSpec as P


def silu_slope(pre_act):
    sigmoid_z = jax.nn.sigmoid(pre_act)
    return sigmoid_z * (1.0 + pre_act * (1.0 - sigmoid_z))


def local(
    features,
    tile_weights,
    tile_rows,
    tile_owners,
    tile_blocks,
    tile_counts,
    cotangent,
    w_self,
    w_neigh,
    bias,
):
    owned = lax.all_to_all(features, "feat", split_axis=1, concat_axis=2, tiled=True)[0]
    node_rows, feat_width = owned.shape
    slot_count = tile_weights.shape[1]
    tile_side = tile_weights.shape[2]
    row_blocks = node_rows // tile_side
    peer_count = lax.axis_size("feat")
    row_index = tile_rows[0]
    owner_index = tile_owners[0, :, 0]
    block_index = tile_blocks[0]
    live = jnp.arange(slot_count, dtype=jnp.int32) < tile_counts[0, 0]
    whole = lax.all_gather(owned, "feat", axis=0, tiled=True)
    picked = whole.reshape(-1, tile_side, feat_width)[owner_index * row_blocks + block_index]
    products = jnp.einsum(
        "kij,kjf->kif", tile_weights[0], picked, preferred_element_type=jnp.float32
    )
    select = (
        (row_index[None, :] == jnp.arange(row_blocks, dtype=jnp.int32)[:, None]) & live[None, :]
    ).astype(jnp.float32)
    summed = jnp.einsum("rk,kif->rif", select, products, precision=lax.Precision.HIGHEST)
    neighbour = summed.reshape(node_rows, feat_width).astype(jnp.bfloat16)
    pre_act = (
        jnp.dot(owned, w_self, preferred_element_type=jnp.float32)
        + jnp.dot(neighbour, w_neigh, preferred_element_type=jnp.float32)
        + bias
    )
    slope = (cotangent[0].astype(jnp.float32) * silu_slope(pre_act)).astype(jnp.bfloat16)
    grad_s = jnp.einsum("nf,nh->fh", owned, slope, preferred_element_type=jnp.float32)
    grad_n = jnp.einsum("nf,nh->fh", neighbour, slope, preferred_element_type=jnp.float32)
    grad_b = jnp.sum(slope.astype(jnp.float32), axis=0)
    total_s, total_n, total_b = lax.psum((grad_s, grad_n, grad_b), ("dp", "feat"))
    column_count = w_self.shape[1] // peer_count
    start = lax.axis_index("feat") * column_count
    out_s = lax.dynamic_slice_in_dim(total_s, start, column_count, 1)
    out_n = lax.dynamic_slice_in_dim(total_n, start, column_count, 1)
    out_b = lax.dynamic_slice_in_dim(total_b, start, column_count, 0)
    return (out_s, out_n, out_b)


def solution(mesh):
    return jax.shard_map(
        local,
        mesh=mesh,
        in_specs=(
            P("dp", None, "feat"),
            P("dp", "feat", None, None),
            P("dp", "feat"),
            P("dp", "feat", None),
            P("dp", "feat"),
            P("dp", "feat"),
            P("dp", "feat", None),
            P(),
            P(),
            P(),
        ),
        out_specs=(P(None, "feat"), P(None, "feat"), P("feat")),
        check_vma=False,
    )
```

profile of v0, /device:TPU:24, one launch (start us, length us, event | category | flops | bytes accessed | tf_op | source)
XLA Modules:
  0.0 554.2 jit_solution(6314317441695136422)
XLA Ops:
  7.2 15.4 %copy.26 = bf16[1,16384,2]{2,0,1:T(2,128)(2,1)} copy(bf16[1,16384,2]{1,2,0:T(2,128)(2,1)} %param.10) | data formatting | bytes 131072 | tf_op args[0]
  22.6 0.5 broadcast.52
  23.1 90.8 %reduce = bf16[16384,2]{1,0:T(8,128)(2,1)} reduce(bf16[16384,1,2]{2,1,0:T(2,128)(2,1)} %bitcast.51, bf16[]{:T(256)} %broadcast.52), dimensions={1}, to_apply=%bitcast.36.reduce_sub_computation | reduce | bytes 131074
  113.9 7.1 %reshape.61 = bf16[64,2,256]{2,1,0:T(2,128)(2,1)S(1)} reshape(bf16[16384,2]{1,0:T(8,128)(2,1)} %reduce) | data formatting | bytes 131072
  121.0 23.3 %all_to_all.15 = bf16[64,2,256]{2,1,0:T(2,128)(2,1)S(1)} all-to-all(bf16[64,2,256]{2,1,0:T(2,128)(2,1)S(1)} %reshape.61), channel_id=1, replica_groups=mesh['dp'=8,'feat'=64] {'feat'}, dimensions={0} | all-to-all | bytes 131072 | tf_op jit(solution)/shard_map/all_to_all | solution.py:24
  144.3 16.4 %reshape.62 = bf16[16384,1,2]{2,1,0:T(2,128)(2,1)} reshape(bf16[64,2,256]{2,1,0:T(2,128)(2,1)S(1)} %all_to_all.15) | data formatting | bytes 131072
  160.7 15.4 %copy.27 = bf16[1,16384,2]{1,2,0:T(2,128)(2,1)S(1)} copy(bf16[1,16384,2]{2,0,1:T(2,128)(2,1)} %bitcast.52) | data formatting | bytes 131072 | tf_op jit(solution)/shard_map/all_to_all | solution.py:24
  176.1 0.1 copy.28
  176.2 0.7 squeeze.14
  176.9 0.2 all-reduce.3.cloned.1.call-start
  177.8 1.2 fusion.10
  179.0 75.6 %all-gather.2.cloned.1.call-done = bf16[16384,128]{0,1:T(8,128)(2,1)} async-done(((bf16[256,128]{0,1:T(8,128)(2,1)}), bf16[16384,128]{0,1:T(8,128)(2,1)}) %all-gather.2.cloned.1.call-update) | async-done | bytes 4194320 | tf_op jit(solution)/shard_map/all_gather | solution.py:34
  254.6 6.4 %copy.29 = bf16[16384,128]{1,0:T(8,128)(2,1)} copy(bf16[16384,128]{0,1:T(8,128)(2,1)} %all-gather.2.cloned.1.call-done) | data formatting | bytes 8388608 | tf_op jit(solution)/shard_map/all_gather | solution.py:34
  261.0 2.9 gather_fusion
  264.0 1.9 convolution_bitcast_fusion
  265.8 2.0 copy.31
  267.8 0.6 convolution_convert_fusion
  268.5 1.8 convert_reduce_fusion
  270.2 1.1 fusion.11
  271.4 1.1 convolution_bitcast_fusion.1
  272.5 99.9 %psum.23 = f32[1024]{0:T(1024)S(1)} all-reduce(f32[1024]{0:T(1024)S(1)} %get-tuple-element.5), channel_id=1, replica_groups=mesh['dp'=8,'feat'=64] {'dp','feat'}, use_global_device_ids=true, to_apply=%region_3.0 | all-reduce | flops 1024 | bytes 8192 | tf_op jit(solution)/shard_map/psum | solution.py:53
  372.4 0.6 dynamic_slice.11
  373.0 173.0 %all-reduce.3.cloned.1.call-done = (f32[128,1024]{0,1:T(8,128)}, f32[128,1024]{0,1:T(8,128)}) async-done(((f32[128,1024]{0,1:T(8,128)}, f32[128,1024]{0,1:T(8,128)}), (f32[128,1024]{0,1:T(8,128)}, f32[128,1024]{0,1:T(8,128)})) %all-reduce.3.cloned.1.call-update) | async-done | bytes 1048592 | tf_op jit(solution)/shard_map/psum | solution.py:53
  546.0 1.3 constant_dynamic-slice_fusion
  (22 shorter events, 0.1 us)
Async XLA Ops:
  7.2 256.8 %copy-start = (bf16[1,24,128,128]{3,2,1,0:T(8,128)(2,1)S(1)}, bf16[1,24,128,128]{3,2,1,0:T(8,128)(2,1)}, u32[]{:S(2)}) copy-start(bf16[1,24,128,128]{3,2,1,0:T(8,128)(2,1)} %param.11) | copy-start | bytes 2359300
  7.2 247.4 %all-gather.2.cloned.1.call-start = ((), (), s32[]{:S(2)}) async-start(), calls=%async_computation.1 | async-start | bytes 4259840 | tf_op jit(solution)/shard_map/all_gather | solution.py:34
  160.7 17.1 %copy-start.5 = (s32[1,24]{1,0:T(1,128)S(1)}, s32[1,24]{1,0:T(1,128)}, u32[]{:S(2)}) copy-start(s32[1,24]{1,0:T(1,128)} %param.14) | copy-start | bytes 292
  160.7 17.1 %copy-start.6 = (s32[1,24,1]{1,2,0:T(1,128)S(1)}, s32[1,24,1]{1,2,0:T(1,128)}, u32[]{:S(2)}) copy-start(s32[1,24,1]{1,2,0:T(1,128)} %param.13) | copy-start | bytes 292
  160.7 17.1 %copy-start.2 = (bf16[128,1024]{1,0:T(8,128)(2,1)S(1)}, bf16[128,1024]{1,0:T(8,128)(2,1)}, u32[]{:S(2)}) copy-start(bf16[128,1024]{1,0:T(8,128)(2,1)} %param.17) | copy-start | bytes 786436
  176.9 369.1 %all-reduce.3.cloned.1.call-start = ((), (), s32[]{:S(2)}) async-start(), calls=%async_computation.2 | async-start | bytes 2097152 | tf_op jit(solution)/shard_map/psum | solution.py:53
  261.0 6.8 %copy-start.3 = (s32[1,24]{1,0:T(1,128)S(1)}, s32[1,24]{1,0:T(1,128)}, u32[]{:S(2)}) copy-start(s32[1,24]{1,0:T(1,128)} %param.12) | copy-start | bytes 292
  264.0 4.5 copy-start.4
  268.4 3.0 copy-start.1
Sparse Core Ops, SparseCore 0:
  177.0 77.5 all-gather.1
  272.7 273.2 all-reduce.2
where the time goes:
time: 556 us; the launch traced here: 554 us
  waiting for transfers between devices  249 us (45%)
  blocking collectives  123 us (22%)
  other arithmetic  90.8 us (16%)
  local copies, waits for them, and re-layouts  68.7 us (12%)
  between operations  14.9 us (3%)
  matrix products  7.67 us (1%)
    psum x1, waiting for transfers between devices, local(): lax.psum((grad_s, grad_n, grad_b), ('dp', 'feat'))  173 us
    psum x1, blocking collectives, local(): lax.psum((grad_s, grad_n, grad_b), ('dp', 'feat'))  99.9 us
    unnamed x1, other arithmetic  90.8 us
    all_gather x1, waiting for transfers between devices, local(): whole = lax.all_gather(owned, 'feat', axis=0, tiled=True)  75.6 us
    unnamed x19, local copies, waits for them, and re-layouts  39.5 us
    all_to_all x1, blocking collectives, local(): lax.all_to_all(features, 'feat', split_axis=1, concat_axis=2, tiled=True)[0]  23.3 us
    all_to_all x2, local copies, waits for them, and re-layouts, local(): lax.all_to_all(features, 'feat', split_axis=1, concat_axis=2, tiled=True)[0]  15.5 us
  transfers between devices with their start and end apart: 2, of which 2 were waited for; matrix products, arithmetic and copies ran while one was open for 0% of the time, Pallas kernels for 0%

commit v1 on v0

v1 whole, which is shorter than its diff:
```python
import jax
import jax.numpy as jnp
from jax import lax
from jax.experimental import pallas as pl
from jax.experimental.pallas import tpu as pltpu
from jax.sharding import Mesh, PartitionSpec as P

CORES = 2
LANES = 128
PAD_SLOTS = 32
BF16, F32 = jnp.bfloat16, jnp.float32
VMEM = pl.BlockSpec(memory_space=pltpu.VMEM)
SMEM = pl.BlockSpec(memory_space=pltpu.SMEM)
LIMIT = 56 * 1024 * 1024


def call(kernel, outs, specs, scratch=(), cost=None):
    return pl.pallas_call(
        kernel,
        out_shape=outs,
        in_specs=specs,
        out_specs=jax.tree.map(lambda _: VMEM, outs),
        scratch_shapes=list(scratch),
        compiler_params=pltpu.CompilerParams(vmem_limit_bytes=LIMIT),
        cost_estimate=cost,
    )


def pack_kernel(core_ref, lists_ref, own_ref, other_ref, sent_ref, pairs_ref):
    blocks = own_ref.shape[1] // LANES
    width = own_ref.shape[0]
    core = core_ref[0]
    for side, ref in enumerate((own_ref, other_ref)):
        place = side + core - 2 * side * core
        for b in range(blocks):
            pairs_ref[place, pl.ds(width * b, width), :] = ref[
                :, b * LANES : (b + 1) * LANES
            ].astype(F32)
    table = jnp.concatenate(
        [
            pairs_ref[c, pl.ds(f, blocks, stride=width), :].astype(BF16)
            for c in range(CORES)
            for f in range(width)
        ],
        axis=1,
    )
    group = LANES // PAD_SLOTS
    lane_group = lax.broadcasted_iota(jnp.int32, (1, LANES), 1) // PAD_SLOTS
    block_of = lax.broadcasted_iota(jnp.int32, (blocks, LANES), 0)
    for g in range(lists_ref.shape[0] // group):
        row = lists_ref[g * group]
        for j in range(1, group):
            row = jnp.where(lane_group == j, lists_ref[g * group + j], row)
        chosen = jnp.where(block_of == row, 1.0, 0.0).astype(BF16)
        sent_ref[g * LANES : (g + 1) * LANES, :] = lax.dot_general(
            chosen, table, (((0,), (0,)), ((), ())), preferred_element_type=F32
        ).astype(BF16)


def layer_kernel(
    core_ref,
    count_ref,
    rows_ref,
    got_ref,
    tiles_ref,
    cot_ref,
    w_self_ref,
    w_neigh_ref,
    bias_ref,
    kept_ref,
    away_ref,
    wide_ref,
    picked_ref,
    masked_ref,
    order_ref,
    grad_ref,
):
    columns = wide_ref.shape[0]
    slots, side = tiles_ref.shape[0], tiles_ref.shape[1]
    chips = got_ref.shape[0] // PAD_SLOTS
    feats = columns * chips
    for q in range(columns):
        wide_ref[q] = got_ref[:, q * LANES : (q + 1) * LANES].astype(F32)

    def block(slot):
        return jnp.concatenate(
            [wide_ref[q, pl.ds(slot, chips, stride=PAD_SLOTS), :] for q in range(columns)],
            axis=0,
        )

    row_blocks = masked_ref.shape[0] // side
    for s in range(slots):
        at = slice(s * side, (s + 1) * side)
        picked_ref[:, at] = block(s).astype(BF16)
        tile = tiles_ref[s]
        live = s < count_ref[0]
        for r in range(row_blocks):
            use = jnp.logical_and(live, rows_ref[s] == r)
            masked_ref[r * side : (r + 1) * side, at] = jnp.where(
                use, tile, jnp.zeros_like(tile)
            )
    agg = lax.dot_general(
        picked_ref[...],
        masked_ref[...],
        (((1,), (1,)), ((), ())),
        preferred_element_type=F32,
    )

    def node_major(r, value):
        for q in range(columns):
            order_ref[r, pl.ds(q, chips, stride=columns), :] = value[
                q * chips : (q + 1) * chips
            ]
        return order_ref[r].T.astype(BF16)

    nodes = []
    for r in range(row_blocks):
        nodes.append(
            jnp.concatenate(
                [
                    node_major(2 * r, block(slots + r)),
                    node_major(2 * r + 1, agg[:, r * side : (r + 1) * side]),
                ],
                axis=1,
            )
        )
    inputs = jnp.concatenate(nodes, axis=0)
    weights = jnp.concatenate([w_self_ref[...], w_neigh_ref[...]], axis=0)
    pre = jnp.dot(inputs, weights, preferred_element_type=F32) + bias_ref[...]
    s = jax.nn.sigmoid(pre)
    slope = (cot_ref[...].astype(F32) * (s * (1.0 + pre * (1.0 - s)))).astype(BF16)
    ones = jnp.ones((inputs.shape[0], LANES), BF16)
    grad_ref[...] = lax.dot_general(
        slope,
        jnp.concatenate([inputs, ones], axis=1),
        (((0,), (0,)), ((), ())),
        preferred_element_type=F32,
    )
    part = kept_ref.shape[0] // chips
    core = core_ref[0]
    for k in range(chips):
        at = slice(k * part, (k + 1) * part)
        here = pl.multiple_of(k * CORES * part + core * part, part)
        there = pl.multiple_of(k * CORES * part + (1 - core) * part, part)
        kept_ref[at, :] = grad_ref[pl.ds(here, part), :]
        away_ref[at, :] = grad_ref[pl.ds(there, part), :].astype(BF16)


def add_kernel(kept_ref, came_ref, out_ref):
    out_ref[...] = (kept_ref[...] + came_ref[...].astype(F32)).astype(BF16)


def spread_kernel(got_ref, out_ref):
    total = jnp.sum(got_ref[...].astype(F32), axis=0)
    for b in range(out_ref.shape[0]):
        out_ref[b] = total


def final_kernel(got_ref, self_ref, neigh_ref, bias_ref):
    total = jnp.sum(got_ref[...], axis=0)
    feats = self_ref.shape[1]
    self_ref[...] = total[:, :feats]
    neigh_ref[...] = total[:, feats : 2 * feats]
    bias_ref[...] = total[:, 2 * feats : 3 * feats].T[:1]


def local(
    features,
    tile_weights,
    tile_rows,
    tile_owners,
    tile_blocks,
    tile_counts,
    cotangent,
    w_self,
    w_neigh,
    bias,
):
    own = features[0].T
    width, node_count = own.shape
    slots, side = tile_weights.shape[1], tile_weights.shape[2]
    chips = lax.axis_size("chip")
    batches = lax.axis_size("dp")
    feats, hidden = w_self.shape
    nodes_here = cotangent.shape[1]
    row_blocks = nodes_here // side
    core = lax.axis_index("core")
    device = lax.axis_index("chip") * CORES + core
    swap = [(i, CORES - 1 - i) for i in range(CORES)]

    other = lax.ppermute(own, "core", swap)
    named = tile_owners[0, :, 0] * row_blocks + tile_blocks[0]
    mine = device * row_blocks + jnp.arange(row_blocks, dtype=jnp.int32)
    rest = jnp.zeros((PAD_SLOTS - slots - row_blocks,), jnp.int32)
    names = jnp.concatenate([named, mine, rest])
    names = jnp.broadcast_to(
        jnp.tile(names, LANES // PAD_SLOTS)[None, None], (chips, 1, LANES)
    )
    lists = lax.all_to_all(names, "chip", split_axis=0, concat_axis=0, tiled=True)

    core_at = core[None].astype(jnp.int32)
    columns = CORES * width
    sent = call(
        pack_kernel,
        jax.ShapeDtypeStruct((chips * PAD_SLOTS, columns * side), BF16),
        [SMEM, VMEM, VMEM, VMEM],
        [pltpu.VMEM((CORES, node_count // side * width, side), F32)],
    )(core_at, lists, own, other)
    got = lax.all_to_all(
        sent.reshape(chips, PAD_SLOTS, columns * side),
        "chip",
        split_axis=0,
        concat_axis=0,
        tiled=True,
    ).reshape(chips * PAD_SLOTS, columns * side)

    part = hidden // (chips * CORES)
    wide = 2 * feats + LANES
    kept, away = call(
        layer_kernel,
        (
            jax.ShapeDtypeStruct((chips * part, wide), F32),
            jax.ShapeDtypeStruct((chips * part, wide), BF16),
        ),
        [SMEM, SMEM, SMEM] + [VMEM] * 6,
        [
            pltpu.VMEM((columns, chips * PAD_SLOTS, side), F32),
            pltpu.VMEM((feats, slots * side), BF16),
            pltpu.VMEM((row_blocks * side, slots * side), BF16),
            pltpu.VMEM((2 * row_blocks, feats, side), F32),
            pltpu.VMEM((hidden, wide), F32),
        ],
    )(
        core_at,
        tile_counts[0],
        tile_rows[0],
        got,
        tile_weights[0],
        cotangent[0],
        w_self,
        w_neigh,
        bias[None],
    )
    came = lax.ppermute(away, "core", swap)
    summed = call(
        add_kernel,
        jax.ShapeDtypeStruct(away.shape, BF16),
        [VMEM, VMEM],
    )(kept, came).reshape(chips, part, wide)
    parts = lax.all_to_all(summed, "chip", split_axis=0, concat_axis=0, tiled=True)
    spread = call(
        spread_kernel, jax.ShapeDtypeStruct((batches, part, wide), F32), [VMEM]
    )(parts)
    totals = lax.all_to_all(spread, "dp", split_axis=0, concat_axis=0, tiled=True)
    out_s, out_n, out_b = call(
        final_kernel,
        (
            jax.ShapeDtypeStruct((part, feats), F32),
            jax.ShapeDtypeStruct((part, feats), F32),
            jax.ShapeDtypeStruct((1, part), F32),
        ),
        [VMEM],
    )(totals)
    return (out_s.T, out_n.T, out_b[0])


def solution(mesh):
    batches, owners = mesh.devices.shape
    split = Mesh(
        mesh.devices.reshape(batches, owners // CORES, CORES), ("dp", "chip", "core")
    )
    feat = ("chip", "core")
    return jax.shard_map(
        local,
        mesh=split,
        in_specs=(
            P("dp", None, feat),
            P("dp", feat, None, None),
            P("dp", feat),
            P("dp", feat, None),
            P("dp", feat),
            P("dp", feat),
            P("dp", feat, None),
            P(),
            P(),
            P(),
        ),
        out_specs=(P(None, feat), P(None, feat), P(feat)),
        check_vma=False,
    )
```

time: 556 us -> 115 us (0.21)
  the two profiles are of different devices: /device:TPU:24 before, /device:TPU:64 now
where the time goes in v1:
time: 115 us
  blocking collectives  58.6 us (51%)
  waiting for transfers between devices  29.6 us (26%)
  Pallas kernels  13.3 us (12%)
  starting transfers between devices  8.73 us (8%)
  local copies, waits for them, and re-layouts  3.1 us (3%)
  between operations  1.35 us (1%)
    all_to_all x1, waiting for transfers between devices, local(): lax.all_to_all(sent.reshape(chips, PAD_SLOTS, columns * side), 'chip', sp...  27.7 us
    all_to_all x1, blocking collectives, local(): lax.all_to_all(names, 'chip', split_axis=0, concat_axis=0, tiled=True)  21 us
    all_to_all x1, blocking collectives, local(): lax.all_to_all(summed, 'chip', split_axis=0, concat_axis=0, tiled=True)  20.6 us
    all_to_all x1, blocking collectives, local(): lax.all_to_all(spread, 'dp', split_axis=0, concat_axis=0, tiled=True)  17 us
    pallas_call x1, Pallas kernels, local(): call(layer_kernel, (jax.ShapeDtypeStruct((chips * part, wide), F32), jax....  5.61 us
    all_to_all x1, starting transfers between devices, local(): lax.all_to_all(sent.reshape(chips, PAD_SLOTS, columns * side), 'chip', sp...  4.9 us
    unnamed x10, local copies, waits for them, and re-layouts  2.99 us
    pallas_call x1, Pallas kernels, local(): call(pack_kernel, jax.ShapeDtypeStruct((chips * PAD_SLOTS, columns * side...  2.39 us
  transfers between devices with their start and end apart: 3, of which 2 were waited for; matrix products, arithmetic and copies ran while one was open for 0% of the time, Pallas kernels for 0%

profile of v1, /device:TPU:64, one launch (start us, length us, event | category | flops | bytes accessed | tf_op | source)
XLA Modules:
  0.0 114.8 jit_solution(14217248320906163370)
XLA Ops:
  0.6 1.9 %collective-permute-start = (bf16[2,16384]{1,0:T(2,128)(2,1)}, bf16[2,16384]{1,0:T(2,128)(2,1)S(1)}, u32[]{:S(2)}, u32[]{:S(2)}) collective-permute-start(bf16[2,16384]{1,0:T(2,128)(2,1)} %bitcast.25), channel_id=1, source_target_pairs={{0,1},{1,0},{2,3},{3,2},{4,5},{5,4},{6,7},{7,6},{8,9},{9,8},{10,11... | collective-permute-start | bytes 196616 | tf_op jit(solution)/shard_map/ppermute | solution.py:191
  2.6 0.0 copy-start.3
  2.6 0.0 copy-start.4
  2.6 0.6 copy-done.3
  3.2 0.0 copy-done.4
  3.2 0.1 pad_add_fusion
  3.3 0.1 broadcast_in_dim.14
  3.4 21.0 %all_to_all.20.lists_ref = s32[32,1,128]{2,1,0:T(1,128)} all-to-all(s32[32,1,128]{2,1,0:T(1,128)S(1)} %broadcast_in_dim.15), channel_id=1, replica_groups=mesh['dp'=8,'chip'=32,'core'=2] {'chip'}, dimensions={0} | all-to-all | bytes 32768 | tf_op jit(solution)/shard_map/all_to_all | solution.py:199
  24.5 0.0 collective-permute-done.other_ref
  24.5 0.0 copy-start.2
  24.5 0.6 copy-done.2
  25.1 2.4 %shard_map.121 = bf16[1024,512]{1,0:T(8,128)(2,1)} custom-call(s32[1]{0:T(128)} %bitcast.core_ref, s32[32,1,128]{2,1,0:T(1,128)} %all_to_all.20.lists_ref, bf16[2,16384]{1,0:T(2,128)(2,1)} %bitcast.26, bf16[2,16384]{1,0:T(2,128)(2,1)} %copy-done.2), custom_call_target="tpu_custom_call" | custom-call | tf_op jit(solution)/shard_map/pallas_call | solution.py:203
  27.5 4.9 %all-to-all-start.1 = ((bf16[32,32,512]{2,1,0:T(8,128)(2,1)}), bf16[32,32,512]{2,1,0:T(8,128)(2,1)S(1)}, u32[]{:S(2)}, u32[]{:S(2)}) async-start(bf16[32,32,512]{2,1,0:T(8,128)(2,1)} %bitcast.21), calls=%async_computation.1 | async-start | bytes 2097152 | tf_op jit(solution)/shard_map/all_to_all | solution.py:209
  33.1 27.7 %all-to-all-done.1 = bf16[32,32,512]{2,1,0:T(8,128)(2,1)S(1)} async-done(((bf16[32,32,512]{2,1,0:T(8,128)(2,1)}), bf16[32,32,512]{2,1,0:T(8,128)(2,1)S(1)}, u32[]{:S(2)}, u32[]{:S(2)}) %all-to-all-start.1) | async-done | bytes 1048608 | tf_op jit(solution)/shard_map/all_to_all | solution.py:209
  60.7 1.0 copy-done
  61.7 5.6 %shard_map.122 = (f32[512,384]{1,0:T(8,128)}, bf16[512,384]{1,0:T(8,128)(2,1)}) custom-call(s32[1]{0:T(128)} %bitcast.core_ref, s32[1]{0:T(128)} %bitcast.19.count_ref, s32[24]{0:T(128)} %bitcast.28, bf16[1024,512]{1,0:T(8,128)(2,1)} %bitcast.20, bf16[24,128,128]{2,1,0:T(8,128)(2,1)} %bitcast.23, bf16[256,1024]{1,0:T(8,128)(2,1)} %bitcast.24, ...), custom_call_target="tpu_custom_call" | custom-call | tf_op jit(solution)/shard_map/pallas_call | solution.py:219
  67.3 1.9 %collective-permute-start.1 = (bf16[512,384]{1,0:T(8,128)(2,1)}, bf16[512,384]{1,0:T(8,128)(2,1)S(1)}, u32[]{:S(2)}, u32[]{:S(2)}) collective-permute-start(bf16[512,384]{1,0:T(8,128)(2,1)} %get-tuple-element.9), channel_id=1, source_target_pairs={{0,1},{1,0},{2,3},{3,2},{4,5},{5,4},{6,7},{7,6},{8,9},{9,8},{10,11... | collective-permute-start | bytes 1179656 | tf_op jit(solution)/shard_map/ppermute | solution.py:244
  69.2 1.9 %collective-permute-done.1.came_ref = bf16[512,384]{1,0:T(8,128)(2,1)S(1)} collective-permute-done((bf16[512,384]{1,0:T(8,128)(2,1)}, bf16[512,384]{1,0:T(8,128)(2,1)S(1)}, u32[]{:S(2)}, u32[]{:S(2)}) %collective-permute-start.1) | collective-permute-done | bytes 393248 | tf_op jit(solution)/shard_map/ppermute | solution.py:244
  71.1 0.7 copy-done.1
  71.9 2.1 %shard_map.123 = bf16[512,384]{1,0:T(8,128)(2,1)} custom-call(f32[512,384]{1,0:T(8,128)} %get-tuple-element.8.kept_ref, bf16[512,384]{1,0:T(8,128)(2,1)} %copy-done.1), custom_call_target="tpu_custom_call" | custom-call | tf_op jit(solution)/shard_map/pallas_call | solution.py:245
  73.9 20.6 %all_to_all.21.got_ref = bf16[32,16,384]{2,1,0:T(8,128)(2,1)} all-to-all(bf16[32,16,384]{2,1,0:T(8,128)(2,1)} %bitcast.22), channel_id=1, replica_groups=mesh['dp'=8,'chip'=32,'core'=2] {'chip'}, dimensions={0} | all-to-all | bytes 786432 | tf_op jit(solution)/shard_map/all_to_all | solution.py:250
  94.5 1.7 %shard_map.124 = f32[8,16,384]{2,1,0:T(8,128)} custom-call(bf16[32,16,384]{2,1,0:T(8,128)(2,1)} %all_to_all.21.got_ref), custom_call_target="tpu_custom_call" | custom-call | tf_op jit(solution)/shard_map/pallas_call | solution.py:251
  96.3 17.0 %all_to_all.22.got_ref = f32[8,16,384]{2,1,0:T(8,128)} all-to-all(f32[8,16,384]{2,1,0:T(8,128)} %shard_map.124), channel_id=1, replica_groups=mesh['dp'=8,'chip'=32,'core'=2] {'dp'}, dimensions={0} | all-to-all | bytes 393216 | tf_op jit(solution)/shard_map/all_to_all | solution.py:254
  113.2 1.5 %shard_map.125 = (f32[16,128]{1,0:T(8,128)}, f32[16,128]{1,0:T(8,128)}, f32[1,16]{1,0:T(1,128)}) custom-call(f32[8,16,384]{2,1,0:T(8,128)} %all_to_all.22.got_ref), custom_call_target="tpu_custom_call" | custom-call | tf_op jit(solution)/shard_map/pallas_call | solution.py:255
  (7 shorter events, 0.0 us)
Async XLA Ops:
  0.6 23.9 %collective-permute-start = (bf16[2,16384]{1,0:T(2,128)(2,1)}, bf16[2,16384]{1,0:T(2,128)(2,1)S(1)}, u32[]{:S(2)}, u32[]{:S(2)}) collective-permute-start(bf16[2,16384]{1,0:T(2,128)(2,1)} %bitcast.25), channel_id=1, source_target_pairs={{0,1},{1,0},{2,3},{3,2},{4,5},{5,4},{6,7},{7,6},{8,9},{9,8},{10,11... | collective-permute-start | bytes 196616 | tf_op jit(solution)/shard_map/ppermute | solution.py:191
  2.6 0.7 copy-start.3
  2.6 0.7 copy-start.4
  24.5 0.6 copy-start.2
  27.5 33.2 %all-to-all-start.1 = ((bf16[32,32,512]{2,1,0:T(8,128)(2,1)}), bf16[32,32,512]{2,1,0:T(8,128)(2,1)S(1)}, u32[]{:S(2)}, u32[]{:S(2)}) async-start(bf16[32,32,512]{2,1,0:T(8,128)(2,1)} %bitcast.21), calls=%async_computation.1 | async-start | bytes 2097152 | tf_op jit(solution)/shard_map/all_to_all | solution.py:209
  60.7 1.0 copy-start
  67.3 3.8 %collective-permute-start.1 = (bf16[512,384]{1,0:T(8,128)(2,1)}, bf16[512,384]{1,0:T(8,128)(2,1)S(1)}, u32[]{:S(2)}, u32[]{:S(2)}) collective-permute-start(bf16[512,384]{1,0:T(8,128)(2,1)} %get-tuple-element.9), channel_id=1, source_target_pairs={{0,1},{1,0},{2,3},{3,2},{4,5},{5,4},{6,7},{7,6},{8,9},{9,8},{10,11... | collective-permute-start | bytes 1179656 | tf_op jit(solution)/shard_map/ppermute | solution.py:244
  71.1 0.7 copy-start.1

commit v2 on v0

v2 whole, which is shorter than its diff:
```python
import functools

import jax
import jax.numpy as jnp
from jax import lax
from jax.experimental import pallas as pl
from jax.experimental.pallas import tpu as pltpu
from jax.sharding import Mesh, PartitionSpec as P

CORES, DEPTH = 2, 8
LANES, SUBLANES = 128, 8
BF16, F32 = jnp.bfloat16, jnp.float32
VMEM = pl.BlockSpec(memory_space=pltpu.VMEM)
SMEM = pl.BlockSpec(memory_space=pltpu.SMEM)
MIB = 1024 * 1024
FIRST = (((0,), (0,)), ((), ()))
LAST = (((1,), (1,)), ((), ()))


def call(kernel, outs, specs, mib, scratch=()):
    return pl.pallas_call(
        kernel,
        out_shape=outs,
        in_specs=specs,
        out_specs=jax.tree.map(lambda _: VMEM, outs),
        scratch_shapes=list(scratch),
        compiler_params=pltpu.CompilerParams(vmem_limit_bytes=mib * MIB),
    )


def pack_kernel(lists_ref, whole_ref, sent_ref):
    depth, width = whole_ref.shape[0], whole_ref.shape[1]
    slots = sent_ref.shape[2] // LANES

    def peer(p, carry):
        for s in range(slots):
            at = pl.ds(pl.multiple_of(lists_ref[p, 0, s] * LANES, LANES), LANES)
            here = slice(s * LANES, (s + 1) * LANES)
            for z in range(depth):
                sent_ref[p, z * width : (z + 1) * width, here] = whole_ref[z, :, at]
        return carry

    lax.fori_loop(0, sent_ref.shape[0], peer, 0)


def gather_kernel(width, count_ref, rows_ref, got_ref, tiles_ref, inputs_ref, masked_ref):
    slots, side = tiles_ref.shape[0], tiles_ref.shape[1]
    feats = got_ref.shape[0]
    row_blocks = masked_ref.shape[0] // side
    for s in range(slots):
        tile = tiles_ref[s]
        live = s < count_ref[0]
        here = slice(s * side, (s + 1) * side)
        for r in range(row_blocks):
            use = jnp.logical_and(live, rows_ref[s] == r)
            masked_ref[r * side : (r + 1) * side, here] = jnp.where(
                use, tile, jnp.zeros_like(tile)
            )
    agg = lax.dot_general(
        got_ref[:, : slots * side],
        masked_ref[...],
        LAST,
        preferred_element_type=F32,
    ).astype(BF16)
    row = lax.broadcasted_iota(jnp.int32, (feats, feats), 0)
    feature = lax.broadcasted_iota(jnp.int32, (feats, feats), 1)
    column = row % width
    z = row // width % DEPTH
    core = row // (width * DEPTH) % CORES
    x = row // (width * DEPTH * CORES)
    place = ((x * DEPTH + z) * CORES + core) * width + column
    order = jnp.where(place == feature, 1.0, 0.0).astype(BF16)
    for k, value in enumerate((got_ref[:, slots * side :], agg)):
        inputs_ref[:, k * feats : (k + 1) * feats] = lax.dot_general(
            value, order, FIRST, preferred_element_type=F32
        ).astype(BF16)


def split_kernel(
    part,
    core_ref,
    cot_ref,
    w_self_ref,
    w_neigh_ref,
    bias_ref,
    mine_ref,
    theirs_ref,
    weights_ref,
    half_bias_ref,
):
    pair = CORES * LANES
    lane = lax.broadcasted_iota(jnp.int32, (pair, LANES), 0)
    to = lax.broadcasted_iota(jnp.int32, (pair, LANES), 1)
    group = to // part * (CORES * part) + to % part
    here = jnp.where(lane == group + core_ref[0] * part, 1.0, 0.0)
    there = jnp.where(lane == group + (1 - core_ref[0]) * part, 1.0, 0.0)
    here16, there16 = here.astype(BF16), there.astype(BF16)
    feats = w_self_ref.shape[0]

    def pick(value, chosen):
        return jnp.dot(value, chosen, preferred_element_type=F32).astype(BF16)

    for m in range(mine_ref.shape[1] // LANES):
        out = slice(m * LANES, (m + 1) * LANES)
        wide = slice(m * pair, (m + 1) * pair)
        mine_ref[:, out] = pick(cot_ref[:, wide], here16)
        theirs_ref[:, out] = pick(cot_ref[:, wide], there16)
        weights_ref[:feats, out] = pick(w_self_ref[:, wide], here16)
        weights_ref[feats:, out] = pick(w_neigh_ref[:, wide], here16)
        half_bias_ref[:, out] = jnp.dot(
            jnp.broadcast_to(bias_ref[:, wide], (SUBLANES, pair)),
            here,
            precision=lax.Precision.HIGHEST,
            preferred_element_type=F32,
        )[:1]


def layer_kernel(
    mine_ref, theirs_ref, cot_ref, their_cot_ref, weights_ref, bias_ref, sent_ref
):
    half = cot_ref.shape[1]
    weights, bias = weights_ref[...], bias_ref[...]
    total, sums = 0.0, 0.0
    for inputs, cot in (
        (mine_ref[...], cot_ref[...]),
        (theirs_ref[...], their_cot_ref[...]),
    ):
        pre = jnp.dot(inputs, weights, preferred_element_type=F32) + bias
        s = jax.nn.sigmoid(pre)
        slope = (cot.astype(F32) * (s * (1.0 + pre * (1.0 - s)))).astype(BF16)
        total += lax.dot_general(slope, inputs, FIRST, preferred_element_type=F32)
        sums += jnp.sum(slope.astype(F32), axis=0, keepdims=True)
    chips, rows = sent_ref.shape[0], sent_ref.shape[1]
    part = half // chips
    feats = total.shape[1] // 2
    total = total.astype(BF16)
    tail = jnp.concatenate(
        [sums[:, k * LANES : (k + 1) * LANES] for k in range(half // LANES)]
        + [jnp.zeros((SUBLANES - half // LANES, LANES), F32)],
        axis=0,
    ).astype(BF16)
    for k in range(chips):
        here = slice(k * part, (k + 1) * part)
        sent_ref[k, :part, :] = total[here, :feats]
        sent_ref[k, part : 2 * part, :] = total[here, feats:]
        sent_ref[k, 2 * part : rows, :] = tail


def spread_kernel(got_ref, out_ref):
    total = jnp.sum(got_ref[...].astype(F32), axis=0)
    for b in range(out_ref.shape[0]):
        out_ref[b] = total


def final_kernel(chip_ref, got_ref, self_ref, neigh_ref, bias_ref, sums_ref):
    part = self_ref.shape[0]
    total = jnp.sum(got_ref[...], axis=0)
    self_ref[...] = total[:part]
    neigh_ref[...] = total[part : 2 * part]
    sums_ref[...] = total[2 * part :]
    per_row = LANES // part
    row = sums_ref[pl.ds(chip_ref[0] // per_row, 1), :]
    lane = lax.broadcasted_iota(jnp.int32, (LANES, LANES), 0)
    to = lax.broadcasted_iota(jnp.int32, (LANES, LANES), 1)
    shift = chip_ref[0] % per_row * part
    moved = jnp.where(lane == to + shift, jnp.broadcast_to(row, (LANES, LANES)).T, 0.0)
    bias_ref[...] = jnp.sum(moved, axis=0, keepdims=True)[:, :part]


def local(
    features,
    tile_weights,
    tile_rows,
    tile_owners,
    tile_blocks,
    tile_counts,
    cotangent,
    w_self,
    w_neigh,
    bias,
):
    own = features[0].T
    width, node_count = own.shape
    slots, side = tile_weights.shape[1], tile_weights.shape[2]
    batches = lax.axis_size("dp")
    peers = lax.axis_size("x") * CORES
    chips = lax.axis_size("x") * DEPTH
    feats, hidden = w_self.shape
    nodes_here = cotangent.shape[1]
    row_blocks = nodes_here // side
    core = lax.axis_index("core")
    chip = lax.axis_index("x") * DEPTH + lax.axis_index("z")
    core_at, chip_at = core[None], chip[None]
    swap = [(i, CORES - 1 - i) for i in range(CORES)]

    whole = lax.all_to_all(
        jnp.broadcast_to(own[None], (DEPTH, width, node_count)),
        "z",
        split_axis=0,
        concat_axis=0,
        tiled=True,
    )
    half = hidden // CORES
    part = half // chips
    cot, away, weights, half_bias = call(
        functools.partial(split_kernel, part),
        (
            jax.ShapeDtypeStruct((nodes_here, half), BF16),
            jax.ShapeDtypeStruct((nodes_here, half), BF16),
            jax.ShapeDtypeStruct((2 * feats, half), BF16),
            jax.ShapeDtypeStruct((1, half), F32),
        ),
        [SMEM] + [VMEM] * 4,
        12,
    )(core_at, cotangent[0], w_self, w_neigh, bias[None])
    their_cot = lax.ppermute(away, "core", swap)
    named = tile_owners[0, :, 0] * row_blocks + tile_blocks[0]
    held = (chip * CORES + core) * row_blocks + jnp.arange(row_blocks, dtype=jnp.int32)
    names = jnp.pad(jnp.concatenate([named, held]), (0, LANES - slots - row_blocks))
    lists = lax.all_to_all(
        jnp.broadcast_to(names[None, None], (peers, 1, LANES)),
        ("x", "core"),
        split_axis=0,
        concat_axis=0,
        tiled=True,
    )
    sent = call(
        pack_kernel,
        jax.ShapeDtypeStruct((peers, DEPTH * width, (slots + row_blocks) * side), BF16),
        [SMEM, VMEM],
        8,
    )(lists, whole)
    got = lax.all_to_all(
        sent, ("x", "core"), split_axis=0, concat_axis=0, tiled=True
    ).reshape(feats, (slots + row_blocks) * side)
    mine = call(
        functools.partial(gather_kernel, width),
        jax.ShapeDtypeStruct((nodes_here, 2 * feats), BF16),
        [SMEM, SMEM, VMEM, VMEM],
        12,
        [pltpu.VMEM((row_blocks * side, slots * side), BF16)],
    )(tile_counts[0], tile_rows[0], got, tile_weights[0])
    theirs = lax.ppermute(mine, "core", swap)
    rows = 2 * part + SUBLANES
    sums = call(
        layer_kernel,
        jax.ShapeDtypeStruct((chips, rows, feats), BF16),
        [VMEM] * 6,
        16,
    )(mine, theirs, cot, their_cot, weights, half_bias)
    parts = lax.all_to_all(sums, ("x", "z"), split_axis=0, concat_axis=0, tiled=True)
    spread = call(
        spread_kernel,
        jax.ShapeDtypeStruct((batches, rows, feats), F32),
        [VMEM],
        4,
    )(parts)
    totals = lax.all_to_all(spread, "dp", split_axis=0, concat_axis=0, tiled=True)
    out_s, out_n, out_b = call(
        final_kernel,
        (
            jax.ShapeDtypeStruct((part, feats), F32),
            jax.ShapeDtypeStruct((part, feats), F32),
            jax.ShapeDtypeStruct((1, part), F32),
        ),
        [SMEM, VMEM],
        4,
        [pltpu.VMEM((SUBLANES, LANES), F32)],
    )(chip_at, totals)
    return (out_s.T, out_n.T, out_b[0])


def solution(mesh):
    batches, owners = mesh.devices.shape
    split = Mesh(
        mesh.devices.reshape(batches, owners // (DEPTH * CORES), DEPTH, CORES),
        ("dp", "x", "z", "core"),
    )
    feat = ("x", "z", "core")
    return jax.shard_map(
        local,
        mesh=split,
        in_specs=(
            P("dp", None, feat),
            P("dp", feat, None, None),
            P("dp", feat),
            P("dp", feat, None),
            P("dp", feat),
            P("dp", feat),
            P("dp", feat, None),
            P(),
            P(),
            P(),
        ),
        out_specs=(P(None, feat), P(None, feat), P(feat)),
        check_vma=False,
    )
```

time: 556 us -> 100 us (0.18)
  the two profiles are of different devices: /device:TPU:24 before, /device:TPU:64 now
where the time goes in v2:
time: 100 us; the launch traced here: 99.7 us
  blocking collectives  69.8 us (70%)
  waiting for transfers between devices  11.2 us (11%)
  starting transfers between devices  7.9 us (8%)
  Pallas kernels  6.77 us (7%)
  local copies, waits for them, and re-layouts  2.44 us (2%)
  between operations  1.42 us (1%)
    all_to_all x1, blocking collectives, local(): lax.all_to_all(jnp.broadcast_to(own[None], (DEPTH, width, node_count)), '...  25.8 us
    all_to_all x1, blocking collectives, local(): lax.all_to_all(sums, ('x', 'z'), split_axis=0, concat_axis=0, tiled=True)  18.4 us
    all_to_all x1, blocking collectives, local(): lax.all_to_all(spread, 'dp', split_axis=0, concat_axis=0, tiled=True)  16.3 us
    all_to_all x1, waiting for transfers between devices, local(): lax.all_to_all(sent, ('x', 'core'), split_axis=0, concat_axis=0, tiled=True)  9.94 us
    all_to_all x1, blocking collectives, local(): lax.all_to_all(jnp.broadcast_to(names[None, None], (peers, 1, LANES)), ('...  9.35 us
    all_to_all x1, starting transfers between devices, local(): lax.all_to_all(sent, ('x', 'core'), split_axis=0, concat_axis=0, tiled=True)  3.69 us
    pallas_call x1, Pallas kernels, local(): call(pack_kernel, jax.ShapeDtypeStruct((peers, DEPTH * width, (slots + ro...  2.87 us
    ppermute x1, starting transfers between devices, local(): their_cot = lax.ppermute(away, 'core', swap)  2.29 us
  transfers between devices with their start and end apart: 3, of which 2 were waited for; matrix products, arithmetic and copies ran while one was open for 0% of the time, Pallas kernels for 2%

profile of v2, /device:TPU:64, one launch (start us, length us, event | category | flops | bytes accessed | tf_op | source)
XLA Modules:
  0.0 99.7 jit_solution(15595125323663204248)
XLA Ops:
  0.6 0.0 copy-start.6
  0.7 0.0 copy-start.7
  0.7 0.6 copy-done.6
  1.3 0.0 copy-done.7
  1.3 0.1 pad_add_fusion
  1.4 9.3 %all_to_all.25.lists_ref = s32[8,1,128]{2,1,0:T(1,128)S(1)} all-to-all(s32[8,1,128]{2,1,0:T(1,128)S(1)} %broadcast_in_dim.22), channel_id=1, replica_groups=mesh['dp'=8,'x'=4,'z'=8,'core'=2] {'x','core'}, dimensions={0} | all-to-all | bytes 8192 | tf_op jit(solution)/shard_map/all_to_all | solution.py:220
  10.8 1.1 %broadcast_in_dim.23 = bf16[8,2,16384]{2,1,0:T(2,128)(2,1)S(1)} broadcast(bf16[2,16384]{1,0:T(2,128)(2,1)} %bitcast.24), dimensions={1,2} | broadcast | bytes 589824 | tf_op jit(solution)/shard_map/broadcast_in_dim | solution.py:197
  11.9 25.8 %all_to_all.26.whole_ref = bf16[8,2,16384]{2,1,0:T(2,128)(2,1)S(1)} all-to-all(bf16[8,2,16384]{2,1,0:T(2,128)(2,1)S(1)} %broadcast_in_dim.23), channel_id=1, replica_groups=mesh['dp'=8,'x'=4,'z'=8,'core'=2] {'z'}, dimensions={0} | all-to-all | bytes 1048576 | tf_op jit(solution)/shard_map/all_to_all | solution.py:196
  37.7 2.9 %shard_map.121 = bf16[8,16,3328]{2,1,0:T(8,128)(2,1)} custom-call(s32[8,1,128]{2,1,0:T(1,128)S(1)} %all_to_all.25.lists_ref, bf16[8,2,16384]{2,1,0:T(2,128)(2,1)S(1)} %all_to_all.26.whole_ref), custom_call_target="tpu_custom_call" | custom-call | tf_op jit(solution)/shard_map/pallas_call | solution.py:227
  40.5 3.7 %all-to-all-start.2 = ((bf16[8,16,3328]{2,1,0:T(8,128)(2,1)}), bf16[8,16,3328]{2,1,0:T(8,128)(2,1)S(1)}, u32[]{:S(2)}, u32[]{:S(2)}) async-start(bf16[8,16,3328]{2,1,0:T(8,128)(2,1)} %shard_map.121), calls=%async_computation.2 | async-start | bytes 1703936 | tf_op jit(solution)/shard_map/all_to_all | solution.py:233
  44.2 0.0 copy-start
  44.3 0.8 shard_map.123
  45.1 2.3 %collective-permute-start.1 = (bf16[256,512]{1,0:T(8,128)(2,1)S(1)}, bf16[256,512]{1,0:T(8,128)(2,1)S(1)}, u32[]{:S(2)}, u32[]{:S(2)}) collective-permute-start(bf16[256,512]{1,0:T(8,128)(2,1)S(1)} %get-tuple-element.11), channel_id=1, source_target_pairs={{0,1},{1,0},{2,3},{3,2},{4,5},{5,4},{6,7},{7,6},{8,9},{9,8},{10,11... | collective-permute-start | bytes 786440 | tf_op jit(solution)/shard_map/ppermute | solution.py:216
  48.1 9.9 %all-to-all-done.2 = bf16[8,16,3328]{2,1,0:T(8,128)(2,1)S(1)} async-done(((bf16[8,16,3328]{2,1,0:T(8,128)(2,1)}), bf16[8,16,3328]{2,1,0:T(8,128)(2,1)S(1)}, u32[]{:S(2)}, u32[]{:S(2)}) %all-to-all-start.2) | async-done | bytes 852000 | tf_op jit(solution)/shard_map/all_to_all | solution.py:233
  58.0 0.7 copy-done.5
  58.7 1.5 %shard_map.122.mine_ref = bf16[256,256]{1,0:T(8,128)(2,1)S(1)} custom-call(s32[1]{0:T(128)} %bitcast.18.count_ref, s32[24]{0:T(128)S(1)} %bitcast.23, bf16[128,3328]{1,0:T(8,128)(2,1)S(1)} %bitcast.19, bf16[24,128,128]{2,1,0:T(8,128)(2,1)S(1)} %bitcast.20), custom_call_target="tpu_custom_call" | custom-call | tf_op jit(solution)/shard_map/pallas_call | solution.py:236
  60.2 1.9 %collective-permute-start = (bf16[256,256]{1,0:T(8,128)(2,1)S(1)}, bf16[256,256]{1,0:T(8,128)(2,1)S(1)}, u32[]{:S(2)}, u32[]{:S(2)}) collective-permute-start(bf16[256,256]{1,0:T(8,128)(2,1)S(1)} %shard_map.122.mine_ref), channel_id=1, source_target_pairs={{0,1},{1,0},{2,3},{3,2},{4,5},{5,4},{6,7},{7,6},{8,9},{9,8},{10,11... | collective-permute-start | bytes 393224 | tf_op jit(solution)/shard_map/ppermute | solution.py:243
  62.1 0.0 collective-permute-done.1.their_cot_ref
  62.1 1.3 %collective-permute-done.theirs_ref = bf16[256,256]{1,0:T(8,128)(2,1)S(1)} collective-permute-done((bf16[256,256]{1,0:T(8,128)(2,1)S(1)}, bf16[256,256]{1,0:T(8,128)(2,1)S(1)}, u32[]{:S(2)}, u32[]{:S(2)}) %collective-permute-start) | collective-permute-done | bytes 131104 | tf_op jit(solution)/shard_map/ppermute | solution.py:243
  63.4 0.9 shard_map.124
  64.3 18.4 %all_to_all.27.got_ref = bf16[32,40,128]{2,1,0:T(8,128)(2,1)S(1)} all-to-all(bf16[32,40,128]{2,1,0:T(8,128)(2,1)S(1)} %shard_map.124), channel_id=1, replica_groups=mesh['dp'=8,'x'=4,'z'=8,'core'=2] {'x','z'}, dimensions={0} | all-to-all | bytes 655360 | tf_op jit(solution)/shard_map/all_to_all | solution.py:251
  82.7 0.1 shard_map.125
  82.8 16.3 %all_to_all.28.got_ref = f32[8,40,128]{2,1,0:T(8,128)S(1)} all-to-all(f32[8,40,128]{2,1,0:T(8,128)S(1)} %shard_map.125), channel_id=1, replica_groups=mesh['dp'=8,'x'=4,'z'=8,'core'=2] {'dp'}, dimensions={0} | all-to-all | bytes 327680 | tf_op jit(solution)/shard_map/all_to_all | solution.py:258
  99.1 0.6 shard_map.126
  (14 shorter events, 0.0 us)
Async XLA Ops:
  0.6 0.7 copy-start.6
  0.7 0.7 copy-start.7
  40.5 3.7 %copy-start.1 = (bf16[1,256,1024]{2,1,0:T(8,128)(2,1)S(1)}, bf16[1,256,1024]{2,1,0:T(8,128)(2,1)}, u32[]{:S(2)}) copy-start(bf16[1,256,1024]{2,1,0:T(8,128)(2,1)} %param.16) | copy-start | bytes 1572868
  40.5 3.7 %copy-start.2 = (bf16[128,1024]{1,0:T(8,128)(2,1)S(1)}, bf16[128,1024]{1,0:T(8,128)(2,1)}, u32[]{:S(2)}) copy-start(bf16[128,1024]{1,0:T(8,128)(2,1)} %w_self_ref.1) | copy-start | bytes 786436
  40.5 3.7 %copy-start.3 = (bf16[128,1024]{1,0:T(8,128)(2,1)S(1)}, bf16[128,1024]{1,0:T(8,128)(2,1)}, u32[]{:S(2)}) copy-start(bf16[128,1024]{1,0:T(8,128)(2,1)} %w_neigh_ref.1) | copy-start | bytes 786436
  40.5 3.7 %copy-start.4 = (f32[1024]{0:T(1024)S(1)}, f32[1024]{0:T(1024)}, u32[]{:S(2)}) copy-start(f32[1024]{0:T(1024)} %param.19) | copy-start | bytes 12292
  40.5 17.5 %all-to-all-start.2 = ((bf16[8,16,3328]{2,1,0:T(8,128)(2,1)}), bf16[8,16,3328]{2,1,0:T(8,128)(2,1)S(1)}, u32[]{:S(2)}, u32[]{:S(2)}) async-start(bf16[8,16,3328]{2,1,0:T(8,128)(2,1)} %shard_map.121), calls=%async_computation.2 | async-start | bytes 1703936 | tf_op jit(solution)/shard_map/all_to_all | solution.py:233
  44.2 13.8 %copy-start = (bf16[1,24,128,128]{3,2,1,0:T(8,128)(2,1)S(1)}, bf16[1,24,128,128]{3,2,1,0:T(8,128)(2,1)}, u32[]{:S(2)}) copy-start(bf16[1,24,128,128]{3,2,1,0:T(8,128)(2,1)} %param.11) | copy-start | bytes 2359300
  45.1 17.0 %collective-permute-start.1 = (bf16[256,512]{1,0:T(8,128)(2,1)S(1)}, bf16[256,512]{1,0:T(8,128)(2,1)S(1)}, u32[]{:S(2)}, u32[]{:S(2)}) collective-permute-start(bf16[256,512]{1,0:T(8,128)(2,1)S(1)} %get-tuple-element.11), channel_id=1, source_target_pairs={{0,1},{1,0},{2,3},{3,2},{4,5},{5,4},{6,7},{7,6},{8,9},{9,8},{10,11... | collective-permute-start | bytes 786440 | tf_op jit(solution)/shard_map/ppermute | solution.py:216
  58.0 0.7 copy-start.5
  60.2 3.2 %collective-permute-start = (bf16[256,256]{1,0:T(8,128)(2,1)S(1)}, bf16[256,256]{1,0:T(8,128)(2,1)S(1)}, u32[]{:S(2)}, u32[]{:S(2)}) collective-permute-start(bf16[256,256]{1,0:T(8,128)(2,1)S(1)} %shard_map.122.mine_ref), channel_id=1, source_target_pairs={{0,1},{1,0},{2,3},{3,2},{4,5},{5,4},{6,7},{7,6},{8,9},{9,8},{10,11... | collective-permute-start | bytes 393224 | tf_op jit(solution)/shard_map/ppermute | solution.py:243

commit v3 on v2

--- a/solution.py
+++ b/solution.py
@@ -28,36 +28,31 @@
     )
 
 
-def pack_kernel(lists_ref, whole_ref, sent_ref):
+def pack_kernel(at_ref, *refs):
+    *lists_refs, whole_ref, sent_ref = refs
     depth, width = whole_ref.shape[0], whole_ref.shape[1]
     slots = sent_ref.shape[2] // LANES
-
-    def peer(p, carry):
-        for s in range(slots):
-            at = pl.ds(pl.multiple_of(lists_ref[p, 0, s] * LANES, LANES), LANES)
-            here = slice(s * LANES, (s + 1) * LANES)
-            for z in range(depth):
-                sent_ref[p, z * width : (z + 1) * width, here] = whole_ref[z, :, at]
-        return carry
-
-    lax.fori_loop(0, sent_ref.shape[0], peer, 0)
-
-
-def gather_kernel(width, count_ref, rows_ref, got_ref, tiles_ref, inputs_ref, masked_ref):
-    slots, side = tiles_ref.shape[0], tiles_ref.shape[1]
+    reach = len(lists_refs)
+    for step, lists_ref in enumerate(lists_refs):
+        x = lax.rem(at_ref[0] + reach - step, reach)
+
+        def peer(side, carry, x=x, lists_ref=lists_ref):
+            p = x * CORES + lax.rem(at_ref[1] + side, CORES)
+            for s in range(slots):
+                at = pl.ds(pl.multiple_of(lists_ref[side, s] * LANES, LANES), LANES)
+                here = slice(s * LANES, (s + 1) * LANES)
+                for z in range(depth):
+                    sent_ref[p, z * width : (z + 1) * width, here] = whole_ref[z, :, at]
+            return carry
+
+        lax.fori_loop(0, CORES, peer, 0)
+
+
+def gather_kernel(width, got_ref, masked_ref, inputs_ref):
     feats = got_ref.shape[0]
-    row_blocks = masked_ref.shape[0] // side
-    for s in range(slots):
-        tile = tiles_ref[s]
-        live = s < count_ref[0]
-        here = slice(s * side, (s + 1) * side)
-        for r in range(row_blocks):
-            use = jnp.logical_and(live, rows_ref[s] == r)
-            masked_ref[r * side : (r + 1) * side, here] = jnp.where(
-                use, tile, jnp.zeros_like(tile)
-            )
+    named = masked_ref.shape[1]
     agg = lax.dot_general(
-        got_ref[:, : slots * side],
+        got_ref[:, :named],
         masked_ref[...],
         LAST,
         preferred_element_type=F32,
@@ -70,7 +65,7 @@
     x = row // (width * DEPTH * CORES)
     place = ((x * DEPTH + z) * CORES + core) * width + column
     order = jnp.where(place == feature, 1.0, 0.0).astype(BF16)
-    for k, value in enumerate((got_ref[:, slots * side :], agg)):
+    for k, value in enumerate((got_ref[:, named:], agg)):
         inputs_ref[:, k * feats : (k + 1) * feats] = lax.dot_general(
             value, order, FIRST, preferred_element_type=F32
         ).astype(BF16)
@@ -83,11 +78,21 @@
     w_self_ref,
     w_neigh_ref,
     bias_ref,
+    rows_ref,
+    tiles_ref,
     mine_ref,
     theirs_ref,
     weights_ref,
     half_bias_ref,
+    masked_ref,
 ):
+    slots, side = tiles_ref.shape[0], tiles_ref.shape[1]
+    for s in range(slots):
+        tile = tiles_ref[s]
+        for r in range(masked_ref.shape[0] // side):
+            masked_ref[r * side : (r + 1) * side, s * side : (s + 1) * side] = jnp.where(
+                rows_ref[s] == r, tile, jnp.zeros_like(tile)
+            )
     pair = CORES * LANES
     lane = lax.broadcasted_iota(jnp.int32, (pair, LANES), 0)
     to = lax.broadcasted_iota(jnp.int32, (pair, LANES), 1)
@@ -147,14 +152,14 @@
 
 
 def spread_kernel(got_ref, out_ref):
-    total = jnp.sum(got_ref[...].astype(F32), axis=0)
+    total = jnp.sum(got_ref[...].astype(F32), axis=0).astype(BF16)
     for b in range(out_ref.shape[0]):
         out_ref[b] = total
 
 
 def final_kernel(chip_ref, got_ref, self_ref, neigh_ref, bias_ref, sums_ref):
     part = self_ref.shape[0]
-    total = jnp.sum(got_ref[...], axis=0)
+    total = jnp.sum(got_ref[...].astype(F32), axis=0)
     self_ref[...] = total[:part]
     neigh_ref[...] = total[part : 2 * part]
     sums_ref[...] = total[2 * part :]
@@ -202,44 +207,46 @@
     )
     half = hidden // CORES
     part = half // chips
-    cot, away, weights, half_bias = call(
+    live = jnp.arange(slots, dtype=jnp.int32) < tile_counts[0, 0]
+    rows_live = jnp.where(live, tile_rows[0], -1)
+    cot, away, weights, half_bias, masked = call(
         functools.partial(split_kernel, part),
         (
             jax.ShapeDtypeStruct((nodes_here, half), BF16),
             jax.ShapeDtypeStruct((nodes_here, half), BF16),
             jax.ShapeDtypeStruct((2 * feats, half), BF16),
             jax.ShapeDtypeStruct((1, half), F32),
+            jax.ShapeDtypeStruct((row_blocks * side, slots * side), BF16),
         ),
-        [SMEM] + [VMEM] * 4,
+        [SMEM] + [VMEM] * 4 + [SMEM, VMEM],
         12,
-    )(core_at, cotangent[0], w_self, w_neigh, bias[None])
+    )(core_at, cotangent[0], w_self, w_neigh, bias[None], rows_live, tile_weights[0])
     their_cot = lax.ppermute(away, "core", swap)
     named = tile_owners[0, :, 0] * row_blocks + tile_blocks[0]
     held = (chip * CORES + core) * row_blocks + jnp.arange(row_blocks, dtype=jnp.int32)
     names = jnp.pad(jnp.concatenate([named, held]), (0, LANES - slots - row_blocks))
-    lists = lax.all_to_all(
-        jnp.broadcast_to(names[None, None], (peers, 1, LANES)),
-        ("x", "core"),
-        split_axis=0,
-        concat_axis=0,
-        tiled=True,
-    )
+    names = names[None]
+    pair = jnp.concatenate([names, lax.ppermute(names, "core", swap)], axis=0)
+    reach = lax.axis_size("x")
+    lists = [pair] + [
+        lax.ppermute(pair, "x", [(i, (i + step) % reach) for i in range(reach)])
+        for step in range(1, reach)
+    ]
     sent = call(
         pack_kernel,
         jax.ShapeDtypeStruct((peers, DEPTH * width, (slots + row_blocks) * side), BF16),
-        [SMEM, VMEM],
+        [SMEM] * (1 + reach) + [VMEM],
         8,
-    )(lists, whole)
+    )(jnp.stack([lax.axis_index("x"), core]), *lists, whole)
     got = lax.all_to_all(
         sent, ("x", "core"), split_axis=0, concat_axis=0, tiled=True
     ).reshape(feats, (slots + row_blocks) * side)
     mine = call(
         functools.partial(gather_kernel, width),
         jax.ShapeDtypeStruct((nodes_here, 2 * feats), BF16),
-        [SMEM, SMEM, VMEM, VMEM],
+        [VMEM, VMEM],
         12,
-        [pltpu.VMEM((row_blocks * side, slots * side), BF16)],
-    )(tile_counts[0], tile_rows[0], got, tile_weights[0])
+    )(got, masked)
     theirs = lax.ppermute(mine, "core", swap)
     rows = 2 * part + SUBLANES
     sums = call(
@@ -251,7 +258,7 @@
     parts = lax.all_to_all(sums, ("x", "z"), split_axis=0, concat_axis=0, tiled=True)
     spread = call(
         spread_kernel,
-        jax.ShapeDtypeStruct((batches, rows, feats), F32),
+        jax.ShapeDtypeStruct((batches, rows, feats), BF16),
         [VMEM],
         4,
     )(parts)

time: 100 us -> 93.6 us (0.936)
  blocking collectives: 69.8 us -> 37.1 us
  starting transfers between devices: 7.9 us -> 30.1 us
  local copies, waits for them, and re-layouts: 2.44 us -> 5.34 us
  Pallas kernels: 6.77 us -> 7.83 us
    all_to_all x2 -> x0, blocking collectives: 35.1 us -> none  [the longest x1 25.8 us: local(): lax.all_to_all(jnp.broadcast_to(own[None], (DEPTH, width, node_count)), '...]
    ppermute x0 -> x4, starting transfers between devices: none -> 12.2 us  [the longest x3 10.2 us: local(): lax.ppermute(pair, 'x', [(i, (i + step) % reach) for i in range(reach)])]
    all_to_all x0 -> x1, starting transfers between devices: none -> 9.96 us  [local(): lax.all_to_all(jnp.broadcast_to(own[None], (DEPTH, width, node_count)), '...]
    all_to_all x1, waiting for transfers between devices: 9.94 us -> 4.78 us  [local(): lax.all_to_all(sent, ('x', 'core'), split_axis=0, concat_axis=0, tiled=True)]
    ppermute x0 -> x4, waiting for transfers between devices: none -> 4.88 us  [the longest x3 3.79 us: local(): lax.ppermute(pair, 'x', [(i, (i + step) % reach) for i in range(reach)])]
    all_to_all x1, blocking collectives: 18.4 us -> 21.6 us  [local(): lax.all_to_all(sums, ('x', 'z'), split_axis=0, concat_axis=0, tiled=True)]
    unnamed x16 -> x24, local copies, waits for them, and re-layouts: 1.32 us -> 3.41 us
    pallas_call x1, Pallas kernels: 0.84 us -> 2.46 us  [local(): call(functools.partial(split_kernel, part), (jax.ShapeDtypeStruct((nodes_...]
  transfers between devices with their start and end apart: 3 -> 8, of which waited for: 2 -> 5; matrix products, arithmetic and copies ran while one was open for 0% -> 0% of each run, Pallas kernels for 2% -> 4%
where the time goes in v3:
time: 93.6 us; the launch traced here: 93 us
  blocking collectives  37.1 us (40%)
  starting transfers between devices  30.1 us (32%)
  waiting for transfers between devices  11 us (12%)
  Pallas kernels  7.83 us (8%)
  local copies, waits for them, and re-layouts  5.34 us (6%)
  between operations  1.49 us (2%)
    all_to_all x1, blocking collectives, local(): lax.all_to_all(sums, ('x', 'z'), split_axis=0, concat_axis=0, tiled=True)  21.6 us
    all_to_all x1, blocking collectives, local(): lax.all_to_all(spread, 'dp', split_axis=0, concat_axis=0, tiled=True)  15.5 us
    ppermute x3, starting transfers between devices, local(): lax.ppermute(pair, 'x', [(i, (i + step) % reach) for i in range(reach)])  10.2 us
    all_to_all x1, starting transfers between devices, local(): lax.all_to_all(jnp.broadcast_to(own[None], (DEPTH, width, node_count)), '...  9.96 us
    all_to_all x1, waiting for transfers between devices, local(): lax.all_to_all(sent, ('x', 'core'), split_axis=0, concat_axis=0, tiled=True)  4.78 us
    ppermute x3, waiting for transfers between devices, local(): lax.ppermute(pair, 'x', [(i, (i + step) % reach) for i in range(reach)])  3.79 us
    all_to_all x1, starting transfers between devices, local(): lax.all_to_all(sent, ('x', 'core'), split_axis=0, concat_axis=0, tiled=True)  3.55 us
    unnamed x24, local copies, waits for them, and re-layouts  3.41 us
  transfers between devices with their start and end apart: 8, of which 5 were waited for; matrix products, arithmetic and copies ran while one was open for 0% of the time, Pallas kernels for 4%

profile of v3, /device:TPU:64, one launch (start us, length us, event | category | flops | bytes accessed | tf_op | source)
XLA Modules:
  0.0 93.0 jit_solution(7543553926678409710)
XLA Ops:
  0.7 1.9 %broadcast_in_dim.22 = bf16[8,2,16384]{2,1,0:T(2,128)(2,1)} broadcast(bf16[2,16384]{1,0:T(2,128)(2,1)} %bitcast.27), dimensions={1,2} | broadcast | bytes 589824 | tf_op jit(solution)/shard_map/broadcast_in_dim | solution.py:202
  2.6 10.0 %all-to-all-start = ((bf16[8,2,16384]{2,1,0:T(2,128)(2,1)}), bf16[8,2,16384]{2,1,0:T(2,128)(2,1)S(1)}, u32[]{:S(2)}, u32[]{:S(2)}) async-start(bf16[8,2,16384]{2,1,0:T(2,128)(2,1)} %broadcast_in_dim.22), calls=%async_computation | async-start | bytes 1048576 | tf_op jit(solution)/shard_map/all_to_all | solution.py:201
  12.7 2.0 %collective-permute-start = (s32[1,128]{1,0:T(1,128)S(1)}, s32[1,128]{1,0:T(1,128)S(1)}, u32[]{:S(2)}, u32[]{:S(2)}) collective-permute-start(s32[1,128]{1,0:T(1,128)S(1)} %pad_bitcast_fusion), channel_id=1, source_target_pairs={{0,1},{1,0},{2,3},{3,2},{4,5},{5,4},{6,7},{7,6},{8,9},{9,8},{10,11... | collective-permute-start | bytes 1544 | tf_op jit(solution)/shard_map/ppermute | solution.py:229
  14.8 1.1 %collective-permute-done = s32[1,128]{1,0:T(1,128)S(1)} collective-permute-done((s32[1,128]{1,0:T(1,128)S(1)}, s32[1,128]{1,0:T(1,128)S(1)}, u32[]{:S(2)}, u32[]{:S(2)}) %collective-permute-start) | collective-permute-done | bytes 544 | tf_op jit(solution)/shard_map/ppermute | solution.py:229
  15.8 4.7 %collective-permute-start.3 = (s32[2,128]{1,0:T(2,128)S(1)}, s32[2,128]{1,0:T(2,128)S(1)}, u32[]{:S(2)}, u32[]{:S(2)}) collective-permute-start(s32[2,128]{1,0:T(2,128)S(1)} %pad_add_fusion.refs_0_), channel_id=1, source_target_pairs={{0,48},{16,0},{32,16},{48,32},{1,49},{17,1},{33,17},{49,33},{2,50}... | collective-permute-start | bytes 3080 | tf_op jit(solution)/shard_map/ppermute | solution.py:232
  20.5 2.7 %collective-permute-start.2 = (s32[2,128]{1,0:T(2,128)S(1)}, s32[2,128]{1,0:T(2,128)S(1)}, u32[]{:S(2)}, u32[]{:S(2)}) collective-permute-start(s32[2,128]{1,0:T(2,128)S(1)} %pad_add_fusion.refs_0_), channel_id=1, source_target_pairs={{0,32},{16,48},{32,0},{48,16},{1,33},{17,49},{33,1},{49,17},{2,34}... | collective-permute-start | bytes 3080 | tf_op jit(solution)/shard_map/ppermute | solution.py:232
  23.2 2.8 %collective-permute-start.1 = (s32[2,128]{1,0:T(2,128)S(1)}, s32[2,128]{1,0:T(2,128)S(1)}, u32[]{:S(2)}, u32[]{:S(2)}) collective-permute-start(s32[2,128]{1,0:T(2,128)S(1)} %pad_add_fusion.refs_0_), channel_id=1, source_target_pairs={{0,16},{16,32},{32,48},{48,0},{1,17},{17,33},{33,49},{49,1},{2,18}... | collective-permute-start | bytes 3080 | tf_op jit(solution)/shard_map/ppermute | solution.py:232
  26.1 1.4 %collective-permute-done.2.refs_2_ = s32[2,128]{1,0:T(2,128)S(1)} collective-permute-done((s32[2,128]{1,0:T(2,128)S(1)}, s32[2,128]{1,0:T(2,128)S(1)}, u32[]{:S(2)}, u32[]{:S(2)}) %collective-permute-start.2) | collective-permute-done | bytes 1056 | tf_op jit(solution)/shard_map/ppermute | solution.py:232
  27.5 2.4 %collective-permute-done.1.refs_1_ = s32[2,128]{1,0:T(2,128)S(1)} collective-permute-done((s32[2,128]{1,0:T(2,128)S(1)}, s32[2,128]{1,0:T(2,128)S(1)}, u32[]{:S(2)}, u32[]{:S(2)}) %collective-permute-start.1) | collective-permute-done | bytes 1056 | tf_op jit(solution)/shard_map/ppermute | solution.py:232
  29.9 2.9 %shard_map.121 = bf16[8,16,3328]{2,1,0:T(8,128)(2,1)} custom-call(s32[2]{0:T(128)S(1)} %pad_add_fusion.1.at_ref, s32[2,128]{1,0:T(2,128)S(1)} %pad_add_fusion.refs_0_, s32[2,128]{1,0:T(2,128)S(1)} %collective-permute-done.1.refs_1_, s32[2,128]{1,0:T(2,128)S(1)} %collective-permute-done.2.refs_2_, s32[2,128]{1,0:T(2,128)S(1)} %collective-permute-done.3.refs_3_, ...), custom_call_target="tpu_custom_call" | custom-call | tf_op jit(solution)/shard_map/pallas_call | solution.py:235
  32.8 3.5 %all-to-all-start.1 = ((bf16[8,16,3328]{2,1,0:T(8,128)(2,1)}), bf16[8,16,3328]{2,1,0:T(8,128)(2,1)S(1)}, u32[]{:S(2)}, u32[]{:S(2)}) async-start(bf16[8,16,3328]{2,1,0:T(8,128)(2,1)} %shard_map.121), calls=%async_computation.1 | async-start | bytes 1703936 | tf_op jit(solution)/shard_map/all_to_all | solution.py:241
  37.1 1.0 %copy-done.1 = bf16[1,256,1024]{2,1,0:T(8,128)(2,1)S(1)} copy-done((bf16[1,256,1024]{2,1,0:T(8,128)(2,1)S(1)}, bf16[1,256,1024]{2,1,0:T(8,128)(2,1)}, u32[]{:S(2)}) %copy-start.1) | copy-done | bytes 524312
  38.1 0.9 %copy-done.3 = bf16[128,1024]{1,0:T(8,128)(2,1)S(1)} copy-done((bf16[128,1024]{1,0:T(8,128)(2,1)S(1)}, bf16[128,1024]{1,0:T(8,128)(2,1)}, u32[]{:S(2)}) %copy-start.3) | copy-done | bytes 262168
  39.0 2.5 %shard_map.122 = (bf16[256,512]{1,0:T(8,128)(2,1)S(1)}, bf16[256,512]{1,0:T(8,128)(2,1)}, bf16[256,512]{1,0:T(8,128)(2,1)S(1)}, f32[1,512]{1,0:T(1,128)S(1)}, bf16[256,3072]{1,0:T(8,128)(2,1)S(1)}) custom-call(s32[1]{0:T(128)} %bitcast.2.core_ref, bf16[256,1024]{1,0:T(8,128)(2,1)S(1)} %bitcast.25, bf16[128,1024]{1,0:T(8,128)(2,1)S(1)} %copy-done.2, ...), custom_call_target="tpu_custom_call" | custom-call | tf_op jit(solution)/shard_map/pallas_call | solution.py:212
  41.5 0.7 copy-done.4
  42.2 0.7 copy-done.6
  42.9 2.4 %collective-permute-start.5 = (bf16[256,512]{1,0:T(8,128)(2,1)}, bf16[256,512]{1,0:T(8,128)(2,1)S(1)}, u32[]{:S(2)}, u32[]{:S(2)}) collective-permute-start(bf16[256,512]{1,0:T(8,128)(2,1)} %get-tuple-element.13), channel_id=1, source_target_pairs={{0,1},{1,0},{2,3},{3,2},{4,5},{5,4},{6,7},{7,6},{8,9},{9,8},{10,11... | collective-permute-start | bytes 786440 | tf_op jit(solution)/shard_map/ppermute | solution.py:224
  45.3 4.8 %all-to-all-done.1 = bf16[8,16,3328]{2,1,0:T(8,128)(2,1)S(1)} async-done(((bf16[8,16,3328]{2,1,0:T(8,128)(2,1)}), bf16[8,16,3328]{2,1,0:T(8,128)(2,1)S(1)}, u32[]{:S(2)}, u32[]{:S(2)}) %all-to-all-start.1) | async-done | bytes 852000 | tf_op jit(solution)/shard_map/all_to_all | solution.py:241
  50.1 0.9 shard_map.123.mine_ref
  51.0 1.9 %collective-permute-start.4 = (bf16[256,256]{1,0:T(8,128)(2,1)S(1)}, bf16[256,256]{1,0:T(8,128)(2,1)S(1)}, u32[]{:S(2)}, u32[]{:S(2)}) collective-permute-start(bf16[256,256]{1,0:T(8,128)(2,1)S(1)} %shard_map.123.mine_ref), channel_id=1, source_target_pairs={{0,1},{1,0},{2,3},{3,2},{4,5},{5,4},{6,7},{7,6},{8,9},{9,8},{10,11... | collective-permute-start | bytes 393224 | tf_op jit(solution)/shard_map/ppermute | solution.py:250
  53.0 1.3 %collective-permute-done.4.theirs_ref = bf16[256,256]{1,0:T(8,128)(2,1)S(1)} collective-permute-done((bf16[256,256]{1,0:T(8,128)(2,1)S(1)}, bf16[256,256]{1,0:T(8,128)(2,1)S(1)}, u32[]{:S(2)}, u32[]{:S(2)}) %collective-permute-start.4) | collective-permute-done | bytes 131104 | tf_op jit(solution)/shard_map/ppermute | solution.py:250
  54.3 0.9 shard_map.124
  55.2 21.6 %all_to_all.20.got_ref = bf16[32,40,128]{2,1,0:T(8,128)(2,1)S(1)} all-to-all(bf16[32,40,128]{2,1,0:T(8,128)(2,1)S(1)} %shard_map.124), channel_id=1, replica_groups=mesh['dp'=8,'x'=4,'z'=8,'core'=2] {'x','z'}, dimensions={0} | all-to-all | bytes 655360 | tf_op jit(solution)/shard_map/all_to_all | solution.py:258
  76.9 15.5 %all_to_all.21.got_ref = bf16[8,40,128]{2,1,0:T(8,128)(2,1)S(1)} all-to-all(bf16[8,40,128]{2,1,0:T(8,128)(2,1)S(1)} %shard_map.125), channel_id=1, replica_groups=mesh['dp'=8,'x'=4,'z'=8,'core'=2] {'dp'}, dimensions={0} | all-to-all | bytes 163840 | tf_op jit(solution)/shard_map/all_to_all | solution.py:265
  (32 shorter events, 0.9 us)
Async XLA Ops:
  0.6 12.0 %copy-start.9 = (s32[1,24]{1,0:T(1,128)S(1)}, s32[1,24]{1,0:T(1,128)}, u32[]{:S(2)}) copy-start(s32[1,24]{1,0:T(1,128)} %param.14) | copy-start | bytes 292
  0.6 12.0 %copy-start.10 = (s32[1,24,1]{1,2,0:T(1,128)S(1)}, s32[1,24,1]{1,2,0:T(1,128)}, u32[]{:S(2)}) copy-start(s32[1,24,1]{1,2,0:T(1,128)} %param.13) | copy-start | bytes 292
  2.6 27.3 %all-to-all-start = ((bf16[8,2,16384]{2,1,0:T(2,128)(2,1)}), bf16[8,2,16384]{2,1,0:T(2,128)(2,1)S(1)}, u32[]{:S(2)}, u32[]{:S(2)}) async-start(bf16[8,2,16384]{2,1,0:T(2,128)(2,1)} %broadcast_in_dim.22), calls=%async_computation | async-start | bytes 1048576 | tf_op jit(solution)/shard_map/all_to_all | solution.py:201
  12.5 24.5 %copy-start.11 = (s32[1,24]{1,0:T(1,128)S(1)}, s32[1,24]{1,0:T(1,128)}, u32[]{:S(2)}) copy-start(s32[1,24]{1,0:T(1,128)} %param.12) | copy-start | bytes 292
  12.5 24.5 %copy-start = (bf16[1,24,128,128]{3,2,1,0:T(8,128)(2,1)S(1)}, bf16[1,24,128,128]{3,2,1,0:T(8,128)(2,1)}, u32[]{:S(2)}) copy-start(bf16[1,24,128,128]{3,2,1,0:T(8,128)(2,1)} %param.11) | copy-start | bytes 2359300
  12.5 24.5 %copy-start.2 = (bf16[128,1024]{1,0:T(8,128)(2,1)S(1)}, bf16[128,1024]{1,0:T(8,128)(2,1)}, u32[]{:S(2)}) copy-start(bf16[128,1024]{1,0:T(8,128)(2,1)} %w_self_ref.1) | copy-start | bytes 786436
  12.6 24.5 %copy-start.8 = (f32[1024]{0:T(1024)S(1)}, f32[1024]{0:T(1024)}, u32[]{:S(2)}) copy-start(f32[1024]{0:T(1024)} %param.19) | copy-start | bytes 12292
  12.7 3.1 %collective-permute-start = (s32[1,128]{1,0:T(1,128)S(1)}, s32[1,128]{1,0:T(1,128)S(1)}, u32[]{:S(2)}, u32[]{:S(2)}) collective-permute-start(s32[1,128]{1,0:T(1,128)S(1)} %pad_bitcast_fusion), channel_id=1, source_target_pairs={{0,1},{1,0},{2,3},{3,2},{4,5},{5,4},{6,7},{7,6},{8,9},{9,8},{10,11... | collective-permute-start | bytes 1544 | tf_op jit(solution)/shard_map/ppermute | solution.py:229
  15.8 10.3 %collective-permute-start.3 = (s32[2,128]{1,0:T(2,128)S(1)}, s32[2,128]{1,0:T(2,128)S(1)}, u32[]{:S(2)}, u32[]{:S(2)}) collective-permute-start(s32[2,128]{1,0:T(2,128)S(1)} %pad_add_fusion.refs_0_), channel_id=1, source_target_pairs={{0,48},{16,0},{32,16},{48,32},{1,49},{17,1},{33,17},{49,33},{2,50}... | collective-permute-start | bytes 3080 | tf_op jit(solution)/shard_map/ppermute | solution.py:232
  20.5 7.0 %collective-permute-start.2 = (s32[2,128]{1,0:T(2,128)S(1)}, s32[2,128]{1,0:T(2,128)S(1)}, u32[]{:S(2)}, u32[]{:S(2)}) collective-permute-start(s32[2,128]{1,0:T(2,128)S(1)} %pad_add_fusion.refs_0_), channel_id=1, source_target_pairs={{0,32},{16,48},{32,0},{48,16},{1,33},{17,49},{33,1},{49,17},{2,34}... | collective-permute-start | bytes 3080 | tf_op jit(solution)/shard_map/ppermute | solution.py:232
  23.2 6.7 %collective-permute-start.1 = (s32[2,128]{1,0:T(2,128)S(1)}, s32[2,128]{1,0:T(2,128)S(1)}, u32[]{:S(2)}, u32[]{:S(2)}) collective-permute-start(s32[2,128]{1,0:T(2,128)S(1)} %pad_add_fusion.refs_0_), channel_id=1, source_target_pairs={{0,16},{16,32},{32,48},{48,0},{1,17},{17,33},{33,49},{49,1},{2,18}... | collective-permute-start | bytes 3080 | tf_op jit(solution)/shard_map/ppermute | solution.py:232
  32.8 17.3 %all-to-all-start.1 = ((bf16[8,16,3328]{2,1,0:T(8,128)(2,1)}), bf16[8,16,3328]{2,1,0:T(8,128)(2,1)S(1)}, u32[]{:S(2)}, u32[]{:S(2)}) async-start(bf16[8,16,3328]{2,1,0:T(8,128)(2,1)} %shard_map.121), calls=%async_computation.1 | async-start | bytes 1703936 | tf_op jit(solution)/shard_map/all_to_all | solution.py:241
  37.0 1.0 %copy-start.1 = (bf16[1,256,1024]{2,1,0:T(8,128)(2,1)S(1)}, bf16[1,256,1024]{2,1,0:T(8,128)(2,1)}, u32[]{:S(2)}) copy-start(bf16[1,256,1024]{2,1,0:T(8,128)(2,1)} %param.16) | copy-start | bytes 1572868
  38.1 0.9 %copy-start.3 = (bf16[128,1024]{1,0:T(8,128)(2,1)S(1)}, bf16[128,1024]{1,0:T(8,128)(2,1)}, u32[]{:S(2)}) copy-start(bf16[128,1024]{1,0:T(8,128)(2,1)} %w_neigh_ref.1) | copy-start | bytes 786436
  41.5 0.7 copy-start.4
  42.2 0.7 copy-start.6
  42.9 11.4 %copy-start.5 = (bf16[256,512]{1,0:T(8,128)(2,1)S(1)}, bf16[256,512]{1,0:T(8,128)(2,1)}, u32[]{:S(2)}) copy-start(bf16[256,512]{1,0:T(8,128)(2,1)} %copy-done.4) | copy-start | bytes 786436
  42.9 11.4 %copy-start.7 = (bf16[256,512]{1,0:T(8,128)(2,1)S(1)}, bf16[256,512]{1,0:T(8,128)(2,1)}, u32[]{:S(2)}) copy-start(bf16[256,512]{1,0:T(8,128)(2,1)} %copy-done.6) | copy-start | bytes 786436
  42.9 10.1 %collective-permute-start.5 = (bf16[256,512]{1,0:T(8,128)(2,1)}, bf16[256,512]{1,0:T(8,128)(2,1)S(1)}, u32[]{:S(2)}, u32[]{:S(2)}) collective-permute-start(bf16[256,512]{1,0:T(8,128)(2,1)} %get-tuple-element.13), channel_id=1, source_target_pairs={{0,1},{1,0},{2,3},{3,2},{4,5},{5,4},{6,7},{7,6},{8,9},{9,8},{10,11... | collective-permute-start | bytes 786440 | tf_op jit(solution)/shard_map/ppermute | solution.py:224
  51.0 3.2 %collective-permute-start.4 = (bf16[256,256]{1,0:T(8,128)(2,1)S(1)}, bf16[256,256]{1,0:T(8,128)(2,1)S(1)}, u32[]{:S(2)}, u32[]{:S(2)}) collective-permute-start(bf16[256,256]{1,0:T(8,128)(2,1)S(1)} %shard_map.123.mine_ref), channel_id=1, source_target_pairs={{0,1},{1,0},{2,3},{3,2},{4,5},{5,4},{6,7},{7,6},{8,9},{9,8},{10,11... | collective-permute-start | bytes 393224 | tf_op jit(solution)/shard_map/ppermute | solution.py:250

commit v4 on v3

--- a/solution.py
+++ b/solution.py
@@ -28,24 +28,23 @@
     )
 
 
-def pack_kernel(at_ref, *refs):
-    *lists_refs, whole_ref, sent_ref = refs
+def copies_kernel(own_ref, out_ref):
+    own = own_ref[...]
+    for z in range(out_ref.shape[0]):
+        out_ref[z] = own
+
+
+def pack_kernel(at_ref, near_ref, far_ref, whole_ref, sent_ref, table_ref):
     depth, width = whole_ref.shape[0], whole_ref.shape[1]
-    slots = sent_ref.shape[2] // LANES
-    reach = len(lists_refs)
-    for step, lists_ref in enumerate(lists_refs):
-        x = lax.rem(at_ref[0] + reach - step, reach)
-
-        def peer(side, carry, x=x, lists_ref=lists_ref):
-            p = x * CORES + lax.rem(at_ref[1] + side, CORES)
-            for s in range(slots):
-                at = pl.ds(pl.multiple_of(lists_ref[side, s] * LANES, LANES), LANES)
-                here = slice(s * LANES, (s + 1) * LANES)
-                for z in range(depth):
-                    sent_ref[p, z * width : (z + 1) * width, here] = whole_ref[z, :, at]
-            return carry
-
-        lax.fori_loop(0, CORES, peer, 0)
+    for z in range(depth):
+        table_ref[z * width : (z + 1) * width, :] = whole_ref[z]
+    half = near_ref.shape[0]
+    for row in range(2 * half):
+        lists_ref = near_ref if row < half else far_ref
+        p = jnp.bitwise_xor(at_ref[0], row)
+        for s in range(sent_ref.shape[2] // LANES):
+            at = pl.ds(pl.multiple_of(lists_ref[row % half, s] * LANES, LANES), LANES)
+            sent_ref[p, :, s * LANES : (s + 1) * LANES] = table_ref[:, at]
 
 
 def gather_kernel(width, got_ref, masked_ref, inputs_ref):
@@ -198,13 +197,13 @@
     core_at, chip_at = core[None], chip[None]
     swap = [(i, CORES - 1 - i) for i in range(CORES)]
 
-    whole = lax.all_to_all(
-        jnp.broadcast_to(own[None], (DEPTH, width, node_count)),
-        "z",
-        split_axis=0,
-        concat_axis=0,
-        tiled=True,
-    )
+    copies = call(
+        copies_kernel,
+        jax.ShapeDtypeStruct((DEPTH, width, node_count), BF16),
+        [VMEM],
+        2,
+    )(own)
+    whole = lax.all_to_all(copies, "z", split_axis=0, concat_axis=0, tiled=True)
     half = hidden // CORES
     part = half // chips
     live = jnp.arange(slots, dtype=jnp.int32) < tile_counts[0, 0]
@@ -225,19 +224,22 @@
     named = tile_owners[0, :, 0] * row_blocks + tile_blocks[0]
     held = (chip * CORES + core) * row_blocks + jnp.arange(row_blocks, dtype=jnp.int32)
     names = jnp.pad(jnp.concatenate([named, held]), (0, LANES - slots - row_blocks))
-    names = names[None]
-    pair = jnp.concatenate([names, lax.ppermute(names, "core", swap)], axis=0)
+    near = names[None]
+    far = lax.ppermute(near, "core", swap)
     reach = lax.axis_size("x")
-    lists = [pair] + [
-        lax.ppermute(pair, "x", [(i, (i + step) % reach) for i in range(reach)])
-        for step in range(1, reach)
-    ]
+    step = 1
+    while step < reach:
+        near = jnp.concatenate([near, far], axis=0)
+        far = lax.ppermute(near, "x", [(i, i ^ step) for i in range(reach)])
+        step *= 2
+    columns = DEPTH * width
     sent = call(
         pack_kernel,
-        jax.ShapeDtypeStruct((peers, DEPTH * width, (slots + row_blocks) * side), BF16),
-        [SMEM] * (1 + reach) + [VMEM],
+        jax.ShapeDtypeStruct((peers, columns, (slots + row_blocks) * side), BF16),
+        [SMEM, SMEM, SMEM, VMEM],
         8,
-    )(jnp.stack([lax.axis_index("x"), core]), *lists, whole)
+        [pltpu.VMEM((columns, node_count), BF16)],
+    )((lax.axis_index("x") * CORES + core)[None], near, far, whole)
     got = lax.all_to_all(
         sent, ("x", "core"), split_axis=0, concat_axis=0, tiled=True
     ).reshape(feats, (slots + row_blocks) * side)

time: 93.6 us -> 91.7 us (0.980)
  local copies, waits for them, and re-layouts: 5.34 us -> 4.26 us
  starting transfers between devices: 30.1 us -> 29.1 us
    broadcast_in_dim x2 -> x1, local copies, waits for them, and re-layouts: 1.93 us -> 0.01 us  [local(): near = names[None]]
    ppermute x4 -> x3, starting transfers between devices: 12.2 us -> 10.4 us  [the longest x2 8.31 us: local(): far = lax.ppermute(near, 'x', [(i, i ^ step) for i in range(reach)])]
    unnamed x24 -> x26, local copies, waits for them, and re-layouts: 3.41 us -> 4.26 us
    ppermute x4 -> x3, waiting for transfers between devices: 4.88 us -> 5.18 us  [the longest x2 4.09 us: local(): far = lax.ppermute(near, 'x', [(i, i ^ step) for i in range(reach)])]
    pallas_call x1 -> x2, Pallas kernels: 2.88 us -> 2.87 us  [the longest x1 2.03 us: local(): call(pack_kernel, jax.ShapeDtypeStruct((peers, columns, (slots + row_bloc...]
  transfers between devices with their start and end apart: 8 -> 7, of which waited for: 5 -> 6; matrix products, arithmetic and copies ran while one was open for 0% -> 0% of each run, Pallas kernels for 4% -> 4%
where the time goes in v4:
time: 91.7 us; the launch traced here: 91.1 us
  blocking collectives  36.8 us (40%)
  starting transfers between devices  29.1 us (32%)
  waiting for transfers between devices  11.5 us (13%)
  Pallas kernels  7.81 us (9%)
  local copies, waits for them, and re-layouts  4.26 us (5%)
  between operations  1.5 us (2%)
    all_to_all x1, blocking collectives, local(): lax.all_to_all(sums, ('x', 'z'), split_axis=0, concat_axis=0, tiled=True)  21.4 us
    all_to_all x1, blocking collectives, local(): lax.all_to_all(spread, 'dp', split_axis=0, concat_axis=0, tiled=True)  15.4 us
    all_to_all x1, starting transfers between devices, local(): whole = lax.all_to_all(copies, 'z', split_axis=0, concat_axis=0, tiled=True)  9.96 us
    ppermute x2, starting transfers between devices, local(): far = lax.ppermute(near, 'x', [(i, i ^ step) for i in range(reach)])  8.31 us
    all_to_all x1, waiting for transfers between devices, local(): lax.all_to_all(sent, ('x', 'core'), split_axis=0, concat_axis=0, tiled=True)  4.77 us
    all_to_all x1, starting transfers between devices, local(): lax.all_to_all(sent, ('x', 'core'), split_axis=0, concat_axis=0, tiled=True)  4.3 us
    unnamed x26, local copies, waits for them, and re-layouts  4.26 us
    ppermute x2, waiting for transfers between devices, local(): far = lax.ppermute(near, 'x', [(i, i ^ step) for i in range(reach)])  4.09 us
  transfers between devices with their start and end apart: 7, of which 6 were waited for; matrix products, arithmetic and copies ran while one was open for 0% of the time, Pallas kernels for 4%

profile of v4, /device:TPU:64, one launch (start us, length us, event | category | flops | bytes accessed | tf_op | source)
XLA Modules:
  0.0 91.1 jit_solution(18146246977331983309)
XLA Ops:
  0.7 0.8 copy-done.8
  1.5 0.8 shard_map.121
  2.3 10.0 %all-to-all-start = ((bf16[8,2,16384]{2,1,0:T(2,128)(2,1)}), bf16[8,2,16384]{2,1,0:T(2,128)(2,1)S(1)}, u32[]{:S(2)}, u32[]{:S(2)}) async-start(bf16[8,2,16384]{2,1,0:T(2,128)(2,1)} %shard_map.121), calls=%async_computation | async-start | bytes 1048576 | tf_op jit(solution)/shard_map/all_to_all | solution.py:206
  12.5 2.0 %collective-permute-start = (s32[1,128]{1,0:T(1,128)S(1)}, s32[1,128]{1,0:T(1,128)S(1)}, u32[]{:S(2)}, u32[]{:S(2)}) collective-permute-start(s32[1,128]{1,0:T(1,128)S(1)} %pad_bitcast_fusion), channel_id=1, source_target_pairs={{0,1},{1,0},{2,3},{3,2},{4,5},{5,4},{6,7},{7,6},{8,9},{9,8},{10,11... | collective-permute-start | bytes 1544 | tf_op jit(solution)/shard_map/ppermute | solution.py:228
  14.5 1.1 %collective-permute-done = s32[1,128]{1,0:T(1,128)S(1)} collective-permute-done((s32[1,128]{1,0:T(1,128)S(1)}, s32[1,128]{1,0:T(1,128)S(1)}, u32[]{:S(2)}, u32[]{:S(2)}) %collective-permute-start) | collective-permute-done | bytes 544 | tf_op jit(solution)/shard_map/ppermute | solution.py:228
  15.6 3.4 %collective-permute-start.1 = (s32[2,128]{1,0:T(2,128)S(1)}, s32[2,128]{1,0:T(2,128)S(1)}, u32[]{:S(2)}, u32[]{:S(2)}) collective-permute-start(s32[2,128]{1,0:T(2,128)S(1)} %pad_add_fusion.1), channel_id=1, source_target_pairs={{0,16},{16,0},{32,48},{48,32},{1,17},{17,1},{33,49},{49,33},{2,18}... | collective-permute-start | bytes 3080 | tf_op jit(solution)/shard_map/ppermute | solution.py:233
  19.0 2.1 %collective-permute-done.1 = s32[2,128]{1,0:T(2,128)S(1)} collective-permute-done((s32[2,128]{1,0:T(2,128)S(1)}, s32[2,128]{1,0:T(2,128)S(1)}, u32[]{:S(2)}, u32[]{:S(2)}) %collective-permute-start.1) | collective-permute-done | bytes 1056 | tf_op jit(solution)/shard_map/ppermute | solution.py:233
  21.1 4.9 %collective-permute-start.2 = (s32[4,128]{1,0:T(4,128)S(1)}, s32[4,128]{1,0:T(4,128)S(1)}, u32[]{:S(2)}, u32[]{:S(2)}) collective-permute-start(s32[4,128]{1,0:T(4,128)S(1)} %pad_add_fusion.near_ref), channel_id=1, source_target_pairs={{0,32},{16,48},{32,0},{48,16},{1,33},{17,49},{33,1},{49,17},{2,34}... | collective-permute-start | bytes 6152 | tf_op jit(solution)/shard_map/ppermute | solution.py:233
  26.0 2.0 %collective-permute-done.2.far_ref = s32[4,128]{1,0:T(4,128)S(1)} collective-permute-done((s32[4,128]{1,0:T(4,128)S(1)}, s32[4,128]{1,0:T(4,128)S(1)}, u32[]{:S(2)}, u32[]{:S(2)}) %collective-permute-start.2) | collective-permute-done | bytes 2080 | tf_op jit(solution)/shard_map/ppermute | solution.py:233
  28.3 2.0 %shard_map.122 = bf16[8,16,3328]{2,1,0:T(8,128)(2,1)} custom-call(s32[1]{0:T(128)} %bitcast.1.at_ref, s32[4,128]{1,0:T(4,128)S(1)} %pad_add_fusion.near_ref, s32[4,128]{1,0:T(4,128)S(1)} %collective-permute-done.2.far_ref, bf16[8,2,16384]{2,1,0:T(2,128)(2,1)S(1)} %all-to-all-done.whole_ref), custom_call_target="tpu_custom_call" | custom-call | tf_op jit(solution)/shard_map/pallas_call | solution.py:236
  30.4 4.3 %all-to-all-start.1 = ((bf16[8,16,3328]{2,1,0:T(8,128)(2,1)}), bf16[8,16,3328]{2,1,0:T(8,128)(2,1)S(1)}, u32[]{:S(2)}, u32[]{:S(2)}) async-start(bf16[8,16,3328]{2,1,0:T(8,128)(2,1)} %shard_map.122), calls=%async_computation.1 | async-start | bytes 1703936 | tf_op jit(solution)/shard_map/all_to_all | solution.py:243
  35.4 1.0 %copy-done.1 = bf16[1,256,1024]{2,1,0:T(8,128)(2,1)S(1)} copy-done((bf16[1,256,1024]{2,1,0:T(8,128)(2,1)S(1)}, bf16[1,256,1024]{2,1,0:T(8,128)(2,1)}, u32[]{:S(2)}) %copy-start.1) | copy-done | bytes 524312
  36.4 0.9 %copy-done.3 = bf16[128,1024]{1,0:T(8,128)(2,1)S(1)} copy-done((bf16[128,1024]{1,0:T(8,128)(2,1)S(1)}, bf16[128,1024]{1,0:T(8,128)(2,1)}, u32[]{:S(2)}) %copy-start.3) | copy-done | bytes 262168
  37.4 2.5 %shard_map.123 = (bf16[256,512]{1,0:T(8,128)(2,1)S(1)}, bf16[256,512]{1,0:T(8,128)(2,1)}, bf16[256,512]{1,0:T(8,128)(2,1)S(1)}, f32[1,512]{1,0:T(1,128)S(1)}, bf16[256,3072]{1,0:T(8,128)(2,1)S(1)}) custom-call(s32[1]{0:T(128)} %bitcast.8.core_ref, bf16[256,1024]{1,0:T(8,128)(2,1)S(1)} %bitcast.25, bf16[128,1024]{1,0:T(8,128)(2,1)S(1)} %copy-done.2, ...), custom_call_target="tpu_custom_call" | custom-call | tf_op jit(solution)/shard_map/pallas_call | solution.py:211
  39.8 0.7 copy-done.4
  40.5 0.7 copy-done.6
  41.2 2.5 %collective-permute-start.4 = (bf16[256,512]{1,0:T(8,128)(2,1)}, bf16[256,512]{1,0:T(8,128)(2,1)S(1)}, u32[]{:S(2)}, u32[]{:S(2)}) collective-permute-start(bf16[256,512]{1,0:T(8,128)(2,1)} %get-tuple-element.13), channel_id=1, source_target_pairs={{0,1},{1,0},{2,3},{3,2},{4,5},{5,4},{6,7},{7,6},{8,9},{9,8},{10,11... | collective-permute-start | bytes 786440 | tf_op jit(solution)/shard_map/ppermute | solution.py:223
  43.8 4.8 %all-to-all-done.1 = bf16[8,16,3328]{2,1,0:T(8,128)(2,1)S(1)} async-done(((bf16[8,16,3328]{2,1,0:T(8,128)(2,1)}), bf16[8,16,3328]{2,1,0:T(8,128)(2,1)S(1)}, u32[]{:S(2)}, u32[]{:S(2)}) %all-to-all-start.1) | async-done | bytes 852000 | tf_op jit(solution)/shard_map/all_to_all | solution.py:243
  48.5 0.9 shard_map.124.mine_ref
  49.4 1.9 %collective-permute-start.3 = (bf16[256,256]{1,0:T(8,128)(2,1)S(1)}, bf16[256,256]{1,0:T(8,128)(2,1)S(1)}, u32[]{:S(2)}, u32[]{:S(2)}) collective-permute-start(bf16[256,256]{1,0:T(8,128)(2,1)S(1)} %shard_map.124.mine_ref), channel_id=1, source_target_pairs={{0,1},{1,0},{2,3},{3,2},{4,5},{5,4},{6,7},{7,6},{8,9},{9,8},{10,11... | collective-permute-start | bytes 393224 | tf_op jit(solution)/shard_map/ppermute | solution.py:252
  51.4 1.3 %collective-permute-done.3.theirs_ref = bf16[256,256]{1,0:T(8,128)(2,1)S(1)} collective-permute-done((bf16[256,256]{1,0:T(8,128)(2,1)S(1)}, bf16[256,256]{1,0:T(8,128)(2,1)S(1)}, u32[]{:S(2)}, u32[]{:S(2)}) %collective-permute-start.3) | collective-permute-done | bytes 131104 | tf_op jit(solution)/shard_map/ppermute | solution.py:252
  52.7 0.9 shard_map.125
  53.6 21.4 %all_to_all.20.got_ref = bf16[32,40,128]{2,1,0:T(8,128)(2,1)S(1)} all-to-all(bf16[32,40,128]{2,1,0:T(8,128)(2,1)S(1)} %shard_map.125), channel_id=1, replica_groups=mesh['dp'=8,'x'=4,'z'=8,'core'=2] {'x','z'}, dimensions={0} | all-to-all | bytes 655360 | tf_op jit(solution)/shard_map/all_to_all | solution.py:260
  75.0 15.4 %all_to_all.21.got_ref = bf16[8,40,128]{2,1,0:T(8,128)(2,1)S(1)} all-to-all(bf16[8,40,128]{2,1,0:T(8,128)(2,1)S(1)} %shard_map.126), channel_id=1, replica_groups=mesh['dp'=8,'x'=4,'z'=8,'core'=2] {'dp'}, dimensions={0} | all-to-all | bytes 163840 | tf_op jit(solution)/shard_map/all_to_all | solution.py:267
  (32 shorter events, 1.2 us)
Async XLA Ops:
  0.6 11.7 %copy-start.10 = (s32[1,24]{1,0:T(1,128)S(1)}, s32[1,24]{1,0:T(1,128)}, u32[]{:S(2)}) copy-start(s32[1,24]{1,0:T(1,128)} %param.14) | copy-start | bytes 292
  0.6 11.7 %copy-start.11 = (s32[1,24,1]{1,2,0:T(1,128)S(1)}, s32[1,24,1]{1,2,0:T(1,128)}, u32[]{:S(2)}) copy-start(s32[1,24,1]{1,2,0:T(1,128)} %param.13) | copy-start | bytes 292
  0.7 0.9 copy-start.8
  2.3 26.0 %all-to-all-start = ((bf16[8,2,16384]{2,1,0:T(2,128)(2,1)}), bf16[8,2,16384]{2,1,0:T(2,128)(2,1)S(1)}, u32[]{:S(2)}, u32[]{:S(2)}) async-start(bf16[8,2,16384]{2,1,0:T(2,128)(2,1)} %shard_map.121), calls=%async_computation | async-start | bytes 1048576 | tf_op jit(solution)/shard_map/all_to_all | solution.py:206
  12.3 23.0 %copy-start.12 = (s32[1,24]{1,0:T(1,128)S(1)}, s32[1,24]{1,0:T(1,128)}, u32[]{:S(2)}) copy-start(s32[1,24]{1,0:T(1,128)} %param.12) | copy-start | bytes 292
  12.3 23.0 %copy-start = (bf16[1,24,128,128]{3,2,1,0:T(8,128)(2,1)S(1)}, bf16[1,24,128,128]{3,2,1,0:T(8,128)(2,1)}, u32[]{:S(2)}) copy-start(bf16[1,24,128,128]{3,2,1,0:T(8,128)(2,1)} %param.11) | copy-start | bytes 2359300
  12.3 23.0 %copy-start.2 = (bf16[128,1024]{1,0:T(8,128)(2,1)S(1)}, bf16[128,1024]{1,0:T(8,128)(2,1)}, u32[]{:S(2)}) copy-start(bf16[128,1024]{1,0:T(8,128)(2,1)} %w_self_ref.1) | copy-start | bytes 786436
  12.3 23.1 %copy-start.9 = (f32[1024]{0:T(1024)S(1)}, f32[1024]{0:T(1024)}, u32[]{:S(2)}) copy-start(f32[1024]{0:T(1024)} %param.19) | copy-start | bytes 12292
  12.5 3.1 %collective-permute-start = (s32[1,128]{1,0:T(1,128)S(1)}, s32[1,128]{1,0:T(1,128)S(1)}, u32[]{:S(2)}, u32[]{:S(2)}) collective-permute-start(s32[1,128]{1,0:T(1,128)S(1)} %pad_bitcast_fusion), channel_id=1, source_target_pairs={{0,1},{1,0},{2,3},{3,2},{4,5},{5,4},{6,7},{7,6},{8,9},{9,8},{10,11... | collective-permute-start | bytes 1544 | tf_op jit(solution)/shard_map/ppermute | solution.py:228
  15.6 5.5 %collective-permute-start.1 = (s32[2,128]{1,0:T(2,128)S(1)}, s32[2,128]{1,0:T(2,128)S(1)}, u32[]{:S(2)}, u32[]{:S(2)}) collective-permute-start(s32[2,128]{1,0:T(2,128)S(1)} %pad_add_fusion.1), channel_id=1, source_target_pairs={{0,16},{16,0},{32,48},{48,32},{1,17},{17,1},{33,49},{49,33},{2,18}... | collective-permute-start | bytes 3080 | tf_op jit(solution)/shard_map/ppermute | solution.py:233
  21.1 7.0 %collective-permute-start.2 = (s32[4,128]{1,0:T(4,128)S(1)}, s32[4,128]{1,0:T(4,128)S(1)}, u32[]{:S(2)}, u32[]{:S(2)}) collective-permute-start(s32[4,128]{1,0:T(4,128)S(1)} %pad_add_fusion.near_ref), channel_id=1, source_target_pairs={{0,32},{16,48},{32,0},{48,16},{1,33},{17,49},{33,1},{49,17},{2,34}... | collective-permute-start | bytes 6152 | tf_op jit(solution)/shard_map/ppermute | solution.py:233
  30.4 18.2 %all-to-all-start.1 = ((bf16[8,16,3328]{2,1,0:T(8,128)(2,1)}), bf16[8,16,3328]{2,1,0:T(8,128)(2,1)S(1)}, u32[]{:S(2)}, u32[]{:S(2)}) async-start(bf16[8,16,3328]{2,1,0:T(8,128)(2,1)} %shard_map.122), calls=%async_computation.1 | async-start | bytes 1703936 | tf_op jit(solution)/shard_map/all_to_all | solution.py:243
  35.4 1.0 %copy-start.1 = (bf16[1,256,1024]{2,1,0:T(8,128)(2,1)S(1)}, bf16[1,256,1024]{2,1,0:T(8,128)(2,1)}, u32[]{:S(2)}) copy-start(bf16[1,256,1024]{2,1,0:T(8,128)(2,1)} %param.16) | copy-start | bytes 1572868
  36.4 0.9 %copy-start.3 = (bf16[128,1024]{1,0:T(8,128)(2,1)S(1)}, bf16[128,1024]{1,0:T(8,128)(2,1)}, u32[]{:S(2)}) copy-start(bf16[128,1024]{1,0:T(8,128)(2,1)} %w_neigh_ref.1) | copy-start | bytes 786436
  39.8 0.7 copy-start.4
  40.5 0.7 copy-start.6
  41.2 11.5 %copy-start.5 = (bf16[256,512]{1,0:T(8,128)(2,1)S(1)}, bf16[256,512]{1,0:T(8,128)(2,1)}, u32[]{:S(2)}) copy-start(bf16[256,512]{1,0:T(8,128)(2,1)} %copy-done.4) | copy-start | bytes 786436
  41.2 11.5 %copy-start.7 = (bf16[256,512]{1,0:T(8,128)(2,1)S(1)}, bf16[256,512]{1,0:T(8,128)(2,1)}, u32[]{:S(2)}) copy-start(bf16[256,512]{1,0:T(8,128)(2,1)} %copy-done.6) | copy-start | bytes 786436
  41.2 10.1 %collective-permute-start.4 = (bf16[256,512]{1,0:T(8,128)(2,1)}, bf16[256,512]{1,0:T(8,128)(2,1)S(1)}, u32[]{:S(2)}, u32[]{:S(2)}) collective-permute-start(bf16[256,512]{1,0:T(8,128)(2,1)} %get-tuple-element.13), channel_id=1, source_target_pairs={{0,1},{1,0},{2,3},{3,2},{4,5},{5,4},{6,7},{7,6},{8,9},{9,8},{10,11... | collective-permute-start | bytes 786440 | tf_op jit(solution)/shard_map/ppermute | solution.py:223
  49.4 3.2 %collective-permute-start.3 = (bf16[256,256]{1,0:T(8,128)(2,1)S(1)}, bf16[256,256]{1,0:T(8,128)(2,1)S(1)}, u32[]{:S(2)}, u32[]{:S(2)}) collective-permute-start(bf16[256,256]{1,0:T(8,128)(2,1)S(1)} %shard_map.124.mine_ref), channel_id=1, source_target_pairs={{0,1},{1,0},{2,3},{3,2},{4,5},{5,4},{6,7},{7,6},{8,9},{9,8},{10,11... | collective-permute-start | bytes 393224 | tf_op jit(solution)/shard_map/ppermute | solution.py:252

commit v5 on v4

--- a/solution.py
+++ b/solution.py
@@ -12,26 +12,32 @@
 BF16, F32 = jnp.bfloat16, jnp.float32
 VMEM = pl.BlockSpec(memory_space=pltpu.VMEM)
 SMEM = pl.BlockSpec(memory_space=pltpu.SMEM)
+HBM = pl.BlockSpec(memory_space=pltpu.HBM)
 MIB = 1024 * 1024
 FIRST = (((0,), (0,)), ((), ()))
 LAST = (((1,), (1,)), ((), ()))
 
 
-def call(kernel, outs, specs, mib, scratch=()):
+def call(kernel, outs, specs, mib, scratch=(), out_spec=VMEM):
     return pl.pallas_call(
         kernel,
         out_shape=outs,
         in_specs=specs,
-        out_specs=jax.tree.map(lambda _: VMEM, outs),
+        out_specs=jax.tree.map(lambda _: out_spec, outs),
         scratch_shapes=list(scratch),
         compiler_params=pltpu.CompilerParams(vmem_limit_bytes=mib * MIB),
     )
 
 
-def copies_kernel(own_ref, out_ref):
-    own = own_ref[...]
-    for z in range(out_ref.shape[0]):
-        out_ref[z] = own
+def copies_kernel(own_ref, out_ref, sems):
+    copies = [
+        pltpu.make_async_copy(own_ref, out_ref.at[z], sems.at[z])
+        for z in range(out_ref.shape[0])
+    ]
+    for copy in copies:
+        copy.start()
+    for copy in copies:
+        copy.wait()
 
 
 def pack_kernel(at_ref, near_ref, far_ref, whole_ref, sent_ref, table_ref):
@@ -41,7 +47,11 @@
     half = near_ref.shape[0]
     for row in range(2 * half):
         lists_ref = near_ref if row < half else far_ref
-        p = jnp.bitwise_xor(at_ref[0], row)
+        differs, k = row % CORES, 1
+        while row >> k:
+            differs ^= (row >> k) % 2 * ((1 << k) - 1) * CORES
+            k += 1
+        p = jnp.bitwise_xor(at_ref[0], differs)
         for s in range(sent_ref.shape[2] // LANES):
             at = pl.ds(pl.multiple_of(lists_ref[row % half, s] * LANES, LANES), LANES)
             sent_ref[p, :, s * LANES : (s + 1) * LANES] = table_ref[:, at]
@@ -200,8 +210,10 @@
     copies = call(
         copies_kernel,
         jax.ShapeDtypeStruct((DEPTH, width, node_count), BF16),
-        [VMEM],
-        2,
+        [HBM],
+        60,
+        [pltpu.SemaphoreType.DMA((DEPTH,))],
+        HBM,
     )(own)
     whole = lax.all_to_all(copies, "z", split_axis=0, concat_axis=0, tiled=True)
     half = hidden // CORES
@@ -230,7 +242,7 @@
     step = 1
     while step < reach:
         near = jnp.concatenate([near, far], axis=0)
-        far = lax.ppermute(near, "x", [(i, i ^ step) for i in range(reach)])
+        far = lax.ppermute(near, "x", [(i, i ^ (2 * step - 1)) for i in range(reach)])
         step *= 2
     columns = DEPTH * width
     sent = call(

time: 91.7 us -> 106 us (1.16)
  Pallas kernels: 7.81 us -> 24 us
    pallas_call x1, Pallas kernels: 0.84 us -> 17.1 us  [local(): call(copies_kernel, jax.ShapeDtypeStruct((DEPTH, width, node_count), BF16...]
    unnamed x26 -> x24, local copies, waits for them, and re-layouts: 4.26 us -> 3.43 us
  transfers between devices with their start and end apart: 7 -> 7, of which waited for: 6 -> 6; matrix products, arithmetic and copies ran while one was open for 0% -> 0% of each run, Pallas kernels for 4% -> 3%
where the time goes in v5:
time: 106 us
  blocking collectives  36.3 us (34%)
  starting transfers between devices  28.8 us (27%)
  Pallas kernels  24 us (23%)
  waiting for transfers between devices  11.8 us (11%)
  local copies, waits for them, and re-layouts  3.44 us (3%)
  between operations  1.5 us (1%)
    all_to_all x1, blocking collectives, local(): lax.all_to_all(sums, ('x', 'z'), split_axis=0, concat_axis=0, tiled=True)  20.8 us
    pallas_call x1, Pallas kernels, local(): call(copies_kernel, jax.ShapeDtypeStruct((DEPTH, width, node_count), BF16...  17.1 us
    all_to_all x1, blocking collectives, local(): lax.all_to_all(spread, 'dp', split_axis=0, concat_axis=0, tiled=True)  15.5 us
    all_to_all x1, starting transfers between devices, local(): whole = lax.all_to_all(copies, 'z', split_axis=0, concat_axis=0, tiled=True)  9.98 us
    ppermute x2, starting transfers between devices, local(): far = lax.ppermute(near, 'x', [(i, i ^ 2 * step - 1) for i in range(reach)])  8.05 us
    all_to_all x1, waiting for transfers between devices, local(): lax.all_to_all(sent, ('x', 'core'), split_axis=0, concat_axis=0, tiled=True)  4.74 us
    all_to_all x1, starting transfers between devices, local(): lax.all_to_all(sent, ('x', 'core'), split_axis=0, concat_axis=0, tiled=True)  4.3 us
    ppermute x2, waiting for transfers between devices, local(): far = lax.ppermute(near, 'x', [(i, i ^ 2 * step - 1) for i in range(reach)])  4.06 us
  transfers between devices with their start and end apart: 7, of which 6 were waited for; matrix products, arithmetic and copies ran while one was open for 0% of the time, Pallas kernels for 3%

profile of v5, /device:TPU:64, one launch (start us, length us, event | category | flops | bytes accessed | tf_op | source)
XLA Modules:
  0.0 105.9 jit_solution(17564453879052052331)
XLA Ops:
  0.7 17.1 %shard_map.121 = bf16[8,2,16384]{2,1,0:T(2,128)(2,1)} custom-call(bf16[2,16384]{1,0:T(2,128)(2,1)} %bitcast.27), custom_call_target="tpu_custom_call" | custom-call | tf_op jit(solution)/shard_map/pallas_call | solution.py:210
  17.7 10.0 %all-to-all-start = ((bf16[8,2,16384]{2,1,0:T(2,128)(2,1)}), bf16[8,2,16384]{2,1,0:T(2,128)(2,1)S(1)}, u32[]{:S(2)}, u32[]{:S(2)}) async-start(bf16[8,2,16384]{2,1,0:T(2,128)(2,1)} %shard_map.121), calls=%async_computation | async-start | bytes 1048576 | tf_op jit(solution)/shard_map/all_to_all | solution.py:218
  27.9 2.0 %collective-permute-start = (s32[1,128]{1,0:T(1,128)S(1)}, s32[1,128]{1,0:T(1,128)S(1)}, u32[]{:S(2)}, u32[]{:S(2)}) collective-permute-start(s32[1,128]{1,0:T(1,128)S(1)} %pad_bitcast_fusion), channel_id=1, source_target_pairs={{0,1},{1,0},{2,3},{3,2},{4,5},{5,4},{6,7},{7,6},{8,9},{9,8},{10,11... | collective-permute-start | bytes 1544 | tf_op jit(solution)/shard_map/ppermute | solution.py:240
  29.9 1.1 %collective-permute-done = s32[1,128]{1,0:T(1,128)S(1)} collective-permute-done((s32[1,128]{1,0:T(1,128)S(1)}, s32[1,128]{1,0:T(1,128)S(1)}, u32[]{:S(2)}, u32[]{:S(2)}) %collective-permute-start) | collective-permute-done | bytes 544 | tf_op jit(solution)/shard_map/ppermute | solution.py:240
  31.0 3.4 %collective-permute-start.1 = (s32[2,128]{1,0:T(2,128)S(1)}, s32[2,128]{1,0:T(2,128)S(1)}, u32[]{:S(2)}, u32[]{:S(2)}) collective-permute-start(s32[2,128]{1,0:T(2,128)S(1)} %pad_add_fusion.1), channel_id=1, source_target_pairs={{0,16},{16,0},{32,48},{48,32},{1,17},{17,1},{33,49},{49,33},{2,18}... | collective-permute-start | bytes 3080 | tf_op jit(solution)/shard_map/ppermute | solution.py:245
  34.4 2.1 %collective-permute-done.1 = s32[2,128]{1,0:T(2,128)S(1)} collective-permute-done((s32[2,128]{1,0:T(2,128)S(1)}, s32[2,128]{1,0:T(2,128)S(1)}, u32[]{:S(2)}, u32[]{:S(2)}) %collective-permute-start.1) | collective-permute-done | bytes 1056 | tf_op jit(solution)/shard_map/ppermute | solution.py:245
  36.5 4.7 %collective-permute-start.2 = (s32[4,128]{1,0:T(4,128)S(1)}, s32[4,128]{1,0:T(4,128)S(1)}, u32[]{:S(2)}, u32[]{:S(2)}) collective-permute-start(s32[4,128]{1,0:T(4,128)S(1)} %pad_add_fusion.near_ref), channel_id=1, source_target_pairs={{0,48},{16,32},{32,16},{48,0},{1,49},{17,33},{33,17},{49,1},{2,50}... | collective-permute-start | bytes 6152 | tf_op jit(solution)/shard_map/ppermute | solution.py:245
  41.1 2.0 %collective-permute-done.2.far_ref = s32[4,128]{1,0:T(4,128)S(1)} collective-permute-done((s32[4,128]{1,0:T(4,128)S(1)}, s32[4,128]{1,0:T(4,128)S(1)}, u32[]{:S(2)}, u32[]{:S(2)}) %collective-permute-start.2) | collective-permute-done | bytes 2080 | tf_op jit(solution)/shard_map/ppermute | solution.py:245
  43.7 2.0 %shard_map.122 = bf16[8,16,3328]{2,1,0:T(8,128)(2,1)} custom-call(s32[1]{0:T(128)} %bitcast.1.at_ref, s32[4,128]{1,0:T(4,128)S(1)} %pad_add_fusion.near_ref, s32[4,128]{1,0:T(4,128)S(1)} %collective-permute-done.2.far_ref, bf16[8,2,16384]{2,1,0:T(2,128)(2,1)S(1)} %all-to-all-done.whole_ref), custom_call_target="tpu_custom_call" | custom-call | tf_op jit(solution)/shard_map/pallas_call | solution.py:248
  45.8 4.3 %all-to-all-start.1 = ((bf16[8,16,3328]{2,1,0:T(8,128)(2,1)}), bf16[8,16,3328]{2,1,0:T(8,128)(2,1)S(1)}, u32[]{:S(2)}, u32[]{:S(2)}) async-start(bf16[8,16,3328]{2,1,0:T(8,128)(2,1)} %shard_map.122), calls=%async_computation.1 | async-start | bytes 1703936 | tf_op jit(solution)/shard_map/all_to_all | solution.py:255
  50.8 1.0 copy-done.1
  51.8 0.9 copy-done.3
  52.8 2.5 %shard_map.123 = (bf16[256,512]{1,0:T(8,128)(2,1)S(1)}, bf16[256,512]{1,0:T(8,128)(2,1)}, bf16[256,512]{1,0:T(8,128)(2,1)S(1)}, f32[1,512]{1,0:T(1,128)S(1)}, bf16[256,3072]{1,0:T(8,128)(2,1)S(1)}) custom-call(s32[1]{0:T(128)} %bitcast.8.core_ref, bf16[256,1024]{1,0:T(8,128)(2,1)S(1)} %bitcast.25, bf16[128,1024]{1,0:T(8,128)(2,1)S(1)} %copy-done.2, ...), custom_call_target="tpu_custom_call" | custom-call | tf_op jit(solution)/shard_map/pallas_call | solution.py:223
  55.2 0.7 copy-done.4
  55.9 0.7 copy-done.6
  56.6 2.5 %collective-permute-start.4 = (bf16[256,512]{1,0:T(8,128)(2,1)}, bf16[256,512]{1,0:T(8,128)(2,1)S(1)}, u32[]{:S(2)}, u32[]{:S(2)}) collective-permute-start(bf16[256,512]{1,0:T(8,128)(2,1)} %get-tuple-element.13), channel_id=1, source_target_pairs={{0,1},{1,0},{2,3},{3,2},{4,5},{5,4},{6,7},{7,6},{8,9},{9,8},{10,11... | collective-permute-start | bytes 786440 | tf_op jit(solution)/shard_map/ppermute | solution.py:235
  59.2 4.7 %all-to-all-done.1 = bf16[8,16,3328]{2,1,0:T(8,128)(2,1)S(1)} async-done(((bf16[8,16,3328]{2,1,0:T(8,128)(2,1)}), bf16[8,16,3328]{2,1,0:T(8,128)(2,1)S(1)}, u32[]{:S(2)}, u32[]{:S(2)}) %all-to-all-start.1) | async-done | bytes 852000 | tf_op jit(solution)/shard_map/all_to_all | solution.py:255
  63.9 0.9 shard_map.124.mine_ref
  64.8 1.9 %collective-permute-start.3 = (bf16[256,256]{1,0:T(8,128)(2,1)S(1)}, bf16[256,256]{1,0:T(8,128)(2,1)S(1)}, u32[]{:S(2)}, u32[]{:S(2)}) collective-permute-start(bf16[256,256]{1,0:T(8,128)(2,1)S(1)} %shard_map.124.mine_ref), channel_id=1, source_target_pairs={{0,1},{1,0},{2,3},{3,2},{4,5},{5,4},{6,7},{7,6},{8,9},{9,8},{10,11... | collective-permute-start | bytes 393224 | tf_op jit(solution)/shard_map/ppermute | solution.py:264
  66.8 1.3 %collective-permute-done.3.theirs_ref = bf16[256,256]{1,0:T(8,128)(2,1)S(1)} collective-permute-done((bf16[256,256]{1,0:T(8,128)(2,1)S(1)}, bf16[256,256]{1,0:T(8,128)(2,1)S(1)}, u32[]{:S(2)}, u32[]{:S(2)}) %collective-permute-start.3) | collective-permute-done | bytes 131104 | tf_op jit(solution)/shard_map/ppermute | solution.py:264
  68.1 0.9 shard_map.125
  69.0 20.8 %all_to_all.20.got_ref = bf16[32,40,128]{2,1,0:T(8,128)(2,1)S(1)} all-to-all(bf16[32,40,128]{2,1,0:T(8,128)(2,1)S(1)} %shard_map.125), channel_id=1, replica_groups=mesh['dp'=8,'x'=4,'z'=8,'core'=2] {'x','z'}, dimensions={0} | all-to-all | bytes 655360 | tf_op jit(solution)/shard_map/all_to_all | solution.py:272
  89.8 15.5 %all_to_all.21.got_ref = bf16[8,40,128]{2,1,0:T(8,128)(2,1)S(1)} all-to-all(bf16[8,40,128]{2,1,0:T(8,128)(2,1)S(1)} %shard_map.126), channel_id=1, replica_groups=mesh['dp'=8,'x'=4,'z'=8,'core'=2] {'dp'}, dimensions={0} | all-to-all | bytes 163840 | tf_op jit(solution)/shard_map/all_to_all | solution.py:279
  105.3 0.6 shard_map.127
  (30 shorter events, 0.8 us)
Async XLA Ops:
  0.6 27.1 %copy-start.9 = (s32[1,24]{1,0:T(1,128)S(1)}, s32[1,24]{1,0:T(1,128)}, u32[]{:S(2)}) copy-start(s32[1,24]{1,0:T(1,128)} %param.14) | copy-start | bytes 292
  0.6 27.1 %copy-start.10 = (s32[1,24,1]{1,2,0:T(1,128)S(1)}, s32[1,24,1]{1,2,0:T(1,128)}, u32[]{:S(2)}) copy-start(s32[1,24,1]{1,2,0:T(1,128)} %param.13) | copy-start | bytes 292
  17.7 26.0 %all-to-all-start = ((bf16[8,2,16384]{2,1,0:T(2,128)(2,1)}), bf16[8,2,16384]{2,1,0:T(2,128)(2,1)S(1)}, u32[]{:S(2)}, u32[]{:S(2)}) async-start(bf16[8,2,16384]{2,1,0:T(2,128)(2,1)} %shard_map.121), calls=%async_computation | async-start | bytes 1048576 | tf_op jit(solution)/shard_map/all_to_all | solution.py:218
  27.7 23.0 %copy-start.11 = (s32[1,24]{1,0:T(1,128)S(1)}, s32[1,24]{1,0:T(1,128)}, u32[]{:S(2)}) copy-start(s32[1,24]{1,0:T(1,128)} %param.12) | copy-start | bytes 292
  27.7 23.0 %copy-start = (bf16[1,24,128,128]{3,2,1,0:T(8,128)(2,1)S(1)}, bf16[1,24,128,128]{3,2,1,0:T(8,128)(2,1)}, u32[]{:S(2)}) copy-start(bf16[1,24,128,128]{3,2,1,0:T(8,128)(2,1)} %param.11) | copy-start | bytes 2359300
  27.7 23.1 %copy-start.2 = (bf16[128,1024]{1,0:T(8,128)(2,1)S(1)}, bf16[128,1024]{1,0:T(8,128)(2,1)}, u32[]{:S(2)}) copy-start(bf16[128,1024]{1,0:T(8,128)(2,1)} %w_self_ref.1) | copy-start | bytes 786436
  27.7 23.1 %copy-start.8 = (f32[1024]{0:T(1024)S(1)}, f32[1024]{0:T(1024)}, u32[]{:S(2)}) copy-start(f32[1024]{0:T(1024)} %param.19) | copy-start | bytes 12292
  27.9 3.1 %collective-permute-start = (s32[1,128]{1,0:T(1,128)S(1)}, s32[1,128]{1,0:T(1,128)S(1)}, u32[]{:S(2)}, u32[]{:S(2)}) collective-permute-start(s32[1,128]{1,0:T(1,128)S(1)} %pad_bitcast_fusion), channel_id=1, source_target_pairs={{0,1},{1,0},{2,3},{3,2},{4,5},{5,4},{6,7},{7,6},{8,9},{9,8},{10,11... | collective-permute-start | bytes 1544 | tf_op jit(solution)/shard_map/ppermute | solution.py:240
  31.0 5.5 %collective-permute-start.1 = (s32[2,128]{1,0:T(2,128)S(1)}, s32[2,128]{1,0:T(2,128)S(1)}, u32[]{:S(2)}, u32[]{:S(2)}) collective-permute-start(s32[2,128]{1,0:T(2,128)S(1)} %pad_add_fusion.1), channel_id=1, source_target_pairs={{0,16},{16,0},{32,48},{48,32},{1,17},{17,1},{33,49},{49,33},{2,18}... | collective-permute-start | bytes 3080 | tf_op jit(solution)/shard_map/ppermute | solution.py:245
  36.5 6.7 %collective-permute-start.2 = (s32[4,128]{1,0:T(4,128)S(1)}, s32[4,128]{1,0:T(4,128)S(1)}, u32[]{:S(2)}, u32[]{:S(2)}) collective-permute-start(s32[4,128]{1,0:T(4,128)S(1)} %pad_add_fusion.near_ref), channel_id=1, source_target_pairs={{0,48},{16,32},{32,16},{48,0},{1,49},{17,33},{33,17},{49,1},{2,50}... | collective-permute-start | bytes 6152 | tf_op jit(solution)/shard_map/ppermute | solution.py:245
  45.8 18.2 %all-to-all-start.1 = ((bf16[8,16,3328]{2,1,0:T(8,128)(2,1)}), bf16[8,16,3328]{2,1,0:T(8,128)(2,1)S(1)}, u32[]{:S(2)}, u32[]{:S(2)}) async-start(bf16[8,16,3328]{2,1,0:T(8,128)(2,1)} %shard_map.122), calls=%async_computation.1 | async-start | bytes 1703936 | tf_op jit(solution)/shard_map/all_to_all | solution.py:255
  50.8 1.0 copy-start.1
  51.8 0.9 copy-start.3
  55.2 0.7 copy-start.4
  55.9 0.7 copy-start.6
  56.6 11.4 %copy-start.5 = (bf16[256,512]{1,0:T(8,128)(2,1)S(1)}, bf16[256,512]{1,0:T(8,128)(2,1)}, u32[]{:S(2)}) copy-start(bf16[256,512]{1,0:T(8,128)(2,1)} %copy-done.4) | copy-start | bytes 786436
  56.6 11.4 %copy-start.7 = (bf16[256,512]{1,0:T(8,128)(2,1)S(1)}, bf16[256,512]{1,0:T(8,128)(2,1)}, u32[]{:S(2)}) copy-start(bf16[256,512]{1,0:T(8,128)(2,1)} %copy-done.6) | copy-start | bytes 786436
  56.6 10.1 %collective-permute-start.4 = (bf16[256,512]{1,0:T(8,128)(2,1)}, bf16[256,512]{1,0:T(8,128)(2,1)S(1)}, u32[]{:S(2)}, u32[]{:S(2)}) collective-permute-start(bf16[256,512]{1,0:T(8,128)(2,1)} %get-tuple-element.13), channel_id=1, source_target_pairs={{0,1},{1,0},{2,3},{3,2},{4,5},{5,4},{6,7},{7,6},{8,9},{9,8},{10,11... | collective-permute-start | bytes 786440 | tf_op jit(solution)/shard_map/ppermute | solution.py:235
  64.8 3.2 %collective-permute-start.3 = (bf16[256,256]{1,0:T(8,128)(2,1)S(1)}, bf16[256,256]{1,0:T(8,128)(2,1)S(1)}, u32[]{:S(2)}, u32[]{:S(2)}) collective-permute-start(bf16[256,256]{1,0:T(8,128)(2,1)S(1)} %shard_map.124.mine_ref), channel_id=1, source_target_pairs={{0,1},{1,0},{2,3},{3,2},{4,5},{5,4},{6,7},{7,6},{8,9},{9,8},{10,11... | collective-permute-start | bytes 393224 | tf_op jit(solution)/shard_map/ppermute | solution.py:264

commit v6 on v4

--- a/solution.py
+++ b/solution.py
@@ -34,16 +34,13 @@
         out_ref[z] = own
 
 
-def pack_kernel(at_ref, near_ref, far_ref, whole_ref, sent_ref, table_ref):
+def pack_kernel(lists_ref, whole_ref, sent_ref, table_ref):
     depth, width = whole_ref.shape[0], whole_ref.shape[1]
     for z in range(depth):
         table_ref[z * width : (z + 1) * width, :] = whole_ref[z]
-    half = near_ref.shape[0]
-    for row in range(2 * half):
-        lists_ref = near_ref if row < half else far_ref
-        p = jnp.bitwise_xor(at_ref[0], row)
+    for p in range(sent_ref.shape[0]):
         for s in range(sent_ref.shape[2] // LANES):
-            at = pl.ds(pl.multiple_of(lists_ref[row % half, s] * LANES, LANES), LANES)
+            at = pl.ds(pl.multiple_of(lists_ref[p, s] * LANES, LANES), LANES)
             sent_ref[p, :, s * LANES : (s + 1) * LANES] = table_ref[:, at]
 
 
@@ -201,7 +198,7 @@
         copies_kernel,
         jax.ShapeDtypeStruct((DEPTH, width, node_count), BF16),
         [VMEM],
-        2,
+        60,
     )(own)
     whole = lax.all_to_all(copies, "z", split_axis=0, concat_axis=0, tiled=True)
     half = hidden // CORES
@@ -224,22 +221,15 @@
     named = tile_owners[0, :, 0] * row_blocks + tile_blocks[0]
     held = (chip * CORES + core) * row_blocks + jnp.arange(row_blocks, dtype=jnp.int32)
     names = jnp.pad(jnp.concatenate([named, held]), (0, LANES - slots - row_blocks))
-    near = names[None]
-    far = lax.ppermute(near, "core", swap)
-    reach = lax.axis_size("x")
-    step = 1
-    while step < reach:
-        near = jnp.concatenate([near, far], axis=0)
-        far = lax.ppermute(near, "x", [(i, i ^ step) for i in range(reach)])
-        step *= 2
+    lists = lax.all_gather(names[None], ("x", "core"), axis=0, tiled=True)
     columns = DEPTH * width
     sent = call(
         pack_kernel,
         jax.ShapeDtypeStruct((peers, columns, (slots + row_blocks) * side), BF16),
-        [SMEM, SMEM, SMEM, VMEM],
+        [SMEM, VMEM],
         8,
         [pltpu.VMEM((columns, node_count), BF16)],
-    )((lax.axis_index("x") * CORES + core)[None], near, far, whole)
+    )(lists, whole)
     got = lax.all_to_all(
         sent, ("x", "core"), split_axis=0, concat_axis=0, tiled=True
     ).reshape(feats, (slots + row_blocks) * side)

time: 91.7 us -> 88.6 us (0.966)
  starting transfers between devices: 29.1 us -> 18.7 us
  blocking collectives: 36.8 us -> 44.4 us
    all_gather x0 -> x1, blocking collectives: none -> 10.6 us  [local(): lists = lax.all_gather(names[None], ('x', 'core'), axis=0, tiled=True)]
    ppermute x3 -> x0, starting transfers between devices: 10.4 us -> none  [the longest x2 8.31 us: local(): far = lax.ppermute(near, 'x', [(i, i ^ step) for i in range(reach)])]
    ppermute x3 -> x0, waiting for transfers between devices: 5.18 us -> none  [the longest x2 4.09 us: local(): far = lax.ppermute(near, 'x', [(i, i ^ step) for i in range(reach)])]
    all_to_all x1, waiting for transfers between devices: 0.29 us -> 5.26 us  [local(): whole = lax.all_to_all(copies, 'z', split_axis=0, concat_axis=0, tiled=True)]
    all_to_all x1, blocking collectives: 21.4 us -> 18.4 us  [local(): lax.all_to_all(sums, ('x', 'z'), split_axis=0, concat_axis=0, tiled=True)]
    unnamed x26 -> x25, local copies, waits for them, and re-layouts: 4.26 us -> 3.4 us
  transfers between devices with their start and end apart: 7 -> 4, of which waited for: 6 -> 3; matrix products, arithmetic and copies ran while one was open for 0% -> 0% of each run, Pallas kernels for 4% -> 4%
where the time goes in v6:
time: 88.6 us; the launch traced here: 88.1 us
  blocking collectives  44.4 us (50%)
  starting transfers between devices  18.7 us (21%)
  waiting for transfers between devices  11.4 us (13%)
  Pallas kernels  8.65 us (10%)
  local copies, waits for them, and re-layouts  3.4 us (4%)
  between operations  1.45 us (2%)
    all_to_all x1, blocking collectives, local(): lax.all_to_all(sums, ('x', 'z'), split_axis=0, concat_axis=0, tiled=True)  18.4 us
    all_to_all x1, blocking collectives, local(): lax.all_to_all(spread, 'dp', split_axis=0, concat_axis=0, tiled=True)  15.5 us
    all_gather x1, blocking collectives, local(): lists = lax.all_gather(names[None], ('x', 'core'), axis=0, tiled=True)  10.6 us
    all_to_all x1, starting transfers between devices, local(): whole = lax.all_to_all(copies, 'z', split_axis=0, concat_axis=0, tiled=True)  9.96 us
    all_to_all x1, waiting for transfers between devices, local(): whole = lax.all_to_all(copies, 'z', split_axis=0, concat_axis=0, tiled=True)  5.26 us
    all_to_all x1, waiting for transfers between devices, local(): lax.all_to_all(sent, ('x', 'core'), split_axis=0, concat_axis=0, tiled=True)  4.79 us
    all_to_all x1, starting transfers between devices, local(): lax.all_to_all(sent, ('x', 'core'), split_axis=0, concat_axis=0, tiled=True)  4.3 us
    unnamed x25, local copies, waits for them, and re-layouts  3.4 us
  transfers between devices with their start and end apart: 4, of which 3 were waited for; matrix products, arithmetic and copies ran while one was open for 0% of the time, Pallas kernels for 4%

profile of v6, /device:TPU:64, one launch (start us, length us, event | category | flops | bytes accessed | tf_op | source)
XLA Modules:
  0.0 88.1 jit_solution(8884174419805347305)
XLA Ops:
  0.7 1.7 %shard_map.121 = bf16[8,2,16384]{2,1,0:T(2,128)(2,1)} custom-call(bf16[2,16384]{1,0:T(2,128)(2,1)} %bitcast.28), custom_call_target="tpu_custom_call" | custom-call | tf_op jit(solution)/shard_map/pallas_call | solution.py:197
  2.3 10.0 %all-to-all-start = ((bf16[8,2,16384]{2,1,0:T(2,128)(2,1)}), bf16[8,2,16384]{2,1,0:T(2,128)(2,1)S(1)}, u32[]{:S(2)}, u32[]{:S(2)}) async-start(bf16[8,2,16384]{2,1,0:T(2,128)(2,1)} %shard_map.121), calls=%async_computation | async-start | bytes 1048576 | tf_op jit(solution)/shard_map/all_to_all | solution.py:203
  12.3 0.0 copy-start.8
  12.4 0.1 pad_add_fusion
  12.5 10.6 %all-gather.1 = s32[8,1,128]{2,1,0:T(1,128)S(1)} all-gather(s32[1,1,128]{2,1,0:T(1,128)S(1)} %pad_bitcast_fusion), channel_id=2, replica_groups=mesh['dp'=8,'x'=4,'z'=8,'core'=2] {'x','core'}, dimensions={0}, use_global_device_ids=true | all-gather | bytes 4608 | tf_op jit(solution)/shard_map/all_gather | solution.py:224
  23.1 5.3 %all-to-all-done.whole_ref = bf16[8,2,16384]{2,1,0:T(2,128)(2,1)S(1)} async-done(((bf16[8,2,16384]{2,1,0:T(2,128)(2,1)}), bf16[8,2,16384]{2,1,0:T(2,128)(2,1)S(1)}, u32[]{:S(2)}, u32[]{:S(2)}) %all-to-all-start) | async-done | bytes 524320 | tf_op jit(solution)/shard_map/all_to_all | solution.py:203
  28.3 2.0 %shard_map.122 = bf16[8,16,3328]{2,1,0:T(8,128)(2,1)} custom-call(s32[8,128]{1,0:T(8,128)S(1)} %bitcast.26, bf16[8,2,16384]{2,1,0:T(2,128)(2,1)S(1)} %all-to-all-done.whole_ref), custom_call_target="tpu_custom_call" | custom-call | tf_op jit(solution)/shard_map/pallas_call | solution.py:226
  30.4 4.3 %all-to-all-start.1 = ((bf16[8,16,3328]{2,1,0:T(8,128)(2,1)}), bf16[8,16,3328]{2,1,0:T(8,128)(2,1)S(1)}, u32[]{:S(2)}, u32[]{:S(2)}) async-start(bf16[8,16,3328]{2,1,0:T(8,128)(2,1)} %shard_map.122), calls=%async_computation.1 | async-start | bytes 1703936 | tf_op jit(solution)/shard_map/all_to_all | solution.py:233
  35.4 0.0 copy-start.1
  35.4 1.0 %copy-done.1 = bf16[1,256,1024]{2,1,0:T(8,128)(2,1)S(1)} copy-done((bf16[1,256,1024]{2,1,0:T(8,128)(2,1)S(1)}, bf16[1,256,1024]{2,1,0:T(8,128)(2,1)}, u32[]{:S(2)}) %copy-start.1) | copy-done | bytes 524312
  36.4 0.9 %copy-done.3 = bf16[128,1024]{1,0:T(8,128)(2,1)S(1)} copy-done((bf16[128,1024]{1,0:T(8,128)(2,1)S(1)}, bf16[128,1024]{1,0:T(8,128)(2,1)}, u32[]{:S(2)}) %copy-start.3) | copy-done | bytes 262168
  37.4 2.5 %shard_map.123 = (bf16[256,512]{1,0:T(8,128)(2,1)S(1)}, bf16[256,512]{1,0:T(8,128)(2,1)}, bf16[256,512]{1,0:T(8,128)(2,1)S(1)}, f32[1,512]{1,0:T(1,128)S(1)}, bf16[256,3072]{1,0:T(8,128)(2,1)S(1)}) custom-call(s32[1]{0:T(128)} %bitcast.8.core_ref, bf16[256,1024]{1,0:T(8,128)(2,1)S(1)} %bitcast.25, bf16[128,1024]{1,0:T(8,128)(2,1)S(1)} %copy-done.2, ...), custom_call_target="tpu_custom_call" | custom-call | tf_op jit(solution)/shard_map/pallas_call | solution.py:208
  39.8 0.7 copy-done.4
  40.5 0.7 copy-done.6
  41.2 2.5 %collective-permute-start.1 = (bf16[256,512]{1,0:T(8,128)(2,1)}, bf16[256,512]{1,0:T(8,128)(2,1)S(1)}, u32[]{:S(2)}, u32[]{:S(2)}) collective-permute-start(bf16[256,512]{1,0:T(8,128)(2,1)} %get-tuple-element.13), channel_id=1, source_target_pairs={{0,1},{1,0},{2,3},{3,2},{4,5},{5,4},{6,7},{7,6},{8,9},{9,8},{10,11... | collective-permute-start | bytes 786440 | tf_op jit(solution)/shard_map/ppermute | solution.py:220
  43.7 4.8 %all-to-all-done.1 = bf16[8,16,3328]{2,1,0:T(8,128)(2,1)S(1)} async-done(((bf16[8,16,3328]{2,1,0:T(8,128)(2,1)}), bf16[8,16,3328]{2,1,0:T(8,128)(2,1)S(1)}, u32[]{:S(2)}, u32[]{:S(2)}) %all-to-all-start.1) | async-done | bytes 852000 | tf_op jit(solution)/shard_map/all_to_all | solution.py:233
  48.5 0.9 %shard_map.124.mine_ref = bf16[256,256]{1,0:T(8,128)(2,1)S(1)} custom-call(bf16[128,3328]{1,0:T(8,128)(2,1)S(1)} %bitcast.23, bf16[256,3072]{1,0:T(8,128)(2,1)S(1)} %get-tuple-element.11.masked_ref), custom_call_target="tpu_custom_call" | custom-call | tf_op jit(solution)/shard_map/pallas_call | solution.py:236
  49.4 1.9 %collective-permute-start = (bf16[256,256]{1,0:T(8,128)(2,1)S(1)}, bf16[256,256]{1,0:T(8,128)(2,1)S(1)}, u32[]{:S(2)}, u32[]{:S(2)}) collective-permute-start(bf16[256,256]{1,0:T(8,128)(2,1)S(1)} %shard_map.124.mine_ref), channel_id=1, source_target_pairs={{0,1},{1,0},{2,3},{3,2},{4,5},{5,4},{6,7},{7,6},{8,9},{9,8},{10,11... | collective-permute-start | bytes 393224 | tf_op jit(solution)/shard_map/ppermute | solution.py:242
  51.4 1.3 %collective-permute-done.theirs_ref = bf16[256,256]{1,0:T(8,128)(2,1)S(1)} collective-permute-done((bf16[256,256]{1,0:T(8,128)(2,1)S(1)}, bf16[256,256]{1,0:T(8,128)(2,1)S(1)}, u32[]{:S(2)}, u32[]{:S(2)}) %collective-permute-start) | collective-permute-done | bytes 131104 | tf_op jit(solution)/shard_map/ppermute | solution.py:242
  52.7 0.9 shard_map.125
  53.6 18.4 %all_to_all.20.got_ref = bf16[32,40,128]{2,1,0:T(8,128)(2,1)S(1)} all-to-all(bf16[32,40,128]{2,1,0:T(8,128)(2,1)S(1)} %shard_map.125), channel_id=1, replica_groups=mesh['dp'=8,'x'=4,'z'=8,'core'=2] {'x','z'}, dimensions={0} | all-to-all | bytes 655360 | tf_op jit(solution)/shard_map/all_to_all | solution.py:250
  72.0 0.1 shard_map.126
  72.0 15.5 %all_to_all.21.got_ref = bf16[8,40,128]{2,1,0:T(8,128)(2,1)S(1)} all-to-all(bf16[8,40,128]{2,1,0:T(8,128)(2,1)S(1)} %shard_map.126), channel_id=1, replica_groups=mesh['dp'=8,'x'=4,'z'=8,'core'=2] {'dp'}, dimensions={0} | all-to-all | bytes 163840 | tf_op jit(solution)/shard_map/all_to_all | solution.py:257
  87.5 0.6 shard_map.127
  (23 shorter events, 0.1 us)
Async XLA Ops:
  0.6 11.7 %copy-start.9 = (s32[1,24]{1,0:T(1,128)S(1)}, s32[1,24]{1,0:T(1,128)}, u32[]{:S(2)}) copy-start(s32[1,24]{1,0:T(1,128)} %param.14) | copy-start | bytes 292
  0.6 11.7 %copy-start.10 = (s32[1,24,1]{1,2,0:T(1,128)S(1)}, s32[1,24,1]{1,2,0:T(1,128)}, u32[]{:S(2)}) copy-start(s32[1,24,1]{1,2,0:T(1,128)} %param.13) | copy-start | bytes 292
  2.3 26.0 %all-to-all-start = ((bf16[8,2,16384]{2,1,0:T(2,128)(2,1)}), bf16[8,2,16384]{2,1,0:T(2,128)(2,1)S(1)}, u32[]{:S(2)}, u32[]{:S(2)}) async-start(bf16[8,2,16384]{2,1,0:T(2,128)(2,1)} %shard_map.121), calls=%async_computation | async-start | bytes 1048576 | tf_op jit(solution)/shard_map/all_to_all | solution.py:203
  12.3 23.0 %copy-start.11 = (s32[1,24]{1,0:T(1,128)S(1)}, s32[1,24]{1,0:T(1,128)}, u32[]{:S(2)}) copy-start(s32[1,24]{1,0:T(1,128)} %param.12) | copy-start | bytes 292
  12.3 23.0 %copy-start = (bf16[1,24,128,128]{3,2,1,0:T(8,128)(2,1)S(1)}, bf16[1,24,128,128]{3,2,1,0:T(8,128)(2,1)}, u32[]{:S(2)}) copy-start(bf16[1,24,128,128]{3,2,1,0:T(8,128)(2,1)} %param.11) | copy-start | bytes 2359300
  12.3 23.1 %copy-start.2 = (bf16[128,1024]{1,0:T(8,128)(2,1)S(1)}, bf16[128,1024]{1,0:T(8,128)(2,1)}, u32[]{:S(2)}) copy-start(bf16[128,1024]{1,0:T(8,128)(2,1)} %w_self_ref.1) | copy-start | bytes 786436
  12.3 23.1 %copy-start.8 = (f32[1024]{0:T(1024)S(1)}, f32[1024]{0:T(1024)}, u32[]{:S(2)}) copy-start(f32[1024]{0:T(1024)} %param.19) | copy-start | bytes 12292
  30.4 18.2 %all-to-all-start.1 = ((bf16[8,16,3328]{2,1,0:T(8,128)(2,1)}), bf16[8,16,3328]{2,1,0:T(8,128)(2,1)S(1)}, u32[]{:S(2)}, u32[]{:S(2)}) async-start(bf16[8,16,3328]{2,1,0:T(8,128)(2,1)} %shard_map.122), calls=%async_computation.1 | async-start | bytes 1703936 | tf_op jit(solution)/shard_map/all_to_all | solution.py:233
  35.4 1.0 %copy-start.1 = (bf16[1,256,1024]{2,1,0:T(8,128)(2,1)S(1)}, bf16[1,256,1024]{2,1,0:T(8,128)(2,1)}, u32[]{:S(2)}) copy-start(bf16[1,256,1024]{2,1,0:T(8,128)(2,1)} %param.16) | copy-start | bytes 1572868
  36.4 0.9 %copy-start.3 = (bf16[128,1024]{1,0:T(8,128)(2,1)S(1)}, bf16[128,1024]{1,0:T(8,128)(2,1)}, u32[]{:S(2)}) copy-start(bf16[128,1024]{1,0:T(8,128)(2,1)} %w_neigh_ref.1) | copy-start | bytes 786436
  39.8 0.7 copy-start.4
  40.5 0.7 copy-start.6
  41.2 11.5 %copy-start.5 = (bf16[256,512]{1,0:T(8,128)(2,1)S(1)}, bf16[256,512]{1,0:T(8,128)(2,1)}, u32[]{:S(2)}) copy-start(bf16[256,512]{1,0:T(8,128)(2,1)} %copy-done.4) | copy-start | bytes 786436
  41.2 11.5 %copy-start.7 = (bf16[256,512]{1,0:T(8,128)(2,1)S(1)}, bf16[256,512]{1,0:T(8,128)(2,1)}, u32[]{:S(2)}) copy-start(bf16[256,512]{1,0:T(8,128)(2,1)} %copy-done.6) | copy-start | bytes 786436
  41.2 10.2 %collective-permute-start.1 = (bf16[256,512]{1,0:T(8,128)(2,1)}, bf16[256,512]{1,0:T(8,128)(2,1)S(1)}, u32[]{:S(2)}, u32[]{:S(2)}) collective-permute-start(bf16[256,512]{1,0:T(8,128)(2,1)} %get-tuple-element.13), channel_id=1, source_target_pairs={{0,1},{1,0},{2,3},{3,2},{4,5},{5,4},{6,7},{7,6},{8,9},{9,8},{10,11... | collective-permute-start | bytes 786440 | tf_op jit(solution)/shard_map/ppermute | solution.py:220
  49.4 3.2 %collective-permute-start = (bf16[256,256]{1,0:T(8,128)(2,1)S(1)}, bf16[256,256]{1,0:T(8,128)(2,1)S(1)}, u32[]{:S(2)}, u32[]{:S(2)}) collective-permute-start(bf16[256,256]{1,0:T(8,128)(2,1)S(1)} %shard_map.124.mine_ref), channel_id=1, source_target_pairs={{0,1},{1,0},{2,3},{3,2},{4,5},{5,4},{6,7},{7,6},{8,9},{9,8},{10,11... | collective-permute-start | bytes 393224 | tf_op jit(solution)/shard_map/ppermute | solution.py:242

commit v7 on v6

--- a/solution.py
+++ b/solution.py
@@ -7,7 +7,7 @@
 from jax.experimental.pallas import tpu as pltpu
 from jax.sharding import Mesh, PartitionSpec as P
 
-CORES, DEPTH = 2, 8
+CORES, HIGH, LOW = 2, 4, 2
 LANES, SUBLANES = 128, 8
 BF16, F32 = jnp.bfloat16, jnp.float32
 VMEM = pl.BlockSpec(memory_space=pltpu.VMEM)
@@ -34,17 +34,23 @@
         out_ref[z] = own
 
 
-def pack_kernel(lists_ref, whole_ref, sent_ref, table_ref):
-    depth, width = whole_ref.shape[0], whole_ref.shape[1]
-    for z in range(depth):
+def table_kernel(lists_ref, whole_ref, table_ref):
+    del lists_ref
+    high, width = whole_ref.shape[0], whole_ref.shape[1]
+    for z in range(high):
         table_ref[z * width : (z + 1) * width, :] = whole_ref[z]
+
+
+def pack_kernel(lists_ref, own_ref, other_ref, sent_ref):
     for p in range(sent_ref.shape[0]):
         for s in range(sent_ref.shape[2] // LANES):
             at = pl.ds(pl.multiple_of(lists_ref[p, s] * LANES, LANES), LANES)
-            sent_ref[p, :, s * LANES : (s + 1) * LANES] = table_ref[:, at]
-
-
-def gather_kernel(width, got_ref, masked_ref, inputs_ref):
+            sent_ref[p, :, s * LANES : (s + 1) * LANES] = jnp.concatenate(
+                [own_ref[:, at], other_ref[:, at]], axis=0
+            )
+
+
+def gather_kernel(width, core_ref, got_ref, masked_ref, inputs_ref):
     feats = got_ref.shape[0]
     named = masked_ref.shape[1]
     agg = lax.dot_general(
@@ -55,11 +61,12 @@
     ).astype(BF16)
     row = lax.broadcasted_iota(jnp.int32, (feats, feats), 0)
     feature = lax.broadcasted_iota(jnp.int32, (feats, feats), 1)
-    column = row % width
-    z = row // width % DEPTH
-    core = row // (width * DEPTH) % CORES
-    x = row // (width * DEPTH * CORES)
-    place = ((x * DEPTH + z) * CORES + core) * width + column
+    column, zh = row % width, row // width % HIGH
+    rest = row // (width * HIGH)
+    parity = jnp.bitwise_xor(rest % CORES, core_ref[0])
+    reach = feats // (width * HIGH * CORES * LOW)
+    x, zl = rest // CORES % reach, rest // (CORES * reach)
+    place = (((x * HIGH + zh) * LOW + zl) * CORES + parity) * width + column
     order = jnp.where(place == feature, 1.0, 0.0).astype(BF16)
     for k, value in enumerate((got_ref[:, named:], agg)):
         inputs_ref[:, k * feats : (k + 1) * feats] = lax.dot_general(
@@ -184,23 +191,24 @@
     width, node_count = own.shape
     slots, side = tile_weights.shape[1], tile_weights.shape[2]
     batches = lax.axis_size("dp")
-    peers = lax.axis_size("x") * CORES
-    chips = lax.axis_size("x") * DEPTH
+    peers = lax.axis_size("x") * LOW
+    chips = peers * HIGH
     feats, hidden = w_self.shape
     nodes_here = cotangent.shape[1]
     row_blocks = nodes_here // side
     core = lax.axis_index("core")
-    chip = lax.axis_index("x") * DEPTH + lax.axis_index("z")
+    chip = lax.axis_index("x") * HIGH + lax.axis_index("zh")
+    chip = chip * LOW + lax.axis_index("zl")
     core_at, chip_at = core[None], chip[None]
     swap = [(i, CORES - 1 - i) for i in range(CORES)]
 
     copies = call(
         copies_kernel,
-        jax.ShapeDtypeStruct((DEPTH, width, node_count), BF16),
+        jax.ShapeDtypeStruct((HIGH, width, node_count), BF16),
         [VMEM],
         60,
     )(own)
-    whole = lax.all_to_all(copies, "z", split_axis=0, concat_axis=0, tiled=True)
+    whole = lax.all_to_all(copies, "zh", split_axis=0, concat_axis=0, tiled=True)
     half = hidden // CORES
     part = half // chips
     live = jnp.arange(slots, dtype=jnp.int32) < tile_counts[0, 0]
@@ -221,24 +229,31 @@
     named = tile_owners[0, :, 0] * row_blocks + tile_blocks[0]
     held = (chip * CORES + core) * row_blocks + jnp.arange(row_blocks, dtype=jnp.int32)
     names = jnp.pad(jnp.concatenate([named, held]), (0, LANES - slots - row_blocks))
-    lists = lax.all_gather(names[None], ("x", "core"), axis=0, tiled=True)
-    columns = DEPTH * width
+    lists = lax.all_gather(names[None], "x", axis=0, tiled=True)
+    table = call(
+        table_kernel,
+        jax.ShapeDtypeStruct((HIGH * width, node_count), BF16),
+        [SMEM, VMEM],
+        4,
+    )(lists, whole)
+    other = lax.ppermute(table, "core", swap)
+    lists = lax.all_gather(lists, "zl", axis=0, tiled=True)
+    columns = CORES * HIGH * width
     sent = call(
         pack_kernel,
         jax.ShapeDtypeStruct((peers, columns, (slots + row_blocks) * side), BF16),
-        [SMEM, VMEM],
+        [SMEM, VMEM, VMEM],
         8,
-        [pltpu.VMEM((columns, node_count), BF16)],
-    )(lists, whole)
+    )(lists, table, other)
     got = lax.all_to_all(
-        sent, ("x", "core"), split_axis=0, concat_axis=0, tiled=True
+        sent, ("zl", "x"), split_axis=0, concat_axis=0, tiled=True
     ).reshape(feats, (slots + row_blocks) * side)
     mine = call(
         functools.partial(gather_kernel, width),
         jax.ShapeDtypeStruct((nodes_here, 2 * feats), BF16),
-        [VMEM, VMEM],
+        [SMEM, VMEM, VMEM],
         12,
-    )(got, masked)
+    )(core_at, got, masked)
     theirs = lax.ppermute(mine, "core", swap)
     rows = 2 * part + SUBLANES
     sums = call(
@@ -247,7 +262,7 @@
         [VMEM] * 6,
         16,
     )(mine, theirs, cot, their_cot, weights, half_bias)
-    parts = lax.all_to_all(sums, ("x", "z"), split_axis=0, concat_axis=0, tiled=True)
+    parts = lax.all_to_all(sums, ("x", "zh", "zl"), split_axis=0, concat_axis=0, tiled=True)
     spread = call(
         spread_kernel,
         jax.ShapeDtypeStruct((batches, rows, feats), BF16),
@@ -270,12 +285,12 @@
 
 
 def solution(mesh):
-    batches, owners = mesh.devices.shape
+    batches = mesh.devices.shape[0]
     split = Mesh(
-        mesh.devices.reshape(batches, owners // (DEPTH * CORES), DEPTH, CORES),
-        ("dp", "x", "z", "core"),
+        mesh.devices.reshape(batches, -1, HIGH, LOW, CORES),
+        ("dp", "x", "zh", "zl", "core"),
     )
-    feat = ("x", "z", "core")
+    feat = ("x", "zh", "zl", "core")
     return jax.shard_map(
         local,
         mesh=split,

time: 88.6 us -> 91.7 us (1.035)
  waiting for transfers between devices: 11.4 us -> 4.36 us
  blocking collectives: 44.4 us -> 50.9 us
  starting transfers between devices: 18.7 us -> 21.1 us
    all_to_all x2, waiting for transfers between devices: 10 us -> 3.05 us  [the longest x1 3.05 us: local(): lax.all_to_all(sent, ('zl', 'x'), split_axis=0, concat_axis=0, tiled=True)]
    all_gather x1 -> x2, blocking collectives: 10.6 us -> 14 us  [the longest x1 9.65 us: local(): lists = lax.all_gather(names[None], 'x', axis=0, tiled=True)]
    all_to_all x1, blocking collectives: 18.4 us -> 21.4 us  [local(): lax.all_to_all(sums, ('x', 'zh', 'zl'), split_axis=0, concat_axis=0, tile...]
    ppermute x0 -> x1, starting transfers between devices: none -> 2.05 us  [local(): other = lax.ppermute(table, 'core', swap)]
    pallas_call x1 -> x2, Pallas kernels: 1.68 us -> 2.27 us  [the longest x1 1.56 us: local(): call(copies_kernel, jax.ShapeDtypeStruct((HIGH, width, node_count), BF16)...]
    unnamed x25 -> x21, local copies, waits for them, and re-layouts: 3.4 us -> 3.41 us
  transfers between devices with their start and end apart: 4 -> 5, of which waited for: 3 -> 2; matrix products, arithmetic and copies ran while one was open for 0% -> 1% of each run, Pallas kernels for 4% -> 4%
where the time goes in v7:
time: 91.7 us; the launch traced here: 91.1 us
  blocking collectives  50.9 us (56%)
  starting transfers between devices  21.1 us (23%)
  Pallas kernels  9.1 us (10%)
  waiting for transfers between devices  4.36 us (5%)
  local copies, waits for them, and re-layouts  3.41 us (4%)
  between operations  1.43 us (2%)
    all_to_all x1, blocking collectives, local(): lax.all_to_all(sums, ('x', 'zh', 'zl'), split_axis=0, concat_axis=0, tile...  21.4 us
    all_to_all x1, blocking collectives, local(): lax.all_to_all(spread, 'dp', split_axis=0, concat_axis=0, tiled=True)  15.4 us
    all_gather x1, blocking collectives, local(): lists = lax.all_gather(names[None], 'x', axis=0, tiled=True)  9.65 us
    all_to_all x1, starting transfers between devices, local(): lax.all_to_all(copies, 'zh', split_axis=0, concat_axis=0, tiled=True)  9.4 us
    all_to_all x1, starting transfers between devices, local(): lax.all_to_all(sent, ('zl', 'x'), split_axis=0, concat_axis=0, tiled=True)  5.73 us
    all_gather x1, blocking collectives, local(): lists = lax.all_gather(lists, 'zl', axis=0, tiled=True)  4.34 us
    unnamed x21, local copies, waits for them, and re-layouts  3.41 us
    all_to_all x1, waiting for transfers between devices, local(): lax.all_to_all(sent, ('zl', 'x'), split_axis=0, concat_axis=0, tiled=True)  3.05 us
  transfers between devices with their start and end apart: 5, of which 2 were waited for; matrix products, arithmetic and copies ran while one was open for 1% of the time, Pallas kernels for 4%

profile of v7, /device:TPU:64, one launch (start us, length us, event | category | flops | bytes accessed | tf_op | source)
XLA Modules:
  0.0 91.1 jit_solution(7363559130238994882)
XLA Ops:
  0.6 1.6 %shard_map.121 = bf16[4,2,16384]{2,1,0:T(2,128)(2,1)} custom-call(bf16[2,16384]{1,0:T(2,128)(2,1)} %bitcast.32), custom_call_target="tpu_custom_call" | custom-call | tf_op jit(solution)/shard_map/pallas_call | solution.py:205
  2.2 9.4 %all-to-all-start = ((bf16[4,2,16384]{2,1,0:T(2,128)(2,1)}), bf16[4,2,16384]{2,1,0:T(2,128)(2,1)S(1)}, u32[]{:S(2)}, u32[]{:S(2)}) async-start(bf16[4,2,16384]{2,1,0:T(2,128)(2,1)} %shard_map.121), calls=%async_computation | async-start | bytes 524288 | tf_op jit(solution)/shard_map/all_to_all | solution.py:211
  11.6 0.7 bitcast_add_fusion
  12.3 0.1 pad_add_fusion
  12.4 9.7 %all-gather.1 = s32[4,1,128]{2,1,0:T(1,128)S(1)} all-gather(s32[1,1,128]{2,1,0:T(1,128)S(1)} %pad_bitcast_fusion), channel_id=2, replica_groups=mesh['dp'=8,'x'=4,'zh'=4,'zl'=2,'core'=2] {'x'}, dimensions={0}, use_global_device_ids=true | all-gather | bytes 2560 | tf_op jit(solution)/shard_map/all_gather | solution.py:232
  22.0 0.7 shard_map.122.own_ref
  22.8 2.1 %collective-permute-start = (bf16[8,16384]{1,0:T(8,128)(2,1)S(1)}, bf16[8,16384]{1,0:T(8,128)(2,1)S(1)}, u32[]{:S(2)}, u32[]{:S(2)}) collective-permute-start(bf16[8,16384]{1,0:T(8,128)(2,1)S(1)} %shard_map.122.own_ref), channel_id=1, source_target_pairs={{0,1},{1,0},{2,3},{3,2},{4,5},{5,4},{6,7},{7,6},{8,9},{9,8},{10,11... | collective-permute-start | bytes 786440 | tf_op jit(solution)/shard_map/ppermute | solution.py:239
  24.8 4.3 %all-gather.2 = s32[2,4,128]{2,1,0:T(4,128)S(1)} all-gather(s32[1,4,128]{2,1,0:T(4,128)S(1)} %bitcast.29), channel_id=1, replica_groups=mesh['dp'=8,'x'=4,'zh'=4,'zl'=2,'core'=2] {'zl'}, dimensions={0}, use_global_device_ids=true | all-gather | bytes 6144 | tf_op jit(solution)/shard_map/all_gather | solution.py:240
  29.2 1.9 %shard_map.123 = bf16[8,16,3328]{2,1,0:T(8,128)(2,1)} custom-call(s32[8,128]{1,0:T(8,128)S(1)} %bitcast.30, bf16[8,16384]{1,0:T(8,128)(2,1)S(1)} %shard_map.122.own_ref, bf16[8,16384]{1,0:T(8,128)(2,1)S(1)} %collective-permute-done.other_ref), custom_call_target="tpu_custom_call" | custom-call | tf_op jit(solution)/shard_map/pallas_call | solution.py:242
  31.1 5.7 %all-to-all-start.1 = ((bf16[8,16,3328]{2,1,0:T(8,128)(2,1)}), bf16[8,16,3328]{2,1,0:T(8,128)(2,1)S(1)}, u32[]{:S(2)}, u32[]{:S(2)}) async-start(bf16[8,16,3328]{2,1,0:T(8,128)(2,1)} %shard_map.123), calls=%async_computation.1 | async-start | bytes 1703936 | tf_op jit(solution)/shard_map/all_to_all | solution.py:248
  37.5 1.0 %copy-done.1 = bf16[1,256,1024]{2,1,0:T(8,128)(2,1)S(1)} copy-done((bf16[1,256,1024]{2,1,0:T(8,128)(2,1)S(1)}, bf16[1,256,1024]{2,1,0:T(8,128)(2,1)}, u32[]{:S(2)}) %copy-start.1) | copy-done | bytes 524312
  38.6 0.9 %copy-done.3 = bf16[128,1024]{1,0:T(8,128)(2,1)S(1)} copy-done((bf16[128,1024]{1,0:T(8,128)(2,1)S(1)}, bf16[128,1024]{1,0:T(8,128)(2,1)}, u32[]{:S(2)}) %copy-start.3) | copy-done | bytes 262168
  39.5 2.5 %shard_map.124 = (bf16[256,512]{1,0:T(8,128)(2,1)S(1)}, bf16[256,512]{1,0:T(8,128)(2,1)}, bf16[256,512]{1,0:T(8,128)(2,1)S(1)}, f32[1,512]{1,0:T(1,128)S(1)}, bf16[256,3072]{1,0:T(8,128)(2,1)S(1)}) custom-call(s32[1]{0:T(128)} %bitcast.1.core_ref, bf16[256,1024]{1,0:T(8,128)(2,1)S(1)} %bitcast.27, bf16[128,1024]{1,0:T(8,128)(2,1)S(1)} %copy-done.2, ...), custom_call_target="tpu_custom_call" | custom-call | tf_op jit(solution)/shard_map/pallas_call | solution.py:216
  42.0 0.7 copy-done.4
  42.7 0.7 copy-done.6
  43.4 2.0 %collective-permute-start.2 = (bf16[256,512]{1,0:T(8,128)(2,1)}, bf16[256,512]{1,0:T(8,128)(2,1)S(1)}, u32[]{:S(2)}, u32[]{:S(2)}) collective-permute-start(bf16[256,512]{1,0:T(8,128)(2,1)} %get-tuple-element.13), channel_id=1, source_target_pairs={{0,1},{1,0},{2,3},{3,2},{4,5},{5,4},{6,7},{7,6},{8,9},{9,8},{10,11... | collective-permute-start | bytes 786440 | tf_op jit(solution)/shard_map/ppermute | solution.py:228
  45.4 3.0 %all-to-all-done.1 = bf16[8,16,3328]{2,1,0:T(8,128)(2,1)S(1)} async-done(((bf16[8,16,3328]{2,1,0:T(8,128)(2,1)}), bf16[8,16,3328]{2,1,0:T(8,128)(2,1)S(1)}, u32[]{:S(2)}, u32[]{:S(2)}) %all-to-all-start.1) | async-done | bytes 852000 | tf_op jit(solution)/shard_map/all_to_all | solution.py:248
  48.4 0.9 shard_map.125.mine_ref
  49.4 1.9 %collective-permute-start.1 = (bf16[256,256]{1,0:T(8,128)(2,1)S(1)}, bf16[256,256]{1,0:T(8,128)(2,1)S(1)}, u32[]{:S(2)}, u32[]{:S(2)}) collective-permute-start(bf16[256,256]{1,0:T(8,128)(2,1)S(1)} %shard_map.125.mine_ref), channel_id=1, source_target_pairs={{0,1},{1,0},{2,3},{3,2},{4,5},{5,4},{6,7},{7,6},{8,9},{9,8},{10,11... | collective-permute-start | bytes 393224 | tf_op jit(solution)/shard_map/ppermute | solution.py:257
  51.3 1.3 %collective-permute-done.1.theirs_ref = bf16[256,256]{1,0:T(8,128)(2,1)S(1)} collective-permute-done((bf16[256,256]{1,0:T(8,128)(2,1)S(1)}, bf16[256,256]{1,0:T(8,128)(2,1)S(1)}, u32[]{:S(2)}, u32[]{:S(2)}) %collective-permute-start.1) | collective-permute-done | bytes 131104 | tf_op jit(solution)/shard_map/ppermute | solution.py:257
  52.6 0.9 shard_map.126
  53.5 21.4 %all_to_all.20.got_ref = bf16[32,40,128]{2,1,0:T(8,128)(2,1)S(1)} all-to-all(bf16[32,40,128]{2,1,0:T(8,128)(2,1)S(1)} %shard_map.126), channel_id=1, replica_groups=mesh['dp'=8,'x'=4,'zh'=4,'zl'=2,'core'=2] {'x','zh','zl'}, dimensions={0} | all-to-all | bytes 655360 | tf_op jit(solution)/shard_map/all_to_all | solution.py:265
  75.0 15.4 %all_to_all.21.got_ref = bf16[8,40,128]{2,1,0:T(8,128)(2,1)S(1)} all-to-all(bf16[8,40,128]{2,1,0:T(8,128)(2,1)S(1)} %shard_map.127), channel_id=1, replica_groups=mesh['dp'=8,'x'=4,'zh'=4,'zl'=2,'core'=2] {'dp'}, dimensions={0} | all-to-all | bytes 163840 | tf_op jit(solution)/shard_map/all_to_all | solution.py:272
  90.4 0.6 shard_map.128
  (23 shorter events, 0.1 us)
Async XLA Ops:
  2.2 19.8 %all-to-all-start = ((bf16[4,2,16384]{2,1,0:T(2,128)(2,1)}), bf16[4,2,16384]{2,1,0:T(2,128)(2,1)S(1)}, u32[]{:S(2)}, u32[]{:S(2)}) async-start(bf16[4,2,16384]{2,1,0:T(2,128)(2,1)} %shard_map.121), calls=%async_computation | async-start | bytes 524288 | tf_op jit(solution)/shard_map/all_to_all | solution.py:211
  22.7 14.7 %copy-start.9 = (s32[1,24]{1,0:T(1,128)S(1)}, s32[1,24]{1,0:T(1,128)}, u32[]{:S(2)}) copy-start(s32[1,24]{1,0:T(1,128)} %param.12) | copy-start | bytes 292
  22.7 14.7 %copy-start = (bf16[1,24,128,128]{3,2,1,0:T(8,128)(2,1)S(1)}, bf16[1,24,128,128]{3,2,1,0:T(8,128)(2,1)}, u32[]{:S(2)}) copy-start(bf16[1,24,128,128]{3,2,1,0:T(8,128)(2,1)} %param.11) | copy-start | bytes 2359300
  22.8 14.7 %copy-start.2 = (bf16[128,1024]{1,0:T(8,128)(2,1)S(1)}, bf16[128,1024]{1,0:T(8,128)(2,1)}, u32[]{:S(2)}) copy-start(bf16[128,1024]{1,0:T(8,128)(2,1)} %w_self_ref.1) | copy-start | bytes 786436
  22.8 14.7 %copy-start.8 = (f32[1024]{0:T(1024)S(1)}, f32[1024]{0:T(1024)}, u32[]{:S(2)}) copy-start(f32[1024]{0:T(1024)} %param.19) | copy-start | bytes 12292
  22.8 6.4 %collective-permute-start = (bf16[8,16384]{1,0:T(8,128)(2,1)S(1)}, bf16[8,16384]{1,0:T(8,128)(2,1)S(1)}, u32[]{:S(2)}, u32[]{:S(2)}) collective-permute-start(bf16[8,16384]{1,0:T(8,128)(2,1)S(1)} %shard_map.122.own_ref), channel_id=1, source_target_pairs={{0,1},{1,0},{2,3},{3,2},{4,5},{5,4},{6,7},{7,6},{8,9},{9,8},{10,11... | collective-permute-start | bytes 786440 | tf_op jit(solution)/shard_map/ppermute | solution.py:239
  31.1 17.4 %all-to-all-start.1 = ((bf16[8,16,3328]{2,1,0:T(8,128)(2,1)}), bf16[8,16,3328]{2,1,0:T(8,128)(2,1)S(1)}, u32[]{:S(2)}, u32[]{:S(2)}) async-start(bf16[8,16,3328]{2,1,0:T(8,128)(2,1)} %shard_map.123), calls=%async_computation.1 | async-start | bytes 1703936 | tf_op jit(solution)/shard_map/all_to_all | solution.py:248
  37.5 1.0 %copy-start.1 = (bf16[1,256,1024]{2,1,0:T(8,128)(2,1)S(1)}, bf16[1,256,1024]{2,1,0:T(8,128)(2,1)}, u32[]{:S(2)}) copy-start(bf16[1,256,1024]{2,1,0:T(8,128)(2,1)} %param.16) | copy-start | bytes 1572868
  38.5 0.9 %copy-start.3 = (bf16[128,1024]{1,0:T(8,128)(2,1)S(1)}, bf16[128,1024]{1,0:T(8,128)(2,1)}, u32[]{:S(2)}) copy-start(bf16[128,1024]{1,0:T(8,128)(2,1)} %w_neigh_ref.1) | copy-start | bytes 786436
  42.0 0.7 copy-start.4
  42.7 0.7 copy-start.6
  43.4 9.2 %copy-start.5 = (bf16[256,512]{1,0:T(8,128)(2,1)S(1)}, bf16[256,512]{1,0:T(8,128)(2,1)}, u32[]{:S(2)}) copy-start(bf16[256,512]{1,0:T(8,128)(2,1)} %copy-done.4) | copy-start | bytes 786436
  43.4 9.2 %copy-start.7 = (bf16[256,512]{1,0:T(8,128)(2,1)S(1)}, bf16[256,512]{1,0:T(8,128)(2,1)}, u32[]{:S(2)}) copy-start(bf16[256,512]{1,0:T(8,128)(2,1)} %copy-done.6) | copy-start | bytes 786436
  43.4 7.9 %collective-permute-start.2 = (bf16[256,512]{1,0:T(8,128)(2,1)}, bf16[256,512]{1,0:T(8,128)(2,1)S(1)}, u32[]{:S(2)}, u32[]{:S(2)}) collective-permute-start(bf16[256,512]{1,0:T(8,128)(2,1)} %get-tuple-element.13), channel_id=1, source_target_pairs={{0,1},{1,0},{2,3},{3,2},{4,5},{5,4},{6,7},{7,6},{8,9},{9,8},{10,11... | collective-permute-start | bytes 786440 | tf_op jit(solution)/shard_map/ppermute | solution.py:228
  49.4 3.2 %collective-permute-start.1 = (bf16[256,256]{1,0:T(8,128)(2,1)S(1)}, bf16[256,256]{1,0:T(8,128)(2,1)S(1)}, u32[]{:S(2)}, u32[]{:S(2)}) collective-permute-start(bf16[256,256]{1,0:T(8,128)(2,1)S(1)} %shard_map.125.mine_ref), channel_id=1, source_target_pairs={{0,1},{1,0},{2,3},{3,2},{4,5},{5,4},{6,7},{7,6},{8,9},{9,8},{10,11... | collective-permute-start | bytes 393224 | tf_op jit(solution)/shard_map/ppermute | solution.py:257

commit v8 on v6

--- a/solution.py
+++ b/solution.py
@@ -17,12 +17,12 @@
 LAST = (((1,), (1,)), ((), ()))
 
 
-def call(kernel, outs, specs, mib, scratch=()):
+def call(kernel, outs, specs, mib, scratch=(), out_spec=VMEM):
     return pl.pallas_call(
         kernel,
         out_shape=outs,
         in_specs=specs,
-        out_specs=jax.tree.map(lambda _: VMEM, outs),
+        out_specs=jax.tree.map(lambda _: out_spec, outs),
         scratch_shapes=list(scratch),
         compiler_params=pltpu.CompilerParams(vmem_limit_bytes=mib * MIB),
     )
@@ -34,14 +34,20 @@
         out_ref[z] = own
 
 
-def pack_kernel(lists_ref, whole_ref, sent_ref, table_ref):
+def pack_kernel(lists_ref, whole_ref, sent_ref, table_ref, chunks_ref, sems):
     depth, width = whole_ref.shape[0], whole_ref.shape[1]
     for z in range(depth):
         table_ref[z * width : (z + 1) * width, :] = whole_ref[z]
-    for p in range(sent_ref.shape[0]):
-        for s in range(sent_ref.shape[2] // LANES):
+    copies = []
+    for p in range(chunks_ref.shape[0]):
+        for s in range(chunks_ref.shape[2] // LANES):
             at = pl.ds(pl.multiple_of(lists_ref[p, s] * LANES, LANES), LANES)
-            sent_ref[p, :, s * LANES : (s + 1) * LANES] = table_ref[:, at]
+            chunks_ref[p, :, s * LANES : (s + 1) * LANES] = table_ref[:, at]
+        copy = pltpu.make_async_copy(chunks_ref.at[p], sent_ref.at[p], sems.at[p])
+        copy.start()
+        copies.append(copy)
+    for copy in copies:
+        copy.wait()
 
 
 def gather_kernel(width, got_ref, masked_ref, inputs_ref):
@@ -57,8 +63,9 @@
     feature = lax.broadcasted_iota(jnp.int32, (feats, feats), 1)
     column = row % width
     z = row // width % DEPTH
-    core = row // (width * DEPTH) % CORES
-    x = row // (width * DEPTH * CORES)
+    reach = feats // (width * DEPTH * CORES)
+    x = row // (width * DEPTH) % reach
+    core = row // (width * DEPTH * reach)
     place = ((x * DEPTH + z) * CORES + core) * width + column
     order = jnp.where(place == feature, 1.0, 0.0).astype(BF16)
     for k, value in enumerate((got_ref[:, named:], agg)):
@@ -221,17 +228,23 @@
     named = tile_owners[0, :, 0] * row_blocks + tile_blocks[0]
     held = (chip * CORES + core) * row_blocks + jnp.arange(row_blocks, dtype=jnp.int32)
     names = jnp.pad(jnp.concatenate([named, held]), (0, LANES - slots - row_blocks))
-    lists = lax.all_gather(names[None], ("x", "core"), axis=0, tiled=True)
+    lists = lax.all_gather(names[None], ("core", "x"), axis=0, tiled=True)
     columns = DEPTH * width
+    chunks = (peers, columns, (slots + row_blocks) * side)
     sent = call(
         pack_kernel,
-        jax.ShapeDtypeStruct((peers, columns, (slots + row_blocks) * side), BF16),
+        jax.ShapeDtypeStruct(chunks, BF16),
         [SMEM, VMEM],
         8,
-        [pltpu.VMEM((columns, node_count), BF16)],
+        [
+            pltpu.VMEM((columns, node_count), BF16),
+            pltpu.VMEM(chunks, BF16),
+            pltpu.SemaphoreType.DMA((peers,)),
+        ],
+        pl.BlockSpec(memory_space=pl.ANY),
     )(lists, whole)
     got = lax.all_to_all(
-        sent, ("x", "core"), split_axis=0, concat_axis=0, tiled=True
+        sent, ("core", "x"), split_axis=0, concat_axis=0, tiled=True
     ).reshape(feats, (slots + row_blocks) * side)
     mine = call(
         functools.partial(gather_kernel, width),

time: 88.6 us -> 88.9 us (level)
  blocking collectives: 44.4 us -> 48.4 us
  waiting for transfers between devices: 11.4 us -> 7.57 us
    all_to_all x1, waiting for transfers between devices: 5.26 us -> 2.25 us  [local(): whole = lax.all_to_all(copies, 'z', split_axis=0, concat_axis=0, tiled=True)]
    all_gather x1, blocking collectives: 10.6 us -> 13.6 us  [local(): lists = lax.all_gather(names[None], ('core', 'x'), axis=0, tiled=True)]
    all_to_all x1, blocking collectives: 18.4 us -> 19.4 us  [local(): lax.all_to_all(sums, ('x', 'z'), split_axis=0, concat_axis=0, tiled=True)]
where the time goes in v8:
time: 88.9 us; the launch traced here: 88.3 us
  blocking collectives  48.4 us (54%)
  starting transfers between devices  18.9 us (21%)
  Pallas kernels  8.5 us (10%)
  waiting for transfers between devices  7.57 us (9%)
  local copies, waits for them, and re-layouts  3.4 us (4%)
  between operations  1.46 us (2%)
    all_to_all x1, blocking collectives, local(): lax.all_to_all(sums, ('x', 'z'), split_axis=0, concat_axis=0, tiled=True)  19.4 us
    all_to_all x1, blocking collectives, local(): lax.all_to_all(spread, 'dp', split_axis=0, concat_axis=0, tiled=True)  15.5 us
    all_gather x1, blocking collectives, local(): lists = lax.all_gather(names[None], ('core', 'x'), axis=0, tiled=True)  13.6 us
    all_to_all x1, starting transfers between devices, local(): whole = lax.all_to_all(copies, 'z', split_axis=0, concat_axis=0, tiled=True)  9.96 us
    all_to_all x1, starting transfers between devices, local(): lax.all_to_all(sent, ('core', 'x'), split_axis=0, concat_axis=0, tiled=True)  4.31 us
    all_to_all x1, waiting for transfers between devices, local(): lax.all_to_all(sent, ('core', 'x'), split_axis=0, concat_axis=0, tiled=True)  4.16 us
    unnamed x25, local copies, waits for them, and re-layouts  3.4 us
    ppermute x1, starting transfers between devices, local(): their_cot = lax.ppermute(away, 'core', swap)  2.53 us
  transfers between devices with their start and end apart: 4, of which 3 were waited for; matrix products, arithmetic and copies ran while one was open for 0% of the time, Pallas kernels for 4%

profile of v8, /device:TPU:64, one launch (start us, length us, event | category | flops | bytes accessed | tf_op | source)
XLA Modules:
  0.0 88.3 jit_solution(12801716584499945546)
XLA Ops:
  0.7 1.7 %shard_map.121 = bf16[8,2,16384]{2,1,0:T(2,128)(2,1)} custom-call(bf16[2,16384]{1,0:T(2,128)(2,1)} %bitcast.28), custom_call_target="tpu_custom_call" | custom-call | tf_op jit(solution)/shard_map/pallas_call | solution.py:204
  2.3 10.0 %all-to-all-start = ((bf16[8,2,16384]{2,1,0:T(2,128)(2,1)}), bf16[8,2,16384]{2,1,0:T(2,128)(2,1)S(1)}, u32[]{:S(2)}, u32[]{:S(2)}) async-start(bf16[8,2,16384]{2,1,0:T(2,128)(2,1)} %shard_map.121), calls=%async_computation | async-start | bytes 1048576 | tf_op jit(solution)/shard_map/all_to_all | solution.py:210
  12.3 0.0 copy-start.8
  12.4 0.1 pad_add_fusion
  12.5 13.6 %all-gather.1 = s32[8,1,128]{2,1,0:T(1,128)S(1)} all-gather(s32[1,1,128]{2,1,0:T(1,128)S(1)} %pad_bitcast_fusion), channel_id=2, replica_groups=mesh['dp'=8,'x'=4,'z'=8,'core'=2] {'core','x'}, dimensions={0}, use_global_device_ids=true | all-gather | bytes 4608 | tf_op jit(solution)/shard_map/all_gather | solution.py:231
  26.1 2.2 %all-to-all-done.whole_ref = bf16[8,2,16384]{2,1,0:T(2,128)(2,1)S(1)} async-done(((bf16[8,2,16384]{2,1,0:T(2,128)(2,1)}), bf16[8,2,16384]{2,1,0:T(2,128)(2,1)S(1)}, u32[]{:S(2)}, u32[]{:S(2)}) %all-to-all-start) | async-done | bytes 524320 | tf_op jit(solution)/shard_map/all_to_all | solution.py:210
  28.3 1.9 %shard_map.122 = bf16[8,16,3328]{2,1,0:T(8,128)(2,1)} custom-call(s32[8,128]{1,0:T(8,128)S(1)} %bitcast.26, bf16[8,2,16384]{2,1,0:T(2,128)(2,1)S(1)} %all-to-all-done.whole_ref), custom_call_target="tpu_custom_call" | custom-call | tf_op jit(solution)/shard_map/pallas_call | solution.py:234
  30.2 4.3 %all-to-all-start.1 = ((bf16[8,16,3328]{2,1,0:T(8,128)(2,1)}), bf16[8,16,3328]{2,1,0:T(8,128)(2,1)S(1)}, u32[]{:S(2)}, u32[]{:S(2)}) async-start(bf16[8,16,3328]{2,1,0:T(8,128)(2,1)} %shard_map.122), calls=%async_computation.1 | async-start | bytes 1703936 | tf_op jit(solution)/shard_map/all_to_all | solution.py:246
  35.2 0.0 copy-start.1
  35.2 1.0 %copy-done.1 = bf16[1,256,1024]{2,1,0:T(8,128)(2,1)S(1)} copy-done((bf16[1,256,1024]{2,1,0:T(8,128)(2,1)S(1)}, bf16[1,256,1024]{2,1,0:T(8,128)(2,1)}, u32[]{:S(2)}) %copy-start.1) | copy-done | bytes 524312
  36.3 0.9 %copy-done.3 = bf16[128,1024]{1,0:T(8,128)(2,1)S(1)} copy-done((bf16[128,1024]{1,0:T(8,128)(2,1)S(1)}, bf16[128,1024]{1,0:T(8,128)(2,1)}, u32[]{:S(2)}) %copy-start.3) | copy-done | bytes 262168
  37.2 2.5 %shard_map.123 = (bf16[256,512]{1,0:T(8,128)(2,1)S(1)}, bf16[256,512]{1,0:T(8,128)(2,1)}, bf16[256,512]{1,0:T(8,128)(2,1)S(1)}, f32[1,512]{1,0:T(1,128)S(1)}, bf16[256,3072]{1,0:T(8,128)(2,1)S(1)}) custom-call(s32[1]{0:T(128)} %bitcast.8.core_ref, bf16[256,1024]{1,0:T(8,128)(2,1)S(1)} %bitcast.25, bf16[128,1024]{1,0:T(8,128)(2,1)S(1)} %copy-done.2, ...), custom_call_target="tpu_custom_call" | custom-call | tf_op jit(solution)/shard_map/pallas_call | solution.py:215
  39.7 0.7 copy-done.4
  40.4 0.7 copy-done.6
  41.1 2.5 %collective-permute-start.1 = (bf16[256,512]{1,0:T(8,128)(2,1)}, bf16[256,512]{1,0:T(8,128)(2,1)S(1)}, u32[]{:S(2)}, u32[]{:S(2)}) collective-permute-start(bf16[256,512]{1,0:T(8,128)(2,1)} %get-tuple-element.13), channel_id=1, source_target_pairs={{0,1},{1,0},{2,3},{3,2},{4,5},{5,4},{6,7},{7,6},{8,9},{9,8},{10,11... | collective-permute-start | bytes 786440 | tf_op jit(solution)/shard_map/ppermute | solution.py:227
  43.6 4.2 %all-to-all-done.1 = bf16[8,16,3328]{2,1,0:T(8,128)(2,1)S(1)} async-done(((bf16[8,16,3328]{2,1,0:T(8,128)(2,1)}), bf16[8,16,3328]{2,1,0:T(8,128)(2,1)S(1)}, u32[]{:S(2)}, u32[]{:S(2)}) %all-to-all-start.1) | async-done | bytes 852000 | tf_op jit(solution)/shard_map/all_to_all | solution.py:246
  47.8 0.9 %shard_map.124.mine_ref = bf16[256,256]{1,0:T(8,128)(2,1)S(1)} custom-call(bf16[128,3328]{1,0:T(8,128)(2,1)S(1)} %bitcast.23, bf16[256,3072]{1,0:T(8,128)(2,1)S(1)} %get-tuple-element.11.masked_ref), custom_call_target="tpu_custom_call" | custom-call | tf_op jit(solution)/shard_map/pallas_call | solution.py:249
  48.7 2.1 %collective-permute-start = (bf16[256,256]{1,0:T(8,128)(2,1)S(1)}, bf16[256,256]{1,0:T(8,128)(2,1)S(1)}, u32[]{:S(2)}, u32[]{:S(2)}) collective-permute-start(bf16[256,256]{1,0:T(8,128)(2,1)S(1)} %shard_map.124.mine_ref), channel_id=1, source_target_pairs={{0,1},{1,0},{2,3},{3,2},{4,5},{5,4},{6,7},{7,6},{8,9},{9,8},{10,11... | collective-permute-start | bytes 393224 | tf_op jit(solution)/shard_map/ppermute | solution.py:255
  50.8 1.2 %collective-permute-done.theirs_ref = bf16[256,256]{1,0:T(8,128)(2,1)S(1)} collective-permute-done((bf16[256,256]{1,0:T(8,128)(2,1)S(1)}, bf16[256,256]{1,0:T(8,128)(2,1)S(1)}, u32[]{:S(2)}, u32[]{:S(2)}) %collective-permute-start) | collective-permute-done | bytes 131104 | tf_op jit(solution)/shard_map/ppermute | solution.py:255
  51.9 0.9 shard_map.125
  52.8 19.4 %all_to_all.20.got_ref = bf16[32,40,128]{2,1,0:T(8,128)(2,1)S(1)} all-to-all(bf16[32,40,128]{2,1,0:T(8,128)(2,1)S(1)} %shard_map.125), channel_id=1, replica_groups=mesh['dp'=8,'x'=4,'z'=8,'core'=2] {'x','z'}, dimensions={0} | all-to-all | bytes 655360 | tf_op jit(solution)/shard_map/all_to_all | solution.py:263
  72.2 0.1 shard_map.126
  72.2 15.5 %all_to_all.21.got_ref = bf16[8,40,128]{2,1,0:T(8,128)(2,1)S(1)} all-to-all(bf16[8,40,128]{2,1,0:T(8,128)(2,1)S(1)} %shard_map.126), channel_id=1, replica_groups=mesh['dp'=8,'x'=4,'z'=8,'core'=2] {'dp'}, dimensions={0} | all-to-all | bytes 163840 | tf_op jit(solution)/shard_map/all_to_all | solution.py:270
  87.7 0.6 shard_map.127
  (23 shorter events, 0.1 us)
Async XLA Ops:
  0.6 11.7 %copy-start.9 = (s32[1,24]{1,0:T(1,128)S(1)}, s32[1,24]{1,0:T(1,128)}, u32[]{:S(2)}) copy-start(s32[1,24]{1,0:T(1,128)} %param.14) | copy-start | bytes 292
  0.6 11.7 %copy-start.10 = (s32[1,24,1]{1,2,0:T(1,128)S(1)}, s32[1,24,1]{1,2,0:T(1,128)}, u32[]{:S(2)}) copy-start(s32[1,24,1]{1,2,0:T(1,128)} %param.13) | copy-start | bytes 292
  2.3 26.0 %all-to-all-start = ((bf16[8,2,16384]{2,1,0:T(2,128)(2,1)}), bf16[8,2,16384]{2,1,0:T(2,128)(2,1)S(1)}, u32[]{:S(2)}, u32[]{:S(2)}) async-start(bf16[8,2,16384]{2,1,0:T(2,128)(2,1)} %shard_map.121), calls=%async_computation | async-start | bytes 1048576 | tf_op jit(solution)/shard_map/all_to_all | solution.py:210
  12.3 22.9 %copy-start.11 = (s32[1,24]{1,0:T(1,128)S(1)}, s32[1,24]{1,0:T(1,128)}, u32[]{:S(2)}) copy-start(s32[1,24]{1,0:T(1,128)} %param.12) | copy-start | bytes 292
  12.3 22.9 %copy-start = (bf16[1,24,128,128]{3,2,1,0:T(8,128)(2,1)S(1)}, bf16[1,24,128,128]{3,2,1,0:T(8,128)(2,1)}, u32[]{:S(2)}) copy-start(bf16[1,24,128,128]{3,2,1,0:T(8,128)(2,1)} %param.11) | copy-start | bytes 2359300
  12.3 22.9 %copy-start.2 = (bf16[128,1024]{1,0:T(8,128)(2,1)S(1)}, bf16[128,1024]{1,0:T(8,128)(2,1)}, u32[]{:S(2)}) copy-start(bf16[128,1024]{1,0:T(8,128)(2,1)} %w_self_ref.1) | copy-start | bytes 786436
  12.3 22.9 %copy-start.8 = (f32[1024]{0:T(1024)S(1)}, f32[1024]{0:T(1024)}, u32[]{:S(2)}) copy-start(f32[1024]{0:T(1024)} %param.19) | copy-start | bytes 12292
  30.2 17.6 %all-to-all-start.1 = ((bf16[8,16,3328]{2,1,0:T(8,128)(2,1)}), bf16[8,16,3328]{2,1,0:T(8,128)(2,1)S(1)}, u32[]{:S(2)}, u32[]{:S(2)}) async-start(bf16[8,16,3328]{2,1,0:T(8,128)(2,1)} %shard_map.122), calls=%async_computation.1 | async-start | bytes 1703936 | tf_op jit(solution)/shard_map/all_to_all | solution.py:246
  35.2 1.0 %copy-start.1 = (bf16[1,256,1024]{2,1,0:T(8,128)(2,1)S(1)}, bf16[1,256,1024]{2,1,0:T(8,128)(2,1)}, u32[]{:S(2)}) copy-start(bf16[1,256,1024]{2,1,0:T(8,128)(2,1)} %param.16) | copy-start | bytes 1572868
  36.3 0.9 %copy-start.3 = (bf16[128,1024]{1,0:T(8,128)(2,1)S(1)}, bf16[128,1024]{1,0:T(8,128)(2,1)}, u32[]{:S(2)}) copy-start(bf16[128,1024]{1,0:T(8,128)(2,1)} %w_neigh_ref.1) | copy-start | bytes 786436
  39.7 0.7 copy-start.4
  40.4 0.7 copy-start.6
  41.1 10.9 %copy-start.5 = (bf16[256,512]{1,0:T(8,128)(2,1)S(1)}, bf16[256,512]{1,0:T(8,128)(2,1)}, u32[]{:S(2)}) copy-start(bf16[256,512]{1,0:T(8,128)(2,1)} %copy-done.4) | copy-start | bytes 786436
  41.1 10.9 %copy-start.7 = (bf16[256,512]{1,0:T(8,128)(2,1)S(1)}, bf16[256,512]{1,0:T(8,128)(2,1)}, u32[]{:S(2)}) copy-start(bf16[256,512]{1,0:T(8,128)(2,1)} %copy-done.6) | copy-start | bytes 786436
  41.1 9.7 %collective-permute-start.1 = (bf16[256,512]{1,0:T(8,128)(2,1)}, bf16[256,512]{1,0:T(8,128)(2,1)S(1)}, u32[]{:S(2)}, u32[]{:S(2)}) collective-permute-start(bf16[256,512]{1,0:T(8,128)(2,1)} %get-tuple-element.13), channel_id=1, source_target_pairs={{0,1},{1,0},{2,3},{3,2},{4,5},{5,4},{6,7},{7,6},{8,9},{9,8},{10,11... | collective-permute-start | bytes 786440 | tf_op jit(solution)/shard_map/ppermute | solution.py:227
  48.7 3.2 %collective-permute-start = (bf16[256,256]{1,0:T(8,128)(2,1)S(1)}, bf16[256,256]{1,0:T(8,128)(2,1)S(1)}, u32[]{:S(2)}, u32[]{:S(2)}) collective-permute-start(bf16[256,256]{1,0:T(8,128)(2,1)S(1)} %shard_map.124.mine_ref), channel_id=1, source_target_pairs={{0,1},{1,0},{2,3},{3,2},{4,5},{5,4},{6,7},{7,6},{8,9},{9,8},{10,11... | collective-permute-start | bytes 393224 | tf_op jit(solution)/shard_map/ppermute | solution.py:255

commit v9 on v8

--- a/solution.py
+++ b/solution.py
@@ -35,13 +35,13 @@
 
 
 def pack_kernel(lists_ref, whole_ref, sent_ref, table_ref, chunks_ref, sems):
-    depth, width = whole_ref.shape[0], whole_ref.shape[1]
-    for z in range(depth):
-        table_ref[z * width : (z + 1) * width, :] = whole_ref[z]
+    table_ref[...] = whole_ref[...].reshape(table_ref.shape)
+    reach = chunks_ref.shape[0] // CORES
     copies = []
     for p in range(chunks_ref.shape[0]):
+        device = p % reach * CORES + p // reach
         for s in range(chunks_ref.shape[2] // LANES):
-            at = pl.ds(pl.multiple_of(lists_ref[p, s] * LANES, LANES), LANES)
+            at = pl.ds(pl.multiple_of(lists_ref[device, s] * LANES, LANES), LANES)
             chunks_ref[p, :, s * LANES : (s + 1) * LANES] = table_ref[:, at]
         copy = pltpu.make_async_copy(chunks_ref.at[p], sent_ref.at[p], sems.at[p])
         copy.start()
@@ -228,7 +228,7 @@
     named = tile_owners[0, :, 0] * row_blocks + tile_blocks[0]
     held = (chip * CORES + core) * row_blocks + jnp.arange(row_blocks, dtype=jnp.int32)
     names = jnp.pad(jnp.concatenate([named, held]), (0, LANES - slots - row_blocks))
-    lists = lax.all_gather(names[None], ("core", "x"), axis=0, tiled=True)
+    lists = lax.all_gather(names[None], ("x", "core"), axis=0, tiled=True)
     columns = DEPTH * width
     chunks = (peers, columns, (slots + row_blocks) * side)
     sent = call(

time: 88.9 us -> 87.7 us (0.987)
  blocking collectives: 48.4 us -> 44.5 us
  waiting for transfers between devices: 7.57 us -> 10.6 us
    all_gather x1, blocking collectives: 13.6 us -> 10.6 us  [local(): lists = lax.all_gather(names[None], ('x', 'core'), axis=0, tiled=True)]
    all_to_all x1, waiting for transfers between devices: 2.25 us -> 5.26 us  [local(): whole = lax.all_to_all(copies, 'z', split_axis=0, concat_axis=0, tiled=True)]
    all_to_all x1, blocking collectives: 19.4 us -> 18.4 us  [local(): lax.all_to_all(sums, ('x', 'z'), split_axis=0, concat_axis=0, tiled=True)]
where the time goes in v9:
time: 87.7 us; the launch traced here: 87.2 us
  blocking collectives  44.5 us (51%)
  starting transfers between devices  18.9 us (22%)
  waiting for transfers between devices  10.6 us (12%)
  Pallas kernels  8.29 us (9%)
  local copies, waits for them, and re-layouts  3.4 us (4%)
  between operations  1.46 us (2%)
    all_to_all x1, blocking collectives, local(): lax.all_to_all(sums, ('x', 'z'), split_axis=0, concat_axis=0, tiled=True)  18.4 us
    all_to_all x1, blocking collectives, local(): lax.all_to_all(spread, 'dp', split_axis=0, concat_axis=0, tiled=True)  15.4 us
    all_gather x1, blocking collectives, local(): lists = lax.all_gather(names[None], ('x', 'core'), axis=0, tiled=True)  10.6 us
    all_to_all x1, starting transfers between devices, local(): whole = lax.all_to_all(copies, 'z', split_axis=0, concat_axis=0, tiled=True)  9.96 us
    all_to_all x1, waiting for transfers between devices, local(): whole = lax.all_to_all(copies, 'z', split_axis=0, concat_axis=0, tiled=True)  5.26 us
    all_to_all x1, starting transfers between devices, local(): lax.all_to_all(sent, ('core', 'x'), split_axis=0, concat_axis=0, tiled=True)  4.31 us
    all_to_all x1, waiting for transfers between devices, local(): lax.all_to_all(sent, ('core', 'x'), split_axis=0, concat_axis=0, tiled=True)  4.16 us
    unnamed x25, local copies, waits for them, and re-layouts  3.4 us
  transfers between devices with their start and end apart: 4, of which 3 were waited for; matrix products, arithmetic and copies ran while one was open for 0% of the time, Pallas kernels for 4%

profile of v9, /device:TPU:64, one launch (start us, length us, event | category | flops | bytes accessed | tf_op | source)
XLA Modules:
  0.0 87.2 jit_solution(4671246596179005999)
XLA Ops:
  0.7 1.7 %shard_map.121 = bf16[8,2,16384]{2,1,0:T(2,128)(2,1)} custom-call(bf16[2,16384]{1,0:T(2,128)(2,1)} %bitcast.28), custom_call_target="tpu_custom_call" | custom-call | tf_op jit(solution)/shard_map/pallas_call | solution.py:204
  2.3 10.0 %all-to-all-start = ((bf16[8,2,16384]{2,1,0:T(2,128)(2,1)}), bf16[8,2,16384]{2,1,0:T(2,128)(2,1)S(1)}, u32[]{:S(2)}, u32[]{:S(2)}) async-start(bf16[8,2,16384]{2,1,0:T(2,128)(2,1)} %shard_map.121), calls=%async_computation | async-start | bytes 1048576 | tf_op jit(solution)/shard_map/all_to_all | solution.py:210
  12.3 0.0 copy-start.8
  12.4 0.1 pad_add_fusion
  12.5 10.6 %all-gather.1 = s32[8,1,128]{2,1,0:T(1,128)S(1)} all-gather(s32[1,1,128]{2,1,0:T(1,128)S(1)} %pad_bitcast_fusion), channel_id=2, replica_groups=mesh['dp'=8,'x'=4,'z'=8,'core'=2] {'x','core'}, dimensions={0}, use_global_device_ids=true | all-gather | bytes 4608 | tf_op jit(solution)/shard_map/all_gather | solution.py:231
  23.1 5.3 %all-to-all-done.whole_ref = bf16[8,2,16384]{2,1,0:T(2,128)(2,1)S(1)} async-done(((bf16[8,2,16384]{2,1,0:T(2,128)(2,1)}), bf16[8,2,16384]{2,1,0:T(2,128)(2,1)S(1)}, u32[]{:S(2)}, u32[]{:S(2)}) %all-to-all-start) | async-done | bytes 524320 | tf_op jit(solution)/shard_map/all_to_all | solution.py:210
  28.3 1.7 %shard_map.122 = bf16[8,16,3328]{2,1,0:T(8,128)(2,1)} custom-call(s32[8,128]{1,0:T(8,128)S(1)} %bitcast.26, bf16[8,2,16384]{2,1,0:T(2,128)(2,1)S(1)} %all-to-all-done.whole_ref), custom_call_target="tpu_custom_call" | custom-call | tf_op jit(solution)/shard_map/pallas_call | solution.py:234
  30.0 4.3 %all-to-all-start.1 = ((bf16[8,16,3328]{2,1,0:T(8,128)(2,1)}), bf16[8,16,3328]{2,1,0:T(8,128)(2,1)S(1)}, u32[]{:S(2)}, u32[]{:S(2)}) async-start(bf16[8,16,3328]{2,1,0:T(8,128)(2,1)} %shard_map.122), calls=%async_computation.1 | async-start | bytes 1703936 | tf_op jit(solution)/shard_map/all_to_all | solution.py:246
  35.0 0.0 copy-start.1
  35.0 1.0 %copy-done.1 = bf16[1,256,1024]{2,1,0:T(8,128)(2,1)S(1)} copy-done((bf16[1,256,1024]{2,1,0:T(8,128)(2,1)S(1)}, bf16[1,256,1024]{2,1,0:T(8,128)(2,1)}, u32[]{:S(2)}) %copy-start.1) | copy-done | bytes 524312
  36.1 0.9 %copy-done.3 = bf16[128,1024]{1,0:T(8,128)(2,1)S(1)} copy-done((bf16[128,1024]{1,0:T(8,128)(2,1)S(1)}, bf16[128,1024]{1,0:T(8,128)(2,1)}, u32[]{:S(2)}) %copy-start.3) | copy-done | bytes 262168
  37.0 2.5 %shard_map.123 = (bf16[256,512]{1,0:T(8,128)(2,1)S(1)}, bf16[256,512]{1,0:T(8,128)(2,1)}, bf16[256,512]{1,0:T(8,128)(2,1)S(1)}, f32[1,512]{1,0:T(1,128)S(1)}, bf16[256,3072]{1,0:T(8,128)(2,1)S(1)}) custom-call(s32[1]{0:T(128)} %bitcast.8.core_ref, bf16[256,1024]{1,0:T(8,128)(2,1)S(1)} %bitcast.25, bf16[128,1024]{1,0:T(8,128)(2,1)S(1)} %copy-done.2, ...), custom_call_target="tpu_custom_call" | custom-call | tf_op jit(solution)/shard_map/pallas_call | solution.py:215
  39.5 0.7 copy-done.4
  40.2 0.7 copy-done.6
  40.9 2.5 %collective-permute-start.1 = (bf16[256,512]{1,0:T(8,128)(2,1)}, bf16[256,512]{1,0:T(8,128)(2,1)S(1)}, u32[]{:S(2)}, u32[]{:S(2)}) collective-permute-start(bf16[256,512]{1,0:T(8,128)(2,1)} %get-tuple-element.13), channel_id=1, source_target_pairs={{0,1},{1,0},{2,3},{3,2},{4,5},{5,4},{6,7},{7,6},{8,9},{9,8},{10,11... | collective-permute-start | bytes 786440 | tf_op jit(solution)/shard_map/ppermute | solution.py:227
  43.4 4.2 %all-to-all-done.1 = bf16[8,16,3328]{2,1,0:T(8,128)(2,1)S(1)} async-done(((bf16[8,16,3328]{2,1,0:T(8,128)(2,1)}), bf16[8,16,3328]{2,1,0:T(8,128)(2,1)S(1)}, u32[]{:S(2)}, u32[]{:S(2)}) %all-to-all-start.1) | async-done | bytes 852000 | tf_op jit(solution)/shard_map/all_to_all | solution.py:246
  47.6 0.9 %shard_map.124.mine_ref = bf16[256,256]{1,0:T(8,128)(2,1)S(1)} custom-call(bf16[128,3328]{1,0:T(8,128)(2,1)S(1)} %bitcast.23, bf16[256,3072]{1,0:T(8,128)(2,1)S(1)} %get-tuple-element.11.masked_ref), custom_call_target="tpu_custom_call" | custom-call | tf_op jit(solution)/shard_map/pallas_call | solution.py:249
  48.5 2.1 %collective-permute-start = (bf16[256,256]{1,0:T(8,128)(2,1)S(1)}, bf16[256,256]{1,0:T(8,128)(2,1)S(1)}, u32[]{:S(2)}, u32[]{:S(2)}) collective-permute-start(bf16[256,256]{1,0:T(8,128)(2,1)S(1)} %shard_map.124.mine_ref), channel_id=1, source_target_pairs={{0,1},{1,0},{2,3},{3,2},{4,5},{5,4},{6,7},{7,6},{8,9},{9,8},{10,11... | collective-permute-start | bytes 393224 | tf_op jit(solution)/shard_map/ppermute | solution.py:255
  50.5 1.2 %collective-permute-done.theirs_ref = bf16[256,256]{1,0:T(8,128)(2,1)S(1)} collective-permute-done((bf16[256,256]{1,0:T(8,128)(2,1)S(1)}, bf16[256,256]{1,0:T(8,128)(2,1)S(1)}, u32[]{:S(2)}, u32[]{:S(2)}) %collective-permute-start) | collective-permute-done | bytes 131104 | tf_op jit(solution)/shard_map/ppermute | solution.py:255
  51.7 0.9 %shard_map.125 = bf16[32,40,128]{2,1,0:T(8,128)(2,1)S(1)} custom-call(bf16[256,256]{1,0:T(8,128)(2,1)S(1)} %shard_map.124.mine_ref, bf16[256,256]{1,0:T(8,128)(2,1)S(1)} %collective-permute-done.theirs_ref, bf16[256,512]{1,0:T(8,128)(2,1)S(1)} %copy-done.5, bf16[256,512]{1,0:T(8,128)(2,1)S(1)} %collective-permute-done.1.their_cot_ref, ...), custom_call_target="tpu_custom_call" | custom-call | tf_op jit(solution)/shard_map/pallas_call | solution.py:257
  52.6 18.4 %all_to_all.20.got_ref = bf16[32,40,128]{2,1,0:T(8,128)(2,1)S(1)} all-to-all(bf16[32,40,128]{2,1,0:T(8,128)(2,1)S(1)} %shard_map.125), channel_id=1, replica_groups=mesh['dp'=8,'x'=4,'z'=8,'core'=2] {'x','z'}, dimensions={0} | all-to-all | bytes 655360 | tf_op jit(solution)/shard_map/all_to_all | solution.py:263
  71.0 0.1 shard_map.126
  71.1 15.4 %all_to_all.21.got_ref = bf16[8,40,128]{2,1,0:T(8,128)(2,1)S(1)} all-to-all(bf16[8,40,128]{2,1,0:T(8,128)(2,1)S(1)} %shard_map.126), channel_id=1, replica_groups=mesh['dp'=8,'x'=4,'z'=8,'core'=2] {'dp'}, dimensions={0} | all-to-all | bytes 163840 | tf_op jit(solution)/shard_map/all_to_all | solution.py:270
  86.5 0.6 shard_map.127
  (23 shorter events, 0.1 us)
Async XLA Ops:
  0.6 11.7 %copy-start.9 = (s32[1,24]{1,0:T(1,128)S(1)}, s32[1,24]{1,0:T(1,128)}, u32[]{:S(2)}) copy-start(s32[1,24]{1,0:T(1,128)} %param.14) | copy-start | bytes 292
  0.6 11.7 %copy-start.10 = (s32[1,24,1]{1,2,0:T(1,128)S(1)}, s32[1,24,1]{1,2,0:T(1,128)}, u32[]{:S(2)}) copy-start(s32[1,24,1]{1,2,0:T(1,128)} %param.13) | copy-start | bytes 292
  2.3 26.0 %all-to-all-start = ((bf16[8,2,16384]{2,1,0:T(2,128)(2,1)}), bf16[8,2,16384]{2,1,0:T(2,128)(2,1)S(1)}, u32[]{:S(2)}, u32[]{:S(2)}) async-start(bf16[8,2,16384]{2,1,0:T(2,128)(2,1)} %shard_map.121), calls=%async_computation | async-start | bytes 1048576 | tf_op jit(solution)/shard_map/all_to_all | solution.py:210
  12.3 22.7 %copy-start.11 = (s32[1,24]{1,0:T(1,128)S(1)}, s32[1,24]{1,0:T(1,128)}, u32[]{:S(2)}) copy-start(s32[1,24]{1,0:T(1,128)} %param.12) | copy-start | bytes 292
  12.3 22.7 %copy-start = (bf16[1,24,128,128]{3,2,1,0:T(8,128)(2,1)S(1)}, bf16[1,24,128,128]{3,2,1,0:T(8,128)(2,1)}, u32[]{:S(2)}) copy-start(bf16[1,24,128,128]{3,2,1,0:T(8,128)(2,1)} %param.11) | copy-start | bytes 2359300
  12.3 22.7 %copy-start.2 = (bf16[128,1024]{1,0:T(8,128)(2,1)S(1)}, bf16[128,1024]{1,0:T(8,128)(2,1)}, u32[]{:S(2)}) copy-start(bf16[128,1024]{1,0:T(8,128)(2,1)} %w_self_ref.1) | copy-start | bytes 786436
  12.3 22.7 %copy-start.8 = (f32[1024]{0:T(1024)S(1)}, f32[1024]{0:T(1024)}, u32[]{:S(2)}) copy-start(f32[1024]{0:T(1024)} %param.19) | copy-start | bytes 12292
  30.0 17.6 %all-to-all-start.1 = ((bf16[8,16,3328]{2,1,0:T(8,128)(2,1)}), bf16[8,16,3328]{2,1,0:T(8,128)(2,1)S(1)}, u32[]{:S(2)}, u32[]{:S(2)}) async-start(bf16[8,16,3328]{2,1,0:T(8,128)(2,1)} %shard_map.122), calls=%async_computation.1 | async-start | bytes 1703936 | tf_op jit(solution)/shard_map/all_to_all | solution.py:246
  35.0 1.0 %copy-start.1 = (bf16[1,256,1024]{2,1,0:T(8,128)(2,1)S(1)}, bf16[1,256,1024]{2,1,0:T(8,128)(2,1)}, u32[]{:S(2)}) copy-start(bf16[1,256,1024]{2,1,0:T(8,128)(2,1)} %param.16) | copy-start | bytes 1572868
  36.1 0.9 %copy-start.3 = (bf16[128,1024]{1,0:T(8,128)(2,1)S(1)}, bf16[128,1024]{1,0:T(8,128)(2,1)}, u32[]{:S(2)}) copy-start(bf16[128,1024]{1,0:T(8,128)(2,1)} %w_neigh_ref.1) | copy-start | bytes 786436
  39.5 0.7 copy-start.4
  40.2 0.7 copy-start.6
  40.9 10.9 %copy-start.5 = (bf16[256,512]{1,0:T(8,128)(2,1)S(1)}, bf16[256,512]{1,0:T(8,128)(2,1)}, u32[]{:S(2)}) copy-start(bf16[256,512]{1,0:T(8,128)(2,1)} %copy-done.4) | copy-start | bytes 786436
  40.9 10.9 %copy-start.7 = (bf16[256,512]{1,0:T(8,128)(2,1)S(1)}, bf16[256,512]{1,0:T(8,128)(2,1)}, u32[]{:S(2)}) copy-start(bf16[256,512]{1,0:T(8,128)(2,1)} %copy-done.6) | copy-start | bytes 786436
  40.9 9.7 %collective-permute-start.1 = (bf16[256,512]{1,0:T(8,128)(2,1)}, bf16[256,512]{1,0:T(8,128)(2,1)S(1)}, u32[]{:S(2)}, u32[]{:S(2)}) collective-permute-start(bf16[256,512]{1,0:T(8,128)(2,1)} %get-tuple-element.13), channel_id=1, source_target_pairs={{0,1},{1,0},{2,3},{3,2},{4,5},{5,4},{6,7},{7,6},{8,9},{9,8},{10,11... | collective-permute-start | bytes 786440 | tf_op jit(solution)/shard_map/ppermute | solution.py:227
  48.5 3.2 %collective-permute-start = (bf16[256,256]{1,0:T(8,128)(2,1)S(1)}, bf16[256,256]{1,0:T(8,128)(2,1)S(1)}, u32[]{:S(2)}, u32[]{:S(2)}) collective-permute-start(bf16[256,256]{1,0:T(8,128)(2,1)S(1)} %shard_map.124.mine_ref), channel_id=1, source_target_pairs={{0,1},{1,0},{2,3},{3,2},{4,5},{5,4},{6,7},{7,6},{8,9},{9,8},{10,11... | collective-permute-start | bytes 393224 | tf_op jit(solution)/shard_map/ppermute | solution.py:255
